TPU v7x, 256 devices: a whole 4x4x8 slice. The times are simulated.
256 devices in a mesh: gx: 16 (over z_lo, y), gy: 16 (over z_hi, x, core).
Axes of the slice: x: 4, y: 4, z: 8 (z_hi: 2, z_lo: 4; z = z_hi * 4 + z_lo), core: 2. Of those that a mesh axis runs over, the one named last changes fastest.
Arguments:
- coarse_out: float32 [64, 64, 64, 128], P(None, 'gx', 'gy'), may hold values from -6 to 6
- coarse_cot: float32 [64, 64, 64, 128], P(None, 'gx', 'gy'), may hold values from -6 to 6
- fine_conv: float32 [27, 32, 8], replicated, may hold values from -0.4375 to 0.4375
- fine_bias_in: float32 [32], replicated, may hold values from -3 to 3
- fine_proj: float32 [16, 32], replicated, may hold values from -1 to 1
- fine_bias_out: float32 [16], replicated, may hold values from -3 to 3
- coarse_conv: float32 [27, 64, 32], replicated, may hold values from -0.21875 to 0.21875
- coarse_bias_in: float32 [64], replicated, may hold values from -3 to 3
- coarse_proj: float32 [64, 64], replicated, may hold values from -0.75 to 0.75
- coarse_bias_out: float32 [64], replicated, may hold values from -3 to 3
Outputs:
- input_field: float32 [16, 128, 128, 128], P(None, 'gx', 'gy')
- input_grad: float32 [16, 128, 128, 128], P(None, 'gx', 'gy')
- grad_fine_conv: float32 [27, 32, 8], replicated
- grad_fine_bias_in: float32 [32], replicated
- grad_fine_proj: float32 [16, 32], replicated
- grad_fine_bias_out: float32 [16], replicated
- grad_coarse_conv: float32 [27, 64, 32], replicated
- grad_coarse_bias_in: float32 [64], replicated
- grad_coarse_proj: float32 [64, 64], replicated
- grad_coarse_bias_out: float32 [64], replicated
All inputs are finite; a program needn't handle non-finite values.
Results may differ from a plain program's by a relative error of at most 0.00021.
Values sent between devices are 32-bit elements; how exact they have to be, the bound alone decides.
No kernel may reach another device: no remote copies, remote signals or barrier semaphores. Data moves between devices by JAX's collectives and lax.ppermute only.
A program may use at most 128 MiB of HBM per device.

v0:
```python
import jax
import jax.numpy as jnp
from jax import lax
from jax.sharding import PartitionSpec as P

precise = lax.Precision.HIGHEST


def extended(x, sides, width):
    for axis, dim in sides:
        size, length = (lax.axis_size(axis), x.shape[dim])
        up = [(i, (i + 1) % size) for i in range(size - 1)]
        down = [(j, i) for i, j in up]
        last = lax.slice_in_dim(x, length - width, length, axis=dim)
        leading = lax.slice_in_dim(x, 0, width, axis=dim)
        before = lax.ppermute(last, axis, up)
        after = lax.ppermute(leading, axis, down)
        x = jnp.concatenate([before, x, after], axis=dim)
    return x


def gather_taps(padded, cells_x, cells_y, cells_z):
    pieces = []
    for stencil in range(27):
        a, b, c = (stencil // 9, stencil // 3 % 3, stencil % 3)
        pieces.append(padded[:, a : a + cells_x, b : b + cells_y, c : c + cells_z])
    return jnp.concatenate(pieces, axis=0)


def level_back(level_out, level_cot, conv_weight, bias_in, projection, bias_out):
    split_at = level_out.shape[0] // 2
    hidden_count = conv_weight.shape[1]
    cells_x, cells_y, cells_z = (level_out.shape[1], level_out.shape[2], level_out.shape[3])
    upper_half = level_out[:split_at]
    lower_half = level_out[split_at:]
    framed = extended(upper_half, (("gx", 1), ("gy", 2)), 1)
    padded = jnp.pad(framed, ((0, 0), (0, 0), (0, 0), (1, 1)))
    patches = gather_taps(padded, cells_x, cells_y, cells_z)
    flat_weight = jnp.transpose(conv_weight, (1, 0, 2)).reshape(hidden_count, 27 * split_at)
    pre_act = (
        jnp.einsum("ok,kxyz->oxyz", flat_weight, patches, precision=precise)
        + bias_in[:, None, None, None]
    )
    sigmoid_pre = jax.nn.sigmoid(pre_act)
    activation = pre_act * sigmoid_pre
    net_out = (
        jnp.einsum("oh,hxyz->oxyz", projection, activation, precision=precise)
        + bias_out[:, None, None, None]
    )
    log_scale = jnp.tanh(net_out[:split_at])
    shift_term = net_out[split_at:]
    centred = lower_half - shift_term
    lower_input = centred * jnp.exp(-log_scale)
    upper_cot = level_cot[:split_at]
    lower_cot = level_cot[split_at:]
    lower_grad = lower_cot * jnp.exp(log_scale)
    out_grad = jnp.concatenate(
        [lower_cot * centred * (1.0 - log_scale * log_scale), lower_cot], axis=0
    )
    grad_proj = jnp.einsum("oxyz,hxyz->oh", out_grad, activation, precision=precise)
    grad_bias_out = jnp.sum(out_grad, axis=(1, 2, 3))
    act_grad = jnp.einsum("oh,oxyz->hxyz", projection, out_grad, precision=precise)
    pre_grad = act_grad * sigmoid_pre * (1.0 + pre_act * (1.0 - sigmoid_pre))
    grad_bias_in = jnp.sum(pre_grad, axis=(1, 2, 3))
    grad_flat = jnp.einsum("oxyz,kxyz->ok", pre_grad, patches, precision=precise)
    grad_conv = jnp.transpose(grad_flat.reshape(hidden_count, 27, split_at), (1, 0, 2))
    framed_grad = extended(pre_grad, (("gx", 1), ("gy", 2)), 1)
    contrib = jnp.einsum(
        "ok,oxyz->kxyz",
        flat_weight,
        jnp.pad(framed_grad, ((0, 0), (0, 0), (0, 0), (1, 1))),
        precision=precise,
    )
    upper_grad = jnp.zeros_like(upper_half)
    for stencil in range(27):
        a, b, c = (stencil // 9, stencil // 3 % 3, stencil % 3)
        upper_grad = (
            upper_grad
            + contrib[
                stencil * split_at : (stencil + 1) * split_at,
                2 - a : 2 - a + cells_x,
                2 - b : 2 - b + cells_y,
                2 - c : 2 - c + cells_z,
            ]
        )
    grads = (grad_conv, grad_bias_in, grad_proj, grad_bias_out)
    level_input = jnp.concatenate([upper_half, lower_input], axis=0)
    input_cot = jnp.concatenate([upper_cot + upper_grad, lower_grad], axis=0)
    return (level_input, input_cot, grads)


def unsqueeze(bands_field):
    count = bands_field.shape[0] // 4
    bands = [bands_field[k * count : (k + 1) * count] for k in range(4)]
    even_even = 0.5 * (bands[0] + bands[1] + bands[2] + bands[3])
    odd_even = 0.5 * (bands[0] - bands[1] + bands[2] - bands[3])
    even_odd = 0.5 * (bands[0] + bands[1] - bands[2] - bands[3])
    odd_odd = 0.5 * (bands[0] - bands[1] - bands[2] + bands[3])
    shape_half = even_even.shape
    rows_even = jnp.stack([even_even, even_odd], axis=3).reshape(
        count, shape_half[1], 2 * shape_half[2], shape_half[3]
    )
    rows_odd = jnp.stack([odd_even, odd_odd], axis=3).reshape(
        count, shape_half[1], 2 * shape_half[2], shape_half[3]
    )
    return jnp.stack([rows_even, rows_odd], axis=2).reshape(
        count, 2 * shape_half[1], 2 * shape_half[2], shape_half[3]
    )


def local(
    coarse_out,
    coarse_cot,
    fine_conv,
    fine_bias_in,
    fine_proj,
    fine_bias_out,
    coarse_conv,
    coarse_bias_in,
    coarse_proj,
    coarse_bias_out,
):
    squeezed, squeezed_cot, coarse_grads = level_back(
        coarse_out, coarse_cot, coarse_conv, coarse_bias_in, coarse_proj, coarse_bias_out
    )
    fine_field = unsqueeze(squeezed)
    fine_cot = unsqueeze(squeezed_cot)
    input_field, input_grad, fine_grads = level_back(
        fine_field, fine_cot, fine_conv, fine_bias_in, fine_proj, fine_bias_out
    )
    summed = lax.psum(
        (
            fine_grads[0],
            fine_grads[1],
            fine_grads[2],
            fine_grads[3],
            coarse_grads[0],
            coarse_grads[1],
            coarse_grads[2],
            coarse_grads[3],
        ),
        ("gx", "gy"),
    )
    fine_grads = summed[0:4]
    coarse_grads = summed[4:8]
    total_cells = (
        input_field.shape[1]
        * input_field.shape[2]
        * input_field.shape[3]
        * lax.axis_size("gx")
        * lax.axis_size("gy")
    )
    factor = float(total_cells) ** (-0.5)
    return (
        input_field,
        input_grad,
        fine_grads[0] * factor,
        fine_grads[1] * factor,
        fine_grads[2] * factor,
        fine_grads[3] * factor,
        coarse_grads[0] * factor,
        coarse_grads[1] * factor,
        coarse_grads[2] * factor,
        coarse_grads[3] * factor,
    )


def solution(mesh):
    placed = (
        P(None, "gx", "gy", None),
        P(None, "gx", "gy", None),
        P(),
        P(),
        P(),
        P(),
        P(),
        P(),
        P(),
        P(),
    )
    return jax.shard_map(
        local,
        mesh=mesh,
        in_specs=placed,
        out_specs=(
            P(None, "gx", "gy", None),
            P(None, "gx", "gy", None),
            P(),
            P(),
            P(),
            P(),
            P(),
            P(),
            P(),
            P(),
        ),
        check_vma=False,
    )
```

profile of v0, /device:TPU:31, one launch (start us, length us, event | category | flops | bytes accessed | tf_op | source)
XLA Modules:
  0.0 511.7 jit_solution(10540509441040586695)
XLA Ops:
  7.2 0.9 fusion.85
  8.2 3.2 collective-permute-start
  11.4 2.1 collective-permute-start.1
  13.5 1.1 fusion.84
  14.6 1.1 fusion.81
  15.8 2.8 collective-permute-done.1
  18.6 9.8 %collective-permute-start.2 = (f32[32,6,1,128]{3,0,2,1:T(8,128)S(1)}, f32[32,6,1,128]{3,0,2,1:T(8,128)S(1)}, u32[]{:S(2)}, u32[]{:S(2)}) collective-permute-start(f32[32,6,1,128]{3,0,2,1:T(8,128)S(1)} %get-tuple-element.71), channel_id=1, source_target_pairs={{0,1},{1,2},{2,3},{3,4},{4,5},{5,6},{6,7},{7,8},{8,9},{9,10},{10,1... | collective-permute-start | bytes 294920 | tf_op jit(solution)/shard_map/ppermute | solution.py:16
  28.4 1.9 collective-permute-start.3
  30.3 1.0 fusion.83
  31.3 9.1 %collective-permute-done.3 = f32[32,6,1,128]{3,0,2,1:T(8,128)S(1)} collective-permute-done((f32[32,6,1,128]{3,0,2,1:T(8,128)S(1)}, f32[32,6,1,128]{3,0,2,1:T(8,128)S(1)}, u32[]{:S(2)}, u32[]{:S(2)}) %collective-permute-start.3) | collective-permute-done | bytes 98336 | tf_op jit(solution)/shard_map/ppermute | solution.py:17
  42.6 4.8 fusion.23
  47.5 0.7 fusion.26
  48.4 0.8 fusion.90
  49.3 6.6 %fusion.91 = f32[64,864,1,1]{0,1,3,2:T(8,128)} fusion(f32[64,4,4,128]{3,0,2,1:T(8,128)S(1)} %get-tuple-element.85, f32[864,4,4,128]{3,0,2,1:T(8,128)S(1)} %slice_dynamic-update-slice_fusion.24), kind=kOutput, calls=%fused_computation.288 | convolution fusion | flops 1358954496 | bytes 7823360 | tf_op jit(solution)/shard_map/oxyz,kxyz->ok/dot_general | solution.py:65
  56.1 2.6 collective-permute-start.4
  58.8 2.6 collective-permute-start.5
  62.2 3.4 collective-permute-done.5
  65.6 2.2 collective-permute-start.6
  67.8 2.1 collective-permute-start.7
  69.9 0.7 convolution_bitcast_fusion.5
  70.7 1.9 collective-permute-start.8
  72.6 3.4 collective-permute-start.9
  76.1 3.0 collective-permute-done.7
  81.2 2.9 copy-done.2
  84.1 4.7 fusion.21
  88.8 1.7 fusion.22
  90.5 1.5 pad_maximum_fusion.23
  92.0 7.0 %collective-permute-start.10 = (f32[64,6,1,128]{3,0,2,1:T(8,128)}, f32[64,6,1,128]{3,0,2,1:T(8,128)S(1)}, u32[]{:S(2)}, u32[]{:S(2)}) collective-permute-start(f32[64,6,1,128]{3,0,2,1:T(8,128)} %get-tuple-element.44), channel_id=1, source_target_pairs={{0,1},{1,2},{2,3},{3,4},{4,5},{5,6},{6,7},{7,8},{8,9},{9,10},{10,1... | collective-permute-start | bytes 589832 | tf_op jit(solution)/shard_map/ppermute | solution.py:16
  99.1 1.9 collective-permute-start.11
  101.0 219.5 %all-reduce.7.cloned.1.call-done = f32[27,64,32]{1,2,0:T(8,128)} async-done(((f32[27,64,32]{1,2,0:T(8,128)}), f32[27,64,32]{1,2,0:T(8,128)}) %all-reduce.7.cloned.1.call-update) | async-done | bytes 221200 | tf_op jit(solution)/shard_map/psum | solution.py:131
  320.5 1.8 broadcast_multiply_fusion
  322.4 30.7 %convolution_bitcast_fusion = f32[864,6,6,130]{3,0,2,1:T(8,128)} fusion(f32[64,864,1,1]{0,1,3,2:T(8,128)S(1)} %bitcast.119, f32[64,6,1,128]{3,0,2,1:T(8,128)} %collective-permute-done.11, f32[64,6,1,128]{3,0,2,1:T(8,128)S(1)} %collective-permute-done.10, f32[64,1,4,128]{3,0,2,1:T(8,128)} %collective-permute-done.9, ...), kind=kOutput, calls=%fused_computation | convolution fusion | flops 3109017600 | bytes 17574912 | tf_op jit(solution)/shard_map/ok,oxyz->kxyz/dot_general | solution.py:68
  353.1 5.8 %fusion.47 = f32[32,4,4,128]{3,0,2,1:T(8,128)S(1)} fusion(f32[864,6,6,130]{3,0,2,1:T(8,128)} %convolution_bitcast_fusion, f32[32,4,4,128]{3,2,1,0:T(4,128)S(1)} %get-tuple-element.55), kind=kLoop, calls=%fused_computation.126 | loop fusion | flops 1769472 | bytes 7602176 | tf_op jit(solution)/shard_map/add | solution.py:88
  359.1 0.8 fusion.44
  360.2 1.0 convolution_bitcast_fusion.6
  361.2 1.4 fusion.89
  363.0 5.6 %convolution_bitcast_fusion.4 = f32[27,32,8]{1,2,0:T(8,128)S(1)} fusion(f32[32,8,8,128]{3,0,2,1:T(8,128)S(1)} %get-tuple-element.83, f32[216,8,8,128]{3,0,2,1:T(8,128)S(1)} %bitcast.121), kind=kOutput, calls=%fused_computation.55 | convolution fusion | flops 679477248 | bytes 8154112 | tf_op jit(solution)/shard_map/oxyz,kxyz->ok/dot_general | solution.py:65
  368.7 75.7 %all-reduce.4 = (f32[27,32,8]{1,2,0:T(8,128)S(1)}, f32[32]{0:T(128)S(1)}, f32[16,32]{1,0:T(8,128)S(1)}, f32[16]{0:T(128)S(1)}, f32[64]{0:T(128)S(1)}, /*index=5*/f32[64,64]{1,0:T(8,128)S(1)}, f32[64]{0:T(128)S(1)}) all-reduce(f32[27,32,8]{1,2,0:T(8,128)S(1)} %convolution_bitcast_fusion.4, ...), channel_id=1, replica_groups=mesh['gx'=16,'gy'=16] {'gx','gy'}, use_global_device_ids=true, to_apply=%region_0.1 | all-reduce | flops 11696 | bytes 93568 | tf_op jit(solution)/shard_map/psum | solution.py:131
  447.3 4.3 collective-permute-start.12
  451.6 1.9 collective-permute-start.13
  453.6 1.0 copy.64
  455.1 4.3 collective-permute-done.13
  459.4 8.1 %collective-permute-start.14 = (f32[32,10,1,128]{3,0,2,1:T(8,128)S(1)}, f32[32,10,1,128]{3,0,2,1:T(8,128)S(1)}, u32[]{:S(2)}, u32[]{:S(2)}) collective-permute-start(f32[32,10,1,128]{3,0,2,1:T(8,128)S(1)} %get-tuple-element.37), channel_id=1, source_target_pairs={{0,1},{1,2},{2,3},{3,4},{4,5},{5,6},{6,7},{7,8},{8,9},{9,10},{10,1... | collective-permute-start | bytes 491528 | tf_op jit(solution)/shard_map/ppermute | solution.py:16
  467.6 2.1 collective-permute-start.15
  470.2 10.2 %collective-permute-done.15 = f32[32,10,1,128]{3,0,2,1:T(8,128)S(1)} collective-permute-done((f32[32,10,1,128]{3,0,2,1:T(8,128)S(1)}, f32[32,10,1,128]{3,0,2,1:T(8,128)S(1)}, u32[]{:S(2)}, u32[]{:S(2)}) %collective-permute-start.15) | collective-permute-done | bytes 163872 | tf_op jit(solution)/shard_map/ppermute | solution.py:17
  480.4 22.0 %convolution_bitcast_fusion.1 = f32[216,10,10,130]{3,0,2,1:T(8,128)S(1)} fusion(f32[32,10,1,128]{3,0,2,1:T(8,128)S(1)} %collective-permute-done.15, f32[32,10,1,128]{3,0,2,1:T(8,128)S(1)} %collective-permute-done.14, f32[32,1,8,128]{3,0,2,1:T(8,128)S(1)} %collective-permute-done.13, f32[32,8,8,128]{3,0,2,1:T(8,128)S(1)} %get-tuple-element.83, ...), kind=kOutput, calls=%fused_computation.1 | convolution fusion | flops 1083264000 | bytes 12898048 | tf_op jit(solution)/shard_map/ok,oxyz->kxyz/dot_general | solution.py:68
  502.4 1.3 fusion.46
  503.7 1.0 copy.65
  (136 shorter events, 10.3 us)
Async XLA Ops:
  7.2 35.4 %copy-start = (f32[27,64,32]{1,2,0:T(8,128)S(1)}, f32[27,64,32]{1,2,0:T(8,128)}, u32[]{:S(2)}) copy-start(f32[27,64,32]{1,2,0:T(8,128)} %param.16) | copy-start | bytes 663556
  7.2 313.3 %all-reduce.7.cloned.1.call-start = ((), (), s32[]{:S(2)}) async-start(), calls=%async_computation | async-start | bytes 884736 | tf_op jit(solution)/shard_map/psum | solution.py:131
  8.2 7.5 %collective-permute-start = (f32[32,1,4,128]{3,0,2,1:T(8,128)S(1)}, f32[32,1,4,128]{3,0,2,1:T(8,128)S(1)}, u32[]{:S(2)}, u32[]{:S(2)}) collective-permute-start(f32[32,1,4,128]{3,0,2,1:T(8,128)S(1)} %copy.89), channel_id=1, source_target_pairs={{0,16},{16,32},{32,48},{48,64},{64,80},{80,96},{96,112},{112,128},... | collective-permute-start | bytes 196616 | tf_op jit(solution)/shard_map/ppermute | solution.py:16
  11.4 7.1 %collective-permute-start.1 = (f32[32,1,4,128]{3,0,2,1:T(8,128)S(1)}, f32[32,1,4,128]{3,0,2,1:T(8,128)S(1)}, u32[]{:S(2)}, u32[]{:S(2)}) collective-permute-start(f32[32,1,4,128]{3,0,2,1:T(8,128)S(1)} %copy.91), channel_id=1, source_target_pairs={{16,0},{32,16},{48,32},{64,48},{80,64},{96,80},{112,96},{128,112},... | collective-permute-start | bytes 196616 | tf_op jit(solution)/shard_map/ppermute | solution.py:17
  18.6 12.8 %collective-permute-start.2 = (f32[32,6,1,128]{3,0,2,1:T(8,128)S(1)}, f32[32,6,1,128]{3,0,2,1:T(8,128)S(1)}, u32[]{:S(2)}, u32[]{:S(2)}) collective-permute-start(f32[32,6,1,128]{3,0,2,1:T(8,128)S(1)} %get-tuple-element.71), channel_id=1, source_target_pairs={{0,1},{1,2},{2,3},{3,4},{4,5},{5,6},{6,7},{7,8},{8,9},{9,10},{10,1... | collective-permute-start | bytes 294920 | tf_op jit(solution)/shard_map/ppermute | solution.py:16
  28.4 12.1 %collective-permute-start.3 = (f32[32,6,1,128]{3,0,2,1:T(8,128)S(1)}, f32[32,6,1,128]{3,0,2,1:T(8,128)S(1)}, u32[]{:S(2)}, u32[]{:S(2)}) collective-permute-start(f32[32,6,1,128]{3,0,2,1:T(8,128)S(1)} %get-tuple-element.72), channel_id=1, source_target_pairs={{1,0},{2,1},{3,2},{4,3},{5,4},{6,5},{7,6},{8,7},{9,8},{10,9},{11,1... | collective-permute-start | bytes 294920 | tf_op jit(solution)/shard_map/ppermute | solution.py:17
  40.9 1.8 copy-start.7
  41.9 5.6 %copy-start.9 = (f32[64,64]{1,0:T(8,128)S(1)}, f32[64,64]{1,0:T(8,128)}, u32[]{:S(2)}) copy-start(f32[64,64]{1,0:T(8,128)} %param.18) | copy-start | bytes 49156
  41.9 5.6 %copy-start.11 = (f32[64]{0:T(128)S(1)}, f32[64]{0:T(128)}, u32[]{:S(2)}) copy-start(f32[64]{0:T(128)} %param.19) | copy-start | bytes 772
  56.1 6.0 %collective-permute-start.4 = (f32[8,1,8,128]{3,0,2,1:T(8,128)S(1)}, f32[8,1,8,128]{3,0,2,1:T(8,128)S(1)}, u32[]{:S(2)}, u32[]{:S(2)}) collective-permute-start(f32[8,1,8,128]{3,0,2,1:T(8,128)S(1)} %get-tuple-element.78), channel_id=1, source_target_pairs={{0,16},{16,32},{32,48},{48,64},{64,80},{80,96},{96,112},{112,128},... | collective-permute-start | bytes 98312 | tf_op jit(solution)/shard_map/ppermute | solution.py:16
  58.8 6.8 %collective-permute-start.5 = (f32[8,1,8,128]{3,0,2,1:T(8,128)S(1)}, f32[8,1,8,128]{3,0,2,1:T(8,128)S(1)}, u32[]{:S(2)}, u32[]{:S(2)}) collective-permute-start(f32[8,1,8,128]{3,0,2,1:T(8,128)S(1)} %get-tuple-element.79), channel_id=1, source_target_pairs={{16,0},{32,16},{48,32},{64,48},{80,64},{96,80},{112,96},{128,112},... | collective-permute-start | bytes 98312 | tf_op jit(solution)/shard_map/ppermute | solution.py:17
  65.6 10.5 %collective-permute-start.6 = (f32[8,10,1,128]{3,0,2,1:T(8,128)S(1)}, f32[8,10,1,128]{3,0,2,1:T(8,128)S(1)}, u32[]{:S(2)}, u32[]{:S(2)}) collective-permute-start(f32[8,10,1,128]{3,0,2,1:T(8,128)S(1)} %get-tuple-element.75), channel_id=1, source_target_pairs={{0,1},{1,2},{2,3},{3,4},{4,5},{5,6},{6,7},{7,8},{8,9},{9,10},{10,1... | collective-permute-start | bytes 122888 | tf_op jit(solution)/shard_map/ppermute | solution.py:16
  67.8 11.3 %collective-permute-start.7 = (f32[8,10,1,128]{3,0,2,1:T(8,128)S(1)}, f32[8,10,1,128]{3,0,2,1:T(8,128)S(1)}, u32[]{:S(2)}, u32[]{:S(2)}) collective-permute-start(f32[8,10,1,128]{3,0,2,1:T(8,128)S(1)} %get-tuple-element.76), channel_id=1, source_target_pairs={{1,0},{2,1},{3,2},{4,3},{5,4},{6,5},{7,6},{8,7},{9,8},{10,9},{11,1... | collective-permute-start | bytes 122888 | tf_op jit(solution)/shard_map/ppermute | solution.py:17
  70.7 19.8 %collective-permute-start.8 = (f32[64,1,4,128]{3,0,2,1:T(8,128)}, f32[64,1,4,128]{3,0,2,1:T(8,128)S(1)}, u32[]{:S(2)}, u32[]{:S(2)}) collective-permute-start(f32[64,1,4,128]{3,0,2,1:T(8,128)} %get-tuple-element.57), channel_id=1, source_target_pairs={{0,16},{16,32},{32,48},{48,64},{64,80},{80,96},{96,112},{112,128},... | collective-permute-start | bytes 393224 | tf_op jit(solution)/shard_map/ppermute | solution.py:16
  72.6 17.9 %collective-permute-start.9 = (f32[64,1,4,128]{3,0,2,1:T(8,128)}, f32[64,1,4,128]{3,0,2,1:T(8,128)}, u32[]{:S(2)}, u32[]{:S(2)}) collective-permute-start(f32[64,1,4,128]{3,0,2,1:T(8,128)} %get-tuple-element.58), channel_id=1, source_target_pairs={{16,0},{32,16},{48,32},{64,48},{80,64},{96,80},{112,96},{128,112},... | collective-permute-start | bytes 393224 | tf_op jit(solution)/shard_map/ppermute | solution.py:17
  79.5 4.6 copy-start.5
  79.5 4.6 copy-start.8
  80.4 8.3 %copy-start.10 = (f32[16,32]{1,0:T(8,128)S(1)}, f32[16,32]{1,0:T(8,128)}, u32[]{:S(2)}) copy-start(f32[16,32]{1,0:T(8,128)} %param.14) | copy-start | bytes 6148
  80.5 8.3 %copy-start.12 = (f32[16]{0:T(128)S(1)}, f32[16]{0:T(128)}, u32[]{:S(2)}) copy-start(f32[16]{0:T(128)} %param.15) | copy-start | bytes 196
  81.2 2.9 copy-start.2
  92.0 230.3 %collective-permute-start.10 = (f32[64,6,1,128]{3,0,2,1:T(8,128)}, f32[64,6,1,128]{3,0,2,1:T(8,128)S(1)}, u32[]{:S(2)}, u32[]{:S(2)}) collective-permute-start(f32[64,6,1,128]{3,0,2,1:T(8,128)} %get-tuple-element.44), channel_id=1, source_target_pairs={{0,1},{1,2},{2,3},{3,4},{4,5},{5,6},{6,7},{7,8},{8,9},{9,10},{10,1... | collective-permute-start | bytes 589832 | tf_op jit(solution)/shard_map/ppermute | solution.py:16
  99.1 223.3 %collective-permute-start.11 = (f32[64,6,1,128]{3,0,2,1:T(8,128)}, f32[64,6,1,128]{3,0,2,1:T(8,128)}, u32[]{:S(2)}, u32[]{:S(2)}) collective-permute-start(f32[64,6,1,128]{3,0,2,1:T(8,128)} %get-tuple-element.45), channel_id=1, source_target_pairs={{1,0},{2,1},{3,2},{4,3},{5,4},{6,5},{7,6},{8,7},{9,8},{10,9},{11,1... | collective-permute-start | bytes 589832 | tf_op jit(solution)/shard_map/ppermute | solution.py:17
  353.1 6.8 %copy-start.4 = (f32[16,8,8,128]{3,0,2,1:T(8,128)S(1)}, f32[16,8,8,128]{3,0,2,1:T(8,128)}, u32[]{:S(2)}) copy-start(f32[16,8,8,128]{3,0,2,1:T(8,128)} %fusion.22) | copy-start | bytes 1572868
  359.8 2.8 slice-start
  360.2 2.8 slice-start.1
  362.6 90.9 %copy-start.3 = (f32[8,4,2,8,128]{4,0,3,1,2:T(8,128)S(1)}, f32[8,4,2,8,128]{4,0,3,1,2:T(8,128)}, u32[]{:S(2)}) copy-start(f32[8,4,2,8,128]{4,0,3,1,2:T(8,128)} %get-tuple-element.49) | copy-start | bytes 786436
  362.7 117.7 %copy-start.6 = (f32[27,32,8]{1,2,0:T(8,128)S(1)}, f32[27,32,8]{1,2,0:T(8,128)}, u32[]{:S(2)}) copy-start(f32[27,32,8]{1,2,0:T(8,128)} %param.12) | copy-start | bytes 82948
  447.3 7.8 %collective-permute-start.12 = (f32[32,1,8,128]{3,0,2,1:T(8,128)S(1)}, f32[32,1,8,128]{3,0,2,1:T(8,128)S(1)}, u32[]{:S(2)}, u32[]{:S(2)}) collective-permute-start(f32[32,1,8,128]{3,0,2,1:T(8,128)S(1)} %get-tuple-element.39), channel_id=1, source_target_pairs={{0,16},{16,32},{32,48},{48,64},{64,80},{80,96},{96,112},{112,128},... | collective-permute-start | bytes 393224 | tf_op jit(solution)/shard_map/ppermute | solution.py:16
  451.6 7.8 %collective-permute-start.13 = (f32[32,1,8,128]{3,0,2,1:T(8,128)S(1)}, f32[32,1,8,128]{3,0,2,1:T(8,128)S(1)}, u32[]{:S(2)}, u32[]{:S(2)}) collective-permute-start(f32[32,1,8,128]{3,0,2,1:T(8,128)S(1)} %get-tuple-element.40), channel_id=1, source_target_pairs={{16,0},{32,16},{48,32},{64,48},{80,64},{96,80},{112,96},{128,112},... | collective-permute-start | bytes 393224 | tf_op jit(solution)/shard_map/ppermute | solution.py:17
  459.4 10.7 %collective-permute-start.14 = (f32[32,10,1,128]{3,0,2,1:T(8,128)S(1)}, f32[32,10,1,128]{3,0,2,1:T(8,128)S(1)}, u32[]{:S(2)}, u32[]{:S(2)}) collective-permute-start(f32[32,10,1,128]{3,0,2,1:T(8,128)S(1)} %get-tuple-element.37), channel_id=1, source_target_pairs={{0,1},{1,2},{2,3},{3,4},{4,5},{5,6},{6,7},{7,8},{8,9},{9,10},{10,1... | collective-permute-start | bytes 491528 | tf_op jit(solution)/shard_map/ppermute | solution.py:16
  467.6 12.8 %collective-permute-start.15 = (f32[32,10,1,128]{3,0,2,1:T(8,128)S(1)}, f32[32,10,1,128]{3,0,2,1:T(8,128)S(1)}, u32[]{:S(2)}, u32[]{:S(2)}) collective-permute-start(f32[32,10,1,128]{3,0,2,1:T(8,128)S(1)} %get-tuple-element.38), channel_id=1, source_target_pairs={{1,0},{2,1},{3,2},{4,3},{5,4},{6,5},{7,6},{8,7},{9,8},{10,9},{11,1... | collective-permute-start | bytes 491528 | tf_op jit(solution)/shard_map/ppermute | solution.py:17
  480.4 24.3 %copy-start.1 = (f32[27,64,32]{1,2,0:T(8,128)S(1)}, f32[27,64,32]{1,2,0:T(8,128)}, u32[]{:S(2)}) copy-start(f32[27,64,32]{1,2,0:T(8,128)} %param.16) | copy-start | bytes 663556
Sparse Core Ops, SparseCore 0:
  70.8 249.7 all-reduce.6
where the time goes:
time: 521 us; the launch traced here: 512 us
  waiting for transfers between devices  252 us (48%)
  matrix products  80.8 us (16%)
  blocking collectives  75.7 us (15%)
  starting transfers between devices  57.3 us (11%)
  other arithmetic  17.1 us (3%)
  between operations  15.2 us (3%)
  local copies, waits for them, and re-layouts  13.1 us (3%)
    psum x1, waiting for transfers between devices, local(): lax.psum((fine_grads[0], fine_grads[1], fine_grads[2], fine_grads[3], coa...  220 us
    psum x1, blocking collectives, local(): lax.psum((fine_grads[0], fine_grads[1], fine_grads[2], fine_grads[3], coa...  75.7 us
    dot_general x2, matrix products, level_back(): jnp.einsum('ok,oxyz->kxyz', flat_weight, jnp.pad(framed_grad, ((0, 0), (0...  52.7 us
    ppermute x8, starting transfers between devices, extended(): before = lax.ppermute(last, axis, up)  39.2 us
    ppermute x8, waiting for transfers between devices, extended(): after = lax.ppermute(leading, axis, down)  32.9 us
    ppermute x8, starting transfers between devices, extended(): after = lax.ppermute(leading, axis, down)  18.1 us
    dot_general x2, matrix products, level_back(): jnp.einsum('oxyz,kxyz->ok', pre_grad, patches, precision=precise)  12.2 us
  transfers between devices with their start and end apart: 17, of which 7 were waited for; matrix products, arithmetic and copies ran while one was open for 4% of the time, Pallas kernels for 0%

commit v1 on v0

v1 whole, which is shorter than its diff:
```python
import jax
import jax.numpy as jnp
from jax import lax
from jax.experimental import pallas as pl
from jax.experimental.pallas import tpu as pltpu
from jax.sharding import PartitionSpec as P

f32 = jnp.float32
bf16 = jnp.bfloat16
VMEM_BYTES = 40 * 1024 * 1024


def dot(a, b):
    return lax.dot_general(a, b, (((1,), (0,)), ((), ())), preferred_element_type=f32)


def dot_cells(a, b):
    return lax.dot_general(a, b, (((1,), (1,)), ((), ())), preferred_element_type=f32)


def split(x):
    top = x.astype(bf16).astype(f32)
    return top, x - top


def stacked(x, spare=0):
    top, rest = split(x)
    rows = [top, rest, top]
    if spare:
        rows.append(jnp.zeros((spare, x.shape[1]), f32))
    return jnp.concatenate(rows, axis=0).astype(bf16)


def weight(w, count):
    top, rest = split(w)
    lane = lax.broadcasted_iota(jnp.int32, w.shape, 1)
    return jnp.where(lane < 2 * count, top, rest).astype(bf16)


def row_of(ref, x, first, count):
    return jnp.concatenate([ref[x, first + y] for y in range(count)], axis=1)


def shifted(x, step):
    lane = lax.broadcasted_iota(jnp.int32, (x.shape[0], 128), 1)
    edge = 0 if step > 0 else 127
    out = []
    for k in range(x.shape[1] // 128):
        moved = pltpu.roll(x[:, 128 * k : 128 * (k + 1)], step % 128, 1)
        out.append(jnp.where(lane == edge, 0.0, moved))
    return jnp.concatenate(out, axis=1)


def taps_along_z(x):
    return jnp.concatenate([shifted(x, 1), x, shifted(x, -1)], axis=0)


def window(o, rows, width, backward):
    parts = []
    for b in range(3):
        at = (2 - b if backward else b) * 128
        parts.append(o[b * rows : (b + 1) * rows, at : at + width])
    return parts[0] + parts[1] + parts[2]


def coupling(pre, v, dv, pj, pt, bo):
    half = v.shape[0]
    sig = jax.nn.sigmoid(pre)
    act = pre * sig
    out = dot(pj, stacked(act)) + bo
    sc = jnp.tanh(out[:half])
    centred = v - out[half:]
    lower = centred * jnp.exp(-sc)
    lower_cot = dv * jnp.exp(sc)
    g = jnp.concatenate([dv * centred * (1.0 - sc * sc), dv], axis=0)
    ga = dot(pt, stacked(g))
    gpre = ga * sig * (1.0 + pre * (1.0 - sig))
    return act, g, gpre, lower, lower_cot


def placed_at(x, before, after):
    rows = x.shape[0]
    parts = []
    if before:
        parts.append(jnp.zeros((rows, 128 * before), f32))
    parts.append(x)
    if after:
        parts.append(jnp.zeros((rows, 128 * after), f32))
    return jnp.concatenate(parts, axis=1) if len(parts) > 1 else x


def weight_products(patch, gpre, act, g):
    tops, rests = [], []
    for piece in [placed_at(gpre, b, 2 - b) for b in range(3)] + [placed_at(act, 1, 1)]:
        top, rest = split(piece)
        tops.append(top)
        rests.append(rest)
    right = jnp.concatenate(tops + rests, axis=0).astype(bf16)
    p_top, p_rest = split(patch)
    g_top, g_rest = split(placed_at(g, 1, 1))
    ones = jnp.ones((16, patch.shape[1]), f32)
    left = jnp.concatenate([p_top, p_rest, ones, g_top, g_rest], axis=0).astype(bf16)
    return dot_cells(left, right)


def lane_sum(x):
    total = x[:, :128]
    for k in range(1, x.shape[1] // 128):
        total = total + x[:, 128 * k : 128 * (k + 1)]
    return total


def packed_grads(products, g_sum, taps, hidden, outs, factor):
    wide = 4 * hidden
    halves = products[:, :wide] + products[:, wide:]
    conv = halves[:taps] + halves[taps : 2 * taps]
    at = 2 * taps
    bias_in = pltpu.roll(halves[at : at + 16], hidden, 1)
    at += 16
    proj = halves[at : at + outs] + halves[at + outs : at + 2 * outs]
    bias_out = jnp.broadcast_to(jnp.sum(g_sum, axis=1, keepdims=True), (outs, wide))
    rest = jnp.zeros((taps - 2 * outs - 16, wide), f32)
    others = jnp.concatenate([proj, bias_out, bias_in, rest], axis=0)
    lane = lax.broadcasted_iota(jnp.int32, (taps, wide), 1)
    return jnp.where(lane < 3 * hidden, conv, others) * factor


def coarse_kernel(factor, u_ref, vd_ref, cot_ref, mask_ref, wp_ref, bi_ref, pj_ref, pt_ref, bo_ref, wd_ref,
                  qv_ref, dq_ref, grads_ref, taps, gpre_s, act_s, g_s, low_s, sums, g_sum):
    nx, ny, k = cot_ref.shape[0], cot_ref.shape[1], u_ref.shape[2]
    h = bi_ref.shape[0]
    wide, own = (ny + 2) * 128, slice(128, 128 * (ny + 1))
    wp = weight(wp_ref[...], 9 * k)
    pj = weight(pj_ref[...], h)
    pt = weight(pt_ref[...], 2 * k)
    wd = weight(wd_ref[...], 3 * h)

    def fill(x, _):
        taps[x] = taps_along_z(row_of(u_ref, x, 0, ny + 4))
        return 0

    lax.fori_loop(0, nx + 4, fill, 0)

    def forward(x, _):
        patch = jnp.concatenate([taps[x], taps[x + 1], taps[x + 2]], axis=0)
        pre = window(dot(wp, stacked(patch)), h, wide, False) + bi_ref[...]
        vd = row_of(vd_ref, x, 0, ny + 2)
        act, g, gpre, lower, lower_cot = coupling(pre, vd[:k], vd[k:], pj, pt, bo_ref[...])
        lower = lower * mask_ref[x]
        for y in range(ny + 2):
            qv_ref[x, y] = lower[:, 128 * y : 128 * (y + 1)]
        gpre_s[x] = gpre
        act_s[x] = act[:, own]
        g_s[x] = g[:, own]
        low_s[x] = lower_cot[:, own]
        return 0

    lax.fori_loop(0, nx + 2, forward, 0)

    sums[...] = jnp.zeros_like(sums)
    g_sum[...] = jnp.zeros_like(g_sum)

    def products(x, _):
        patch = jnp.concatenate([taps[x + 1 + a][:, 128 : 128 + wide] for a in range(3)], axis=0)
        g = g_s[x + 1]
        sums[...] += weight_products(patch, gpre_s[x + 1][:, own], act_s[x + 1], g)
        g_sum[...] += lane_sum(g)
        return 0

    lax.fori_loop(0, nx, products, 0)
    packed = packed_grads(sums[...], g_sum[...], 9 * k, h, 2 * k, factor)
    grads_ref[: 9 * k] = packed[:, :128]
    grads_ref[9 * k :] = packed[:, 128:]

    def back(x, _):
        rows = jnp.concatenate([gpre_s[x + 2], gpre_s[x + 1], gpre_s[x]], axis=0)
        s = window(dot(wd, stacked(rows)), 3 * k, ny * 128, True)
        du = s[k : 2 * k] + shifted(s[:k], -1) + shifted(s[2 * k :], 1)
        low = low_s[x + 1]
        for y in range(ny):
            cols = slice(128 * y, 128 * (y + 1))
            dq_ref[x, y, :k] = cot_ref[x, y, :k] + du[:, cols]
            dq_ref[x, y, k:] = low[:, cols]
        return 0

    lax.fori_loop(0, nx, back, 0)


def finer_rows(upper, lower):
    c = upper.shape[0] // 2
    a, b, d, e = upper[:c], upper[c:], lower[:c], lower[c:]
    sum_u, sum_l, dif_u, dif_l = a + b, d + e, a - b, d - e
    rows = []
    for p, q in ((sum_u, sum_l), (dif_u, dif_l)):
        even, odd = 0.5 * (p + q), 0.5 * (p - q)
        cols = []
        for k in range(even.shape[1] // 128):
            cols += [even[:, 128 * k : 128 * (k + 1)], odd[:, 128 * k : 128 * (k + 1)]]
        rows.append(jnp.concatenate(cols, axis=1))
    return rows


def fine_kernel(factor, u_ref, qv_ref, dq_ref, wp_ref, bi_ref, pj_ref, pt_ref, bo_ref,
                field_ref, cot_ref, gpre_ref, grads_ref, taps, v_s, dz_s, sums, g_sum):
    nx, ny = field_ref.shape[0], field_ref.shape[1]
    k = field_ref.shape[2] // 2
    h = bi_ref.shape[0]
    wp = weight(wp_ref[...], 9 * k)
    pj = weight(pj_ref[...], h)
    pt = weight(pt_ref[...], 2 * k)
    cx, cy = nx // 2, ny // 2

    def store(z, row, own):
        taps[row] = taps_along_z(z[:k, 128 : 128 * (ny + 3)])
        if own:
            v_s[row - 1] = z[k:, 256 : 128 * (ny + 2)]

    for x in range(cx + 2):
        first, second = finer_rows(row_of(u_ref, x + 1, 1, cy + 2), row_of(qv_ref, x, 0, cy + 2))
        if x > 0:
            store(first, 2 * x - 1, x <= cx)
        if x < cx + 1:
            store(second, 2 * x, x >= 1)
    for x in range(cx):
        dq = row_of(dq_ref, x, 0, cy)
        first, second = finer_rows(dq[: 4 * k], dq[4 * k :])
        dz_s[2 * x] = first
        dz_s[2 * x + 1] = second

    sums[...] = jnp.zeros_like(sums)
    g_sum[...] = jnp.zeros_like(g_sum)

    def forward(x, _):
        patch = jnp.concatenate([taps[x], taps[x + 1], taps[x + 2]], axis=0)
        pre = window(dot(wp, stacked(patch, 8)), h, ny * 128, False) + bi_ref[...]
        dz = dz_s[x]
        act, g, gpre, lower, lower_cot = coupling(pre, v_s[x], dz[k:], pj, pt, bo_ref[...])
        sums[...] += weight_products(patch, gpre, act, g)
        g_sum[...] += lane_sum(g)
        field = jnp.concatenate([taps[x + 1][k : 2 * k, 128 : 128 * (ny + 1)], lower], axis=0)
        cot = jnp.concatenate([dz[:k], lower_cot], axis=0)
        for y in range(ny):
            cols = slice(128 * y, 128 * (y + 1))
            field_ref[x, y] = field[:, cols]
            cot_ref[x, y] = cot[:, cols]
            gpre_ref[x, y] = gpre[:, cols]
        return 0

    lax.fori_loop(0, nx, forward, 0)
    grads_ref[...] = packed_grads(sums[...], g_sum[...], 9 * k, h, 2 * k, factor)


def fine_back_kernel(gpre_ref, cot_ref, wd_ref, out_ref):
    nx, ny = cot_ref.shape[0], cot_ref.shape[1]
    k = cot_ref.shape[2] // 2
    h = gpre_ref.shape[2]
    wd = weight(wd_ref[...], 3 * h)

    def back(x, _):
        rows = jnp.concatenate([row_of(gpre_ref, x + 2 - a, 0, ny + 2) for a in range(3)], axis=0)
        s = window(dot(wd, stacked(rows)), 3 * k, ny * 128, True)
        du = s[k : 2 * k] + shifted(s[:k], -1) + shifted(s[2 * k :], 1)
        for y in range(ny):
            cols = slice(128 * y, 128 * (y + 1))
            out_ref[x, y, :k] = cot_ref[x, y, :k] + du[:, cols]
            out_ref[x, y, k:] = cot_ref[x, y, k:]
        return 0

    lax.fori_loop(0, nx, back, 0)


def call(kernel, outs, scratch, flops, *args):
    return pl.pallas_call(
        kernel,
        out_shape=[jax.ShapeDtypeStruct(s, f32) for s in outs],
        scratch_shapes=[pltpu.VMEM(s, f32) for s in scratch],
        compiler_params=pltpu.CompilerParams(vmem_limit_bytes=VMEM_BYTES),
        cost_estimate=pl.CostEstimate(flops=flops, bytes_accessed=4_000_000, transcendentals=0),
    )(*args)


def halos(axis, low, high):
    size = lax.axis_size(axis)
    even = lax.axis_index(axis) % 2 == 0
    inner = [(i, i ^ 1) for i in range(size)]
    outer = []
    for i in range(1, size - 1, 2):
        outer += [(i, i + 1), (i + 1, i)]
    one = lax.ppermute(jnp.where(even, high, low), axis, inner)
    two = lax.ppermute(jnp.where(even, low, high), axis, outer)
    return jnp.where(even, two, one), jnp.where(even, one, two)


def partner(x, axis, bit):
    return lax.ppermute(x, axis, [(i, i ^ bit) for i in range(lax.axis_size(axis))])


def half_sum(x, axis, bit):
    rows = x.shape[0] // 2
    upper = (lax.axis_index(axis) // bit) % 2 == 1
    first, second = x[:rows], x[rows:]
    return jnp.where(upper, second, first) + partner(jnp.where(upper, first, second), axis, bit)


def both_halves(x, axis, bit):
    upper = (lax.axis_index(axis) // bit) % 2 == 1
    other = partner(x, axis, bit)
    return jnp.concatenate([jnp.where(upper, other, x), jnp.where(upper, x, other)], axis=0)


def summed(coarse, fine):
    sizes = {axis: lax.axis_size(axis) for axis in ("gx", "gy")}
    steps = [(axis, 1 << k) for axis in ("gy", "gx") for k in range(sizes[axis].bit_length() - 1)]
    halving = [("gy", 1), ("gx", 1), ("gy", 2)]
    for axis, bit in halving:
        coarse = half_sum(coarse, axis, bit)
        fine = fine + partner(fine, axis, bit)
    rows = coarse.shape[0]
    both = jnp.concatenate([coarse, fine], axis=0)
    for axis, bit in steps:
        if (axis, bit) not in halving:
            both = both + partner(both, axis, bit)
    coarse, fine = both[:rows], both[rows:]
    for axis, bit in halving[::-1]:
        coarse = both_halves(coarse, axis, bit)
    return coarse, fine


def weights(conv, proj, spare):
    hidden, inputs = conv.shape[1], conv.shape[2]
    taps = conv.reshape(3, 3, 3, hidden, inputs)
    ahead = taps.transpose(1, 3, 0, 2, 4).reshape(3 * hidden, 9 * inputs)
    back = taps.transpose(1, 2, 4, 0, 3).reshape(9 * inputs, 3 * hidden)
    ahead = [ahead] * 3 + ([jnp.zeros((3 * hidden, spare), f32)] if spare else [])
    return (
        jnp.concatenate(ahead, axis=1),
        jnp.concatenate([back] * 3, axis=1),
        jnp.concatenate([proj] * 3, axis=1),
        jnp.concatenate([proj.T] * 3, axis=1),
    )


def unpacked(grads, hidden, inputs):
    conv = grads[:, : 3 * hidden].reshape(3, 3, inputs, 3, hidden)
    conv = conv.transpose(0, 3, 1, 4, 2).reshape(27, hidden, inputs)
    outs = 2 * inputs
    others = grads[:, 3 * hidden :]
    return conv, others[2 * outs], others[:outs], others[outs : 2 * outs, 0]


def local(
    coarse_out,
    coarse_cot,
    fine_conv,
    fine_bias_in,
    fine_proj,
    fine_bias_out,
    coarse_conv,
    coarse_bias_in,
    coarse_proj,
    coarse_bias_out,
):
    channels, nx, ny, nz = coarse_out.shape
    k = channels // 2
    h = coarse_conv.shape[1]
    fk, fh = fine_conv.shape[2], fine_conv.shape[1]
    cells = 4 * nx * ny * nz * lax.axis_size("gx") * lax.axis_size("gy")
    factor = float(cells) ** -0.5

    w = jnp.transpose(coarse_out, (1, 2, 0, 3))
    dw = jnp.transpose(coarse_cot, (1, 2, 0, 3))
    u = w[:, :, :k]
    vd = jnp.concatenate([w[:, :, k:], dw[:, :, k:]], axis=2)

    def side(u_part, vd_part):
        return jnp.concatenate([u_part.reshape(-1, k, nz), vd_part.reshape(-1, k, nz)], axis=0)

    def sides(packed, u_shape, vd_shape):
        count = u_shape[0] * u_shape[1]
        return packed[:count].reshape(*u_shape, k, nz), packed[count:].reshape(*vd_shape, 2 * k, nz)

    low, high = halos("gx", side(u[:2], vd[:1]), side(u[-2:], vd[-1:]))
    (u_low, vd_low), (u_high, vd_high) = [sides(s, (2, ny), (1, ny)) for s in (low, high)]
    u = jnp.concatenate([u_low, u, u_high], axis=0)
    vd = jnp.concatenate([vd_low, vd, vd_high], axis=0)
    low, high = halos("gy", side(u[:, :2], vd[:, :1]), side(u[:, -2:], vd[:, -1:]))
    (u_low, vd_low), (u_high, vd_high) = [sides(s, (nx + 4, 2), (nx + 2, 1)) for s in (low, high)]
    u = jnp.concatenate([u_low, u, u_high], axis=1)
    vd = jnp.concatenate([vd_low, vd, vd_high], axis=1)

    def inside(axis, count):
        at = lax.axis_index(axis) * count + jnp.arange(-1, count + 1)
        return ((at >= 0) & (at < lax.axis_size(axis) * count)).astype(f32)

    mask = jnp.repeat(inside("gx", nx)[:, None] * inside("gy", ny)[None, :], nz, axis=1)[:, None, :]

    ahead, back, proj, proj_t = weights(coarse_conv, coarse_proj, 0)
    qv, dq, coarse_grads = call(
        lambda *refs: coarse_kernel(factor, *refs),
        [(nx + 2, ny + 2, k, nz), (nx, ny, 2 * k, nz), (18 * k, 128)],
        [
            (nx + 4, 3 * k, (ny + 4) * nz),
            (nx + 2, h, (ny + 2) * nz),
            (nx + 2, h, ny * nz),
            (nx + 2, 2 * k, ny * nz),
            (nx + 2, k, ny * nz),
            (18 * k + 16 + 4 * k, 8 * h),
            (2 * k, 128),
        ],
        3_000_000_000,
        u,
        vd,
        dw[:, :, :k],
        mask,
        ahead,
        coarse_bias_in[:, None],
        proj,
        proj_t,
        coarse_bias_out[:, None],
        back,
    )

    ahead, back, proj, proj_t = weights(fine_conv, fine_proj, 8)
    fx, fy = 2 * nx, 2 * ny
    field, cot, gpre, fine_grads = call(
        lambda *refs: fine_kernel(factor, *refs),
        [(fx, fy, 2 * fk, nz), (fx, fy, 2 * fk, nz), (fx, fy, fh, nz), (9 * fk, 4 * fh)],
        [
            (fx + 2, 3 * fk, (fy + 2) * nz),
            (fx, fk, fy * nz),
            (fx, 2 * fk, fy * nz),
            (18 * fk + 16 + 4 * fk, 8 * fh),
            (2 * fk, 128),
        ],
        1_500_000_000,
        u,
        qv,
        dq,
        ahead,
        fine_bias_in[:, None],
        proj,
        proj_t,
        fine_bias_out[:, None],
    )

    low, high = halos("gx", gpre[:1], gpre[-1:])
    gpre = jnp.concatenate([low, gpre, high], axis=0)
    low, high = halos("gy", gpre[:, :1], gpre[:, -1:])
    gpre = jnp.concatenate([low, gpre, high], axis=1)
    (cot,) = call(fine_back_kernel, [cot.shape], [], 1_000_000_000, gpre, cot, back)

    coarse_grads, fine_grads = summed(coarse_grads, fine_grads)
    coarse_grads = jnp.concatenate([coarse_grads[: 9 * k], coarse_grads[9 * k :]], axis=1)
    return (
        jnp.transpose(field, (2, 0, 1, 3)),
        jnp.transpose(cot, (2, 0, 1, 3)),
        *unpacked(fine_grads, fh, fk),
        *unpacked(coarse_grads, h, k),
    )


def solution(mesh):
    split_field = P(None, "gx", "gy", None)
    return jax.shard_map(
        local,
        mesh=mesh,
        in_specs=(split_field, split_field) + (P(),) * 8,
        out_specs=(split_field, split_field) + (P(),) * 8,
        check_vma=False,
    )
```

time: 521 us -> 126 us (0.24)
  the two profiles are of different devices: /device:TPU:31 before, /device:TPU:7 now
where the time goes in v1:
time: 126 us
  starting transfers between devices  52.3 us (42%)
  waiting for transfers between devices  29.3 us (23%)
  Pallas kernels  23.2 us (18%)
  local copies, waits for them, and re-layouts  15.6 us (12%)
  other arithmetic  3.91 us (3%)
  between operations  1.35 us (1%)
    pallas_call x3, Pallas kernels, call(): pl.pallas_call(kernel, out_shape=[jax.ShapeDtypeStruct(s, f32) for s in o...  23.2 us
    ppermute x4, starting transfers between devices, halos(): two = lax.ppermute(jnp.where(even, low, high), axis, outer)  21.5 us
    ppermute x14, starting transfers between devices, partner(): lax.ppermute(x, axis, [(i, i ^ bit) for i in range(lax.axis_size(axis))])  18.5 us
    ppermute x14, waiting for transfers between devices, partner(): lax.ppermute(x, axis, [(i, i ^ bit) for i in range(lax.axis_size(axis))])  18.3 us
    ppermute x4, starting transfers between devices, halos(): one = lax.ppermute(jnp.where(even, high, low), axis, inner)  12.2 us
    unnamed x38, local copies, waits for them, and re-layouts  7.29 us
    ppermute x4, waiting for transfers between devices, halos(): two = lax.ppermute(jnp.where(even, low, high), axis, outer)  5.77 us
    ppermute x4, waiting for transfers between devices, halos(): one = lax.ppermute(jnp.where(even, high, low), axis, inner)  5.27 us
  transfers between devices with their start and end apart: 22, of which 9 were waited for; matrix products, arithmetic and copies ran while one was open for 7% of the time, Pallas kernels for 8%

profile of v1, /device:TPU:7, one launch (start us, length us, event | category | flops | bytes accessed | tf_op | source)
XLA Modules:
  0.0 125.7 jit_solution(2538391316706709125)
XLA Ops:
  0.7 1.3 %copy.87 = f32[64,4,4,128]{3,0,2,1:T(8,128)S(1)} copy(f32[64,4,4,128]{3,2,1,0:T(4,128)} %param.10) | data formatting | bytes 1048576 | tf_op args[0]
  2.3 0.8 fusion.3
  3.1 1.4 %collective-permute-start = (f32[16,32,128]{2,1,0:T(8,128)}, f32[16,32,128]{2,1,0:T(8,128)}, u32[]{:S(2)}, u32[]{:S(2)}) collective-permute-start(f32[16,32,128]{2,1,0:T(8,128)} %get-tuple-element.73), channel_id=1, source_target_pairs={{16,32},{32,16},{48,64},{64,48},{80,96},{96,80},{112,128},{128,112... | collective-permute-start | bytes 786440 | tf_op jit(solution)/shard_map/ppermute | solution.py:290
  4.5 3.2 %collective-permute-start.1 = (f32[16,32,128]{2,1,0:T(8,128)}, f32[16,32,128]{2,1,0:T(8,128)}, u32[]{:S(2)}, u32[]{:S(2)}) collective-permute-start(f32[16,32,128]{2,1,0:T(8,128)} %get-tuple-element.74), channel_id=1, source_target_pairs={{0,16},{16,0},{32,48},{48,32},{64,80},{80,64},{96,112},{112,96},{1... | collective-permute-start | bytes 786440 | tf_op jit(solution)/shard_map/ppermute | solution.py:289
  7.8 0.3 copy.85
  8.1 0.3 copy.84
  8.6 0.3 reshape.133
  9.1 0.3 reshape.134
  10.5 3.2 %collective-permute-done.1 = f32[16,32,128]{2,1,0:T(8,128)} collective-permute-done((f32[16,32,128]{2,1,0:T(8,128)}, f32[16,32,128]{2,1,0:T(8,128)}, u32[]{:S(2)}, u32[]{:S(2)}) %collective-permute-start.1) | collective-permute-done | bytes 262176 | tf_op jit(solution)/shard_map/ppermute | solution.py:289
  13.7 1.1 broadcast_select_fusion.3
  15.1 10.2 %collective-permute-start.2 = (f32[28,32,128]{2,1,0:T(8,128)S(1)}, f32[28,32,128]{2,1,0:T(8,128)S(1)}, u32[]{:S(2)}, u32[]{:S(2)}) collective-permute-start(f32[28,32,128]{2,1,0:T(8,128)S(1)} %get-tuple-element.61), channel_id=1, source_target_pairs={{1,2},{2,1},{3,4},{4,3},{5,6},{6,5},{7,8},{8,7},{9,10},{10,9},{11,... | collective-permute-start | bytes 1376264 | tf_op jit(solution)/shard_map/ppermute | solution.py:290
  25.7 5.8 %collective-permute-done.2 = f32[28,32,128]{2,1,0:T(8,128)S(1)} collective-permute-done((f32[28,32,128]{2,1,0:T(8,128)S(1)}, f32[28,32,128]{2,1,0:T(8,128)S(1)}, u32[]{:S(2)}, u32[]{:S(2)}) %collective-permute-start.2) | collective-permute-done | bytes 458784 | tf_op jit(solution)/shard_map/ppermute | solution.py:290
  32.0 12.8 %shard_map.177 = (f32[6,6,32,128]{3,2,1,0:T(8,128)S(1)}, f32[4,4,64,128]{3,2,1,0:T(8,128)S(1)}, f32[576,128]{1,0:T(8,128)S(1)}) custom-call(f32[8,8,32,128]{3,2,1,0:T(8,128)S(1)} %pad_maximum_fusion.2.refs_0_, f32[6,6,64,128]{3,2,1,0:T(8,128)S(1)} %pad_maximum_fusion.1.refs_1_, f32[4,4,32,128]{3,2,1,0:T(8,128)S(1)} %get-tuple-element.65.refs_2_, ...), custom_call_target="tpu_custom_call" | custom-call | flops 3000000000 | bytes 4000000 | tf_op jit(solution)/shard_map/pallas_call | solution.py:273
  44.7 0.8 copy-done.2
  45.5 0.8 copy-done.4
  46.7 1.1 copy-done.3
  47.8 1.0 copy-done.5
  48.8 7.6 %shard_map.178 = (f32[8,8,16,128]{3,2,1,0:T(8,128)S(1)}, f32[8,8,16,128]{3,2,1,0:T(8,128)S(1)}, f32[8,8,32,128]{3,2,1,0:T(8,128)S(1)}, f32[72,128]{1,0:T(8,128)S(1)}) custom-call(f32[8,8,32,128]{3,2,1,0:T(8,128)S(1)} %pad_maximum_fusion.2.refs_0_, f32[6,6,32,128]{3,2,1,0:T(8,128)S(1)} %copy-done.3, f32[4,4,64,128]{3,2,1,0:T(8,128)S(1)} %copy-done.5, ...), custom_call_target="tpu_custom_call" | custom-call | flops 1500000000 | bytes 4000000 | tf_op jit(solution)/shard_map/pallas_call | solution.py:273
  56.4 0.6 collective-permute-start.11
  57.1 1.5 %collective-permute-start.9 = (f32[144,128]{1,0:T(8,128)S(1)}, f32[144,128]{1,0:T(8,128)S(1)}, u32[]{:S(2)}, u32[]{:S(2)}) collective-permute-start(f32[144,128]{1,0:T(8,128)S(1)} %slice_select_fusion.3), channel_id=1, source_target_pairs={{0,16},{16,0},{32,48},{48,32},{64,80},{80,64},{96,112},{112,96},{1... | collective-permute-start | bytes 221192 | tf_op jit(solution)/shard_map/ppermute | solution.py:295
  58.6 0.8 collective-permute-start.12
  59.4 2.1 %collective-permute-done.12 = f32[72,128]{1,0:T(8,128)S(1)} collective-permute-done((f32[72,128]{1,0:T(8,128)S(1)}, f32[72,128]{1,0:T(8,128)S(1)}, u32[]{:S(2)}, u32[]{:S(2)}) %collective-permute-start.12) | collective-permute-done | bytes 36896 | tf_op jit(solution)/shard_map/ppermute | solution.py:295
  61.6 1.5 %collective-permute-start.10 = (f32[72,128]{1,0:T(8,128)S(1)}, f32[72,128]{1,0:T(8,128)S(1)}, u32[]{:S(2)}, u32[]{:S(2)}) collective-permute-start(f32[72,128]{1,0:T(8,128)S(1)} %slice_select_fusion.4), channel_id=1, source_target_pairs={{0,2},{1,3},{2,0},{3,1},{4,6},{5,7},{6,4},{7,5},{8,10},{9,11},{10,... | collective-permute-start | bytes 110600 | tf_op jit(solution)/shard_map/ppermute | solution.py:295
  63.2 0.7 collective-permute-start.4
  63.8 4.3 %collective-permute-start.5 = (f32[1,8,32,128]{3,2,1,0:T(8,128)S(1)}, f32[1,8,32,128]{3,2,1,0:T(8,128)S(1)}, u32[]{:S(2)}, u32[]{:S(2)}) collective-permute-start(f32[1,8,32,128]{3,2,1,0:T(8,128)S(1)} %get-tuple-element.58), channel_id=1, source_target_pairs={{0,16},{16,0},{32,48},{48,32},{64,80},{80,64},{96,112},{112,96},{1... | collective-permute-start | bytes 393224 | tf_op jit(solution)/shard_map/ppermute | solution.py:289
  68.2 0.3 collective-permute-start.14
  68.5 2.0 %collective-permute-done.5 = f32[1,8,32,128]{3,2,1,0:T(8,128)S(1)} collective-permute-done((f32[1,8,32,128]{3,2,1,0:T(8,128)S(1)}, f32[1,8,32,128]{3,2,1,0:T(8,128)S(1)}, u32[]{:S(2)}, u32[]{:S(2)}) %collective-permute-start.5) | collective-permute-done | bytes 131104 | tf_op jit(solution)/shard_map/ppermute | solution.py:289
  70.5 2.6 %collective-permute-done.14 = f32[144,128]{1,0:T(8,128)S(1)} collective-permute-done((f32[144,128]{1,0:T(8,128)S(1)}, f32[144,128]{1,0:T(8,128)S(1)}, u32[]{:S(2)}, u32[]{:S(2)}) %collective-permute-start.14) | collective-permute-done | bytes 73760 | tf_op jit(solution)/shard_map/ppermute | solution.py:295
  73.2 4.5 %collective-permute-start.15 = (f32[144,128]{1,0:T(8,128)S(1)}, f32[144,128]{1,0:T(8,128)S(1)}, u32[]{:S(2)}, u32[]{:S(2)}) collective-permute-start(f32[144,128]{1,0:T(8,128)S(1)} %fusion.4), channel_id=1, source_target_pairs={{0,8},{1,9},{2,10},{3,11},{4,12},{5,13},{6,14},{7,15},{8,0},{9,1},... | collective-permute-start | bytes 221192 | tf_op jit(solution)/shard_map/ppermute | solution.py:295
  77.8 2.6 %collective-permute-done.15 = f32[144,128]{1,0:T(8,128)S(1)} collective-permute-done((f32[144,128]{1,0:T(8,128)S(1)}, f32[144,128]{1,0:T(8,128)S(1)}, u32[]{:S(2)}, u32[]{:S(2)}) %collective-permute-start.15) | collective-permute-done | bytes 73760 | tf_op jit(solution)/shard_map/ppermute | solution.py:295
  80.4 8.5 %collective-permute-start.16 = (f32[144,128]{1,0:T(8,128)S(1)}, f32[144,128]{1,0:T(8,128)S(1)}, u32[]{:S(2)}, u32[]{:S(2)}) collective-permute-start(f32[144,128]{1,0:T(8,128)S(1)} %add.102), channel_id=1, source_target_pairs={{0,32},{16,48},{32,0},{48,16},{64,96},{80,112},{96,64},{112,80},{1... | collective-permute-start | bytes 221192 | tf_op jit(solution)/shard_map/ppermute | solution.py:295
  89.0 4.6 %collective-permute-start.7 = (f32[10,1,32,128]{3,2,1,0:T(8,128)S(1)}, f32[10,1,32,128]{3,2,1,0:T(8,128)S(1)}, u32[]{:S(2)}, u32[]{:S(2)}) collective-permute-start(f32[10,1,32,128]{3,2,1,0:T(8,128)S(1)} %broadcast_select_fusion.6), channel_id=1, source_target_pairs={{0,1},{1,0},{2,3},{3,2},{4,5},{5,4},{6,7},{7,6},{8,9},{9,8},{10,11... | collective-permute-start | bytes 491528 | tf_op jit(solution)/shard_map/ppermute | solution.py:289
  93.6 9.3 %collective-permute-start.6 = (f32[10,1,32,128]{3,2,1,0:T(8,128)S(1)}, f32[10,1,32,128]{3,2,1,0:T(8,128)S(1)}, u32[]{:S(2)}, u32[]{:S(2)}) collective-permute-start(f32[10,1,32,128]{3,2,1,0:T(8,128)S(1)} %get-tuple-element.54), channel_id=1, source_target_pairs={{1,2},{2,1},{3,4},{4,3},{5,6},{6,5},{7,8},{8,7},{9,10},{10,9},{11,... | collective-permute-start | bytes 491528 | tf_op jit(solution)/shard_map/ppermute | solution.py:290
  103.3 1.0 copy.76
  104.3 3.5 %collective-permute-done.17 = f32[144,128]{1,0:T(8,128)S(1)} collective-permute-done((f32[144,128]{1,0:T(8,128)S(1)}, f32[144,128]{1,0:T(8,128)S(1)}, u32[]{:S(2)}, u32[]{:S(2)}) %collective-permute-start.17) | collective-permute-done | bytes 73760 | tf_op jit(solution)/shard_map/ppermute | solution.py:295
  107.9 4.8 %collective-permute-done.18 = f32[144,128]{1,0:T(8,128)S(1)} collective-permute-done((f32[144,128]{1,0:T(8,128)S(1)}, f32[144,128]{1,0:T(8,128)S(1)}, u32[]{:S(2)}, u32[]{:S(2)}) %collective-permute-start.18) | collective-permute-done | bytes 73760 | tf_op jit(solution)/shard_map/ppermute | solution.py:295
  113.1 2.6 %collective-permute-done.19 = f32[72,128]{1,0:T(8,128)S(1)} collective-permute-done((f32[72,128]{1,0:T(8,128)S(1)}, f32[72,128]{1,0:T(8,128)S(1)}, u32[]{:S(2)}, u32[]{:S(2)}) %collective-permute-start.19) | collective-permute-done | bytes 36896 | tf_op jit(solution)/shard_map/ppermute | solution.py:295
  115.7 0.3 collective-permute-start.20
  116.0 2.9 %shard_map.179 = f32[8,8,16,128]{3,2,1,0:T(8,128)S(1)} custom-call(f32[10,10,32,128]{3,2,1,0:T(8,128)S(1)} %pad_maximum_fusion.gpre_ref, f32[8,8,16,128]{3,2,1,0:T(8,128)S(1)} %copy-done.1, f32[72,288]{1,0:T(8,128)S(1)} %pad_maximum_fusion.21.wd_ref), custom_call_target="tpu_custom_call" | custom-call | flops 1000000000 | bytes 4000000 | tf_op jit(solution)/shard_map/pallas_call | solution.py:273
  118.9 1.0 copy.77
  120.0 0.6 slice_bitcast_fusion.1
  120.5 0.7 slice.191
  121.3 0.7 copy.74
  122.0 0.7 slice_reduce_fusion.1
  122.7 0.7 slice.195
  123.4 0.6 slice_bitcast_fusion
  124.0 0.7 slice_reduce_fusion
  124.9 0.8 copy.75
  (121 shorter events, 4.6 us)
Async XLA Ops:
  0.6 1.3 %copy-start.7 = (f32[64,4,4,128]{3,2,1,0:T(4,128)S(1)}, f32[64,4,4,128]{3,2,1,0:T(4,128)}, u32[]{:S(2)}) copy-start(f32[64,4,4,128]{3,2,1,0:T(4,128)} %param.11) | copy-start | bytes 1572868
  2.2 5.5 %copy-start.6 = (f32[27,64,32]{1,2,0:T(8,128)S(1)}, f32[27,64,32]{1,2,0:T(8,128)}, u32[]{:S(2)}) copy-start(f32[27,64,32]{1,2,0:T(8,128)} %param.16) | copy-start | bytes 663556
  3.1 7.4 %collective-permute-start = (f32[16,32,128]{2,1,0:T(8,128)}, f32[16,32,128]{2,1,0:T(8,128)}, u32[]{:S(2)}, u32[]{:S(2)}) collective-permute-start(f32[16,32,128]{2,1,0:T(8,128)} %get-tuple-element.73), channel_id=1, source_target_pairs={{16,32},{32,16},{48,64},{64,48},{80,96},{96,80},{112,128},{128,112... | collective-permute-start | bytes 786440 | tf_op jit(solution)/shard_map/ppermute | solution.py:290
  4.5 9.3 %collective-permute-start.1 = (f32[16,32,128]{2,1,0:T(8,128)}, f32[16,32,128]{2,1,0:T(8,128)}, u32[]{:S(2)}, u32[]{:S(2)}) collective-permute-start(f32[16,32,128]{2,1,0:T(8,128)} %get-tuple-element.74), channel_id=1, source_target_pairs={{0,16},{16,0},{32,48},{48,32},{64,80},{80,64},{96,112},{112,96},{1... | collective-permute-start | bytes 786440 | tf_op jit(solution)/shard_map/ppermute | solution.py:289
  8.5 0.9 copy-start.9
  8.5 1.0 copy-start.12
  8.6 1.1 copy-start.13
  8.6 1.1 copy-start.8
  8.9 1.0 copy-start.10
  15.1 16.4 %collective-permute-start.2 = (f32[28,32,128]{2,1,0:T(8,128)S(1)}, f32[28,32,128]{2,1,0:T(8,128)S(1)}, u32[]{:S(2)}, u32[]{:S(2)}) collective-permute-start(f32[28,32,128]{2,1,0:T(8,128)S(1)} %get-tuple-element.61), channel_id=1, source_target_pairs={{1,2},{2,1},{3,4},{4,3},{5,6},{6,5},{7,8},{8,7},{9,10},{10,9},{11,... | collective-permute-start | bytes 1376264 | tf_op jit(solution)/shard_map/ppermute | solution.py:290
  25.3 6.2 %collective-permute-start.3 = (f32[28,32,128]{2,1,0:T(8,128)S(1)}, f32[28,32,128]{2,1,0:T(8,128)S(1)}, u32[]{:S(2)}, u32[]{:S(2)}) collective-permute-start(f32[28,32,128]{2,1,0:T(8,128)S(1)} %get-tuple-element.62), channel_id=1, source_target_pairs={{0,1},{1,0},{2,3},{3,2},{4,5},{5,4},{6,7},{7,6},{8,9},{9,8},{10,11... | collective-permute-start | bytes 1376264 | tf_op jit(solution)/shard_map/ppermute | solution.py:289
  31.9 14.5 %copy-start.11 = (f32[16,32]{1,0:T(8,128)S(1)}, f32[16,32]{1,0:T(8,128)}, u32[]{:S(2)}) copy-start(f32[16,32]{1,0:T(8,128)} %param.14) | copy-start | bytes 6148
  31.9 14.6 %copy-start.14 = (f32[32]{0:T(128)S(1)}, f32[32]{0:T(128)}, u32[]{:S(2)}) copy-start(f32[32]{0:T(128)} %param.13) | copy-start | bytes 388
  31.9 14.7 %copy-start.15 = (f32[16]{0:T(128)S(1)}, f32[16]{0:T(128)}, u32[]{:S(2)}) copy-start(f32[16]{0:T(128)} %param.15) | copy-start | bytes 196
  44.7 0.8 copy-start.2
  45.5 0.8 copy-start.4
  46.4 10.7 %collective-permute-start.8 = (f32[288,128]{1,0:T(8,128)S(1)}, f32[288,128]{1,0:T(8,128)S(1)}, u32[]{:S(2)}, u32[]{:S(2)}) collective-permute-start(f32[288,128]{1,0:T(8,128)S(1)} %slice_select_fusion), channel_id=1, source_target_pairs={{0,1},{1,0},{2,3},{3,2},{4,5},{5,4},{6,7},{7,6},{8,9},{9,8},{10,11... | collective-permute-start | bytes 442376 | tf_op jit(solution)/shard_map/ppermute | solution.py:295
  46.7 1.1 copy-start.3
  47.8 1.0 copy-start.5
  56.4 2.2 %copy-start = (f32[8,8,16,128]{3,2,1,0:T(8,128)}, f32[8,8,16,128]{3,2,1,0:T(8,128)S(1)}, u32[]{:S(2)}) copy-start(f32[8,8,16,128]{3,2,1,0:T(8,128)S(1)} %get-tuple-element.21.cot_ref) | copy-start | bytes 1572868
  56.4 2.2 %collective-permute-start.11 = (f32[72,128]{1,0:T(8,128)S(1)}, f32[72,128]{1,0:T(8,128)S(1)}, u32[]{:S(2)}, u32[]{:S(2)}) collective-permute-start(f32[72,128]{1,0:T(8,128)S(1)} %get-tuple-element.23), channel_id=1, source_target_pairs={{0,1},{1,0},{2,3},{3,2},{4,5},{5,4},{6,7},{7,6},{8,9},{9,8},{10,11... | collective-permute-start | bytes 110600 | tf_op jit(solution)/shard_map/ppermute | solution.py:295
  57.1 4.5 %collective-permute-start.9 = (f32[144,128]{1,0:T(8,128)S(1)}, f32[144,128]{1,0:T(8,128)S(1)}, u32[]{:S(2)}, u32[]{:S(2)}) collective-permute-start(f32[144,128]{1,0:T(8,128)S(1)} %slice_select_fusion.3), channel_id=1, source_target_pairs={{0,16},{16,0},{32,48},{48,32},{64,80},{80,64},{96,112},{112,96},{1... | collective-permute-start | bytes 221192 | tf_op jit(solution)/shard_map/ppermute | solution.py:295
  58.6 2.9 %collective-permute-start.12 = (f32[72,128]{1,0:T(8,128)S(1)}, f32[72,128]{1,0:T(8,128)S(1)}, u32[]{:S(2)}, u32[]{:S(2)}) collective-permute-start(f32[72,128]{1,0:T(8,128)S(1)} %add.98), channel_id=1, source_target_pairs={{0,16},{16,0},{32,48},{48,32},{64,80},{80,64},{96,112},{112,96},{1... | collective-permute-start | bytes 110600 | tf_op jit(solution)/shard_map/ppermute | solution.py:295
  61.5 6.6 %collective-permute-start.13 = (f32[72,128]{1,0:T(8,128)S(1)}, f32[72,128]{1,0:T(8,128)S(1)}, u32[]{:S(2)}, u32[]{:S(2)}) collective-permute-start(f32[72,128]{1,0:T(8,128)S(1)} %add.99), channel_id=1, source_target_pairs={{0,2},{1,3},{2,0},{3,1},{4,6},{5,7},{6,4},{7,5},{8,10},{9,11},{10,... | collective-permute-start | bytes 110600 | tf_op jit(solution)/shard_map/ppermute | solution.py:295
  61.6 6.6 %collective-permute-start.10 = (f32[72,128]{1,0:T(8,128)S(1)}, f32[72,128]{1,0:T(8,128)S(1)}, u32[]{:S(2)}, u32[]{:S(2)}) collective-permute-start(f32[72,128]{1,0:T(8,128)S(1)} %slice_select_fusion.4), channel_id=1, source_target_pairs={{0,2},{1,3},{2,0},{3,1},{4,6},{5,7},{6,4},{7,5},{8,10},{9,11},{10,... | collective-permute-start | bytes 110600 | tf_op jit(solution)/shard_map/ppermute | solution.py:295
  63.2 5.3 %collective-permute-start.4 = (f32[1,8,32,128]{3,2,1,0:T(8,128)S(1)}, f32[1,8,32,128]{3,2,1,0:T(8,128)S(1)}, u32[]{:S(2)}, u32[]{:S(2)}) collective-permute-start(f32[1,8,32,128]{3,2,1,0:T(8,128)S(1)} %get-tuple-element.57), channel_id=1, source_target_pairs={{16,32},{32,16},{48,64},{64,48},{80,96},{96,80},{112,128},{128,112... | collective-permute-start | bytes 393224 | tf_op jit(solution)/shard_map/ppermute | solution.py:290
  63.8 6.7 %collective-permute-start.5 = (f32[1,8,32,128]{3,2,1,0:T(8,128)S(1)}, f32[1,8,32,128]{3,2,1,0:T(8,128)S(1)}, u32[]{:S(2)}, u32[]{:S(2)}) collective-permute-start(f32[1,8,32,128]{3,2,1,0:T(8,128)S(1)} %get-tuple-element.58), channel_id=1, source_target_pairs={{0,16},{16,0},{32,48},{48,32},{64,80},{80,64},{96,112},{112,96},{1... | collective-permute-start | bytes 393224 | tf_op jit(solution)/shard_map/ppermute | solution.py:289
  68.2 5.0 %collective-permute-start.14 = (f32[144,128]{1,0:T(8,128)S(1)}, f32[144,128]{1,0:T(8,128)S(1)}, u32[]{:S(2)}, u32[]{:S(2)}) collective-permute-start(f32[144,128]{1,0:T(8,128)S(1)} %pad_maximum_fusion.22), channel_id=1, source_target_pairs={{0,4},{1,5},{2,6},{3,7},{4,0},{5,1},{6,2},{7,3},{8,12},{9,13},{10,... | collective-permute-start | bytes 221192 | tf_op jit(solution)/shard_map/ppermute | solution.py:295
  73.2 7.2 %collective-permute-start.15 = (f32[144,128]{1,0:T(8,128)S(1)}, f32[144,128]{1,0:T(8,128)S(1)}, u32[]{:S(2)}, u32[]{:S(2)}) collective-permute-start(f32[144,128]{1,0:T(8,128)S(1)} %fusion.4), channel_id=1, source_target_pairs={{0,8},{1,9},{2,10},{3,11},{4,12},{5,13},{6,14},{7,15},{8,0},{9,1},... | collective-permute-start | bytes 221192 | tf_op jit(solution)/shard_map/ppermute | solution.py:295
  80.4 22.7 %collective-permute-start.16 = (f32[144,128]{1,0:T(8,128)S(1)}, f32[144,128]{1,0:T(8,128)S(1)}, u32[]{:S(2)}, u32[]{:S(2)}) collective-permute-start(f32[144,128]{1,0:T(8,128)S(1)} %add.102), channel_id=1, source_target_pairs={{0,32},{16,48},{32,0},{48,16},{64,96},{80,112},{96,64},{112,80},{1... | collective-permute-start | bytes 221192 | tf_op jit(solution)/shard_map/ppermute | solution.py:295
  89.0 18.9 %collective-permute-start.7 = (f32[10,1,32,128]{3,2,1,0:T(8,128)S(1)}, f32[10,1,32,128]{3,2,1,0:T(8,128)S(1)}, u32[]{:S(2)}, u32[]{:S(2)}) collective-permute-start(f32[10,1,32,128]{3,2,1,0:T(8,128)S(1)} %broadcast_select_fusion.6), channel_id=1, source_target_pairs={{0,1},{1,0},{2,3},{3,2},{4,5},{5,4},{6,7},{7,6},{8,9},{9,8},{10,11... | collective-permute-start | bytes 491528 | tf_op jit(solution)/shard_map/ppermute | solution.py:289
  93.6 14.3 %collective-permute-start.6 = (f32[10,1,32,128]{3,2,1,0:T(8,128)S(1)}, f32[10,1,32,128]{3,2,1,0:T(8,128)S(1)}, u32[]{:S(2)}, u32[]{:S(2)}) collective-permute-start(f32[10,1,32,128]{3,2,1,0:T(8,128)S(1)} %get-tuple-element.54), channel_id=1, source_target_pairs={{1,2},{2,1},{3,4},{4,3},{5,6},{6,5},{7,8},{8,7},{9,10},{10,9},{11,... | collective-permute-start | bytes 491528 | tf_op jit(solution)/shard_map/ppermute | solution.py:290
  103.1 4.6 %collective-permute-start.17 = (f32[144,128]{1,0:T(8,128)S(1)}, f32[144,128]{1,0:T(8,128)S(1)}, u32[]{:S(2)}, u32[]{:S(2)}) collective-permute-start(f32[144,128]{1,0:T(8,128)S(1)} %add.103), channel_id=1, source_target_pairs={{0,64},{16,80},{32,96},{48,112},{64,0},{80,16},{96,32},{112,48},{1... | collective-permute-start | bytes 221192 | tf_op jit(solution)/shard_map/ppermute | solution.py:295
  107.8 5.0 %collective-permute-start.18 = (f32[144,128]{1,0:T(8,128)S(1)}, f32[144,128]{1,0:T(8,128)S(1)}, u32[]{:S(2)}, u32[]{:S(2)}) collective-permute-start(f32[144,128]{1,0:T(8,128)S(1)} %add.104), channel_id=1, source_target_pairs={{0,128},{16,144},{32,160},{48,176},{64,192},{80,208},{96,224},{112... | collective-permute-start | bytes 221192 | tf_op jit(solution)/shard_map/ppermute | solution.py:295
  112.8 2.9 %collective-permute-start.19 = (f32[72,128]{1,0:T(8,128)S(1)}, f32[72,128]{1,0:T(8,128)S(1)}, u32[]{:S(2)}, u32[]{:S(2)}) collective-permute-start(f32[72,128]{1,0:T(8,128)S(1)} %slice.193), channel_id=1, source_target_pairs={{0,2},{1,3},{2,0},{3,1},{4,6},{5,7},{6,4},{7,5},{8,10},{9,11},{10,... | collective-permute-start | bytes 110600 | tf_op jit(solution)/shard_map/ppermute | solution.py:295
  112.9 3.1 %copy-start.1 = (f32[8,8,16,128]{3,2,1,0:T(8,128)S(1)}, f32[8,8,16,128]{3,2,1,0:T(8,128)}, u32[]{:S(2)}) copy-start(f32[8,8,16,128]{3,2,1,0:T(8,128)} %copy-done) | copy-start | bytes 1572868
  115.7 4.1 %collective-permute-start.20 = (f32[144,128]{1,0:T(8,128)S(1)}, f32[144,128]{1,0:T(8,128)S(1)}, u32[]{:S(2)}, u32[]{:S(2)}) collective-permute-start(f32[144,128]{1,0:T(8,128)S(1)} %pad_maximum_fusion.23), channel_id=1, source_target_pairs={{0,16},{16,0},{32,48},{48,32},{64,80},{80,64},{96,112},{112,96},{1... | collective-permute-start | bytes 221192 | tf_op jit(solution)/shard_map/ppermute | solution.py:295
  119.9 2.8 %collective-permute-start.21 = (f32[288,128]{1,0:T(8,128)S(1)}, f32[288,128]{1,0:T(8,128)S(1)}, u32[]{:S(2)}, u32[]{:S(2)}) collective-permute-start(f32[288,128]{1,0:T(8,128)S(1)} %pad_maximum_fusion.18), channel_id=1, source_target_pairs={{0,1},{1,0},{2,3},{3,2},{4,5},{5,4},{6,7},{7,6},{8,9},{9,8},{10,11... | collective-permute-start | bytes 442376 | tf_op jit(solution)/shard_map/ppermute | solution.py:295

commit v2 on v1

v2 whole, which is shorter than its diff:
```python
import jax
import jax.numpy as jnp
from jax import lax
from jax.experimental import pallas as pl
from jax.experimental.pallas import tpu as pltpu
from jax.sharding import PartitionSpec as P

f32 = jnp.float32
bf16 = jnp.bfloat16
VMEM_BYTES = 24 * 1024 * 1024


def dot(a, b):
    return lax.dot_general(a, b, (((1,), (0,)), ((), ())), preferred_element_type=f32)


def dot_cells(a, b):
    return lax.dot_general(a, b, (((1,), (1,)), ((), ())), preferred_element_type=f32)


def split(x):
    top = x.astype(bf16).astype(f32)
    return top, x - top


def stacked(x, spare=0):
    top, rest = split(x)
    rows = [top, rest, top]
    if spare:
        rows.append(jnp.zeros((spare, x.shape[1]), f32))
    return jnp.concatenate(rows, axis=0).astype(bf16)


def thrice(x):
    top, rest = split(x)
    return jnp.concatenate([top, top, rest], axis=0)


def row_of(ref, x, first, count):
    return jnp.concatenate([ref[x, first + y] for y in range(count)], axis=1)


def shifted(x, step):
    lane = lax.broadcasted_iota(jnp.int32, (x.shape[0], 128), 1)
    edge = 0 if step > 0 else 127
    out = []
    for k in range(x.shape[1] // 128):
        moved = pltpu.roll(x[:, 128 * k : 128 * (k + 1)], step % 128, 1)
        out.append(jnp.where(lane == edge, 0.0, moved))
    return jnp.concatenate(out, axis=1)


def taps_along_z(x):
    return jnp.concatenate([shifted(x, 1), x, shifted(x, -1)], axis=0)


def window(o, rows, width, backward):
    parts = []
    for b in range(3):
        at = (2 - b if backward else b) * 128
        parts.append(o[b * rows : (b + 1) * rows, at : at + width])
    return parts[0] + parts[1] + parts[2]


def coupling(pre, v, dv, pj, pt, bo):
    half = v.shape[0]
    sig = jax.nn.sigmoid(pre)
    act = pre * sig
    out = dot(pj, stacked(act)) + bo
    sc = jnp.tanh(out[:half])
    centred = v - out[half:]
    lower = centred * jnp.exp(-sc)
    lower_cot = dv * jnp.exp(sc)
    g = jnp.concatenate([dv * centred * (1.0 - sc * sc), dv], axis=0)
    ga = dot(pt, stacked(g))
    gpre = ga * sig * (1.0 + pre * (1.0 - sig))
    return act, g, gpre, lower, lower_cot


def placed_at(x, before, after):
    rows = x.shape[0]
    parts = []
    if before:
        parts.append(jnp.zeros((rows, 128 * before), f32))
    parts.append(x)
    if after:
        parts.append(jnp.zeros((rows, 128 * after), f32))
    return jnp.concatenate(parts, axis=1) if len(parts) > 1 else x


def weight_products(patch, gpre, act, g):
    tops, rests = [], []
    for piece in [placed_at(gpre, b, 2 - b) for b in range(3)] + [placed_at(act, 1, 1)]:
        top, rest = split(piece)
        tops.append(top)
        rests.append(rest)
    right = jnp.concatenate(tops + rests, axis=0).astype(bf16)
    p_top, p_rest = split(patch)
    g_top, g_rest = split(placed_at(g, 1, 1))
    ones = jnp.ones((16, patch.shape[1]), f32)
    first = jnp.concatenate([p_top, ones, g_top], axis=0).astype(bf16)
    second = jnp.concatenate([p_rest, g_rest], axis=0).astype(bf16)
    wide = right.shape[0] // 2
    a = dot_cells(first, right)
    b = dot_cells(second, right[:wide])
    return a[:, :wide] + a[:, wide:], b


def lane_sum(x):
    total = x[:, :128]
    for k in range(1, x.shape[1] // 128):
        total = total + x[:, 128 * k : 128 * (k + 1)]
    return total


def gathered(first, second, g_sum, taps, outs, lane_of_outs):
    conv = first[:taps] + second[:taps]
    bias_in = first[taps : taps + 8]
    proj = first[taps + 16 :] + second[taps:]
    total = jnp.broadcast_to(jnp.sum(g_sum, axis=1, keepdims=True), (outs, 128))
    row = lax.broadcasted_iota(jnp.int32, (outs, 128), 0)
    lane = lax.broadcasted_iota(jnp.int32, (outs, 128), 1)
    bias_out = jnp.sum(jnp.where(lane == row + lane_of_outs, total, 0.0), axis=0, keepdims=True)
    return conv, bias_in, proj, jnp.broadcast_to(bias_out, (8, 128))


def lanes_from(at, upper, lower):
    lane = lax.broadcasted_iota(jnp.int32, upper.shape, 1)
    return jnp.where(lane >= at, upper, lower)


def column(row):
    n = row.shape[1]
    i = lax.broadcasted_iota(jnp.int32, (n, n), 0)
    j = lax.broadcasted_iota(jnp.int32, (n, n), 1)
    return jnp.sum(jnp.where(i == j, jnp.broadcast_to(row, (n, n)), 0.0), axis=1, keepdims=True)


def forward_weight(conv_ref, spare):
    h = conv_ref.shape[2]
    parts = []
    for b in range(3):
        w = jnp.concatenate([conv_ref[9 * a + 3 * b + c] for a in range(3) for c in range(3)], axis=0)
        rows = thrice(w)
        if spare:
            rows = jnp.concatenate([rows, jnp.zeros((spare, h), f32)], axis=0)
        parts.append(rows.T)
    return jnp.concatenate(parts, axis=0).astype(bf16)


def back_weight(conv_ref):
    w = [jnp.concatenate([conv_ref[9 * a + t] for t in range(9)], axis=0).T for a in range(3)]
    return thrice(jnp.concatenate(w, axis=0)).T.astype(bf16)


def projections(proj_ref):
    p = proj_ref[...]
    return thrice(p.T).T.astype(bf16), thrice(p).T.astype(bf16)


def transposed_block(ref, first, last, x):
    return jnp.swapaxes(ref[first:last, x], 0, 1)


def ends_kernel(at_ref, w_ref, u_ref, one_ref, two_ref):
    nx, ny, k = u_ref.shape[0], u_ref.shape[1], u_ref.shape[2]
    even = at_ref[1] % 2 == 0
    for x in range(nx):
        u = transposed_block(w_ref, 0, k, x)
        u_ref[x] = u
        low, high = u[:2], u[ny - 2 :]
        one_ref[x] = lax.select(even, high, low)
        two_ref[x] = lax.select(even, low, high)


def ends_vd_kernel(at_ref, w_ref, dw_ref, vd_ref, cot_ref, one_ref, two_ref):
    nx, ny, k = cot_ref.shape[0], cot_ref.shape[1], cot_ref.shape[2]
    even = at_ref[1] % 2 == 0
    for x in range(nx):
        cot_ref[x] = transposed_block(dw_ref, 0, k, x)
        vd = jnp.concatenate([transposed_block(w_ref, k, 2 * k, x), transposed_block(dw_ref, k, 2 * k, x)], axis=1)
        vd_ref[x] = vd
        low, high = vd[:1], vd[ny - 1 :]
        one_ref[x] = lax.select(even, high, low)
        two_ref[x] = lax.select(even, low, high)


def sides_kernel(at_ref, f_ref, ya_ref, yb_ref, one_ref, two_ref):
    nx, rows = f_ref.shape[0], one_ref.shape[0]
    even_x, even_y = at_ref[0] % 2 == 0, at_ref[1] % 2 == 0

    def widened(x):
        a, b = ya_ref[x], yb_ref[x]
        return jnp.concatenate([lax.select(even_y, b, a), f_ref[x], lax.select(even_y, a, b)], axis=0)

    for x in range(rows):
        low, high = widened(x), widened(nx - rows + x)
        one_ref[x] = lax.select(even_x, high, low)
        two_ref[x] = lax.select(even_x, low, high)


def conv_inner_kernel(at_ref, u_ref, ya_ref, yb_ref, conv_ref, in_ref, taps_ref, pre_ref, wp_ref, bi_ref):
    nx, ny, k = u_ref.shape[0], u_ref.shape[1], u_ref.shape[2]
    h = conv_ref.shape[2]
    wp = forward_weight(conv_ref, 0)
    wp_ref[...] = wp.astype(f32)
    bi = column(in_ref[...])
    bi_ref[...] = bi
    even_y = at_ref[1] % 2 == 0
    taps = []
    for x in range(nx):
        a, b = row_of(ya_ref, x, 0, 2), row_of(yb_ref, x, 0, 2)
        low, high = lax.select(even_y, b, a), lax.select(even_y, a, b)
        taps_ref[x] = taps_along_z(jnp.concatenate([low, row_of(u_ref, x, 0, ny), high], axis=1))
    for x in range(nx - 2):
        patch = jnp.concatenate([taps_ref[x], taps_ref[x + 1], taps_ref[x + 2]], axis=0)
        pre_ref[x] = window(dot(wp, stacked(patch)), h, (ny + 2) * 128, False) + bi


def conv_outer_kernel(at_ref, inner_ref, xa_ref, xb_ref, wp_ref, bi_ref, taps_ref, pre_ref):
    nx, columns = inner_ref.shape[0], xa_ref.shape[1]
    h = bi_ref.shape[0]
    wp = wp_ref[...].astype(bf16)
    even_x = at_ref[0] % 2 == 0
    for x in range(2):
        a, b = row_of(xa_ref, x, 0, columns), row_of(xb_ref, x, 0, columns)
        taps_ref[x] = taps_along_z(lax.select(even_x, b, a))
        taps_ref[x + 2] = taps_along_z(lax.select(even_x, a, b))
    rows = [taps_ref[0], taps_ref[1], inner_ref[0], inner_ref[1], inner_ref[nx - 2], inner_ref[nx - 1], taps_ref[2], taps_ref[3]]
    for i, at in enumerate((0, 1, 4, 5)):
        patch = jnp.concatenate(rows[at : at + 3], axis=0)
        pre_ref[i] = window(dot(wp, stacked(patch)), h, (columns - 2) * 128, False) + bi_ref[...]


def coarse_kernel(factor, size_x, size_y, at_ref, inner_ref, outer_ref, pre_in_ref, pre_out_ref, vd_ref, ya_ref, yb_ref, xa_ref, xb_ref,
                  proj_ref, out_ref, q_ref, gpre_ref, low_ref, grads_ref,
                  act_s, g_s, sums, rests, g_sum):
    nx, ny, k = vd_ref.shape[0], vd_ref.shape[1], vd_ref.shape[2] // 2
    wide, own = (ny + 2) * 128, slice(128, 128 * (ny + 1))
    pj, pt = projections(proj_ref)
    bo = column(out_ref[...])
    even_x, even_y = at_ref[0] % 2 == 0, at_ref[1] % 2 == 0
    taps = [(outer_ref, 0), (outer_ref, 1)] + [(inner_ref, x) for x in range(nx)] + [(outer_ref, 2), (outer_ref, 3)]
    pres = [(pre_out_ref, 0), (pre_out_ref, 1)] + [(pre_in_ref, x) for x in range(nx - 2)] + [(pre_out_ref, 2), (pre_out_ref, 3)]
    low_x = jnp.where(at_ref[0] == 0, 0.0, 1.0)
    high_x = jnp.where(at_ref[0] == size_x - 1, 0.0, 1.0)
    low_y = jnp.where(at_ref[1] == 0, 0.0, 1.0)
    high_y = jnp.where(at_ref[1] == size_y - 1, 0.0, 1.0)

    def forward(x, vd, inside):
        pre_ref, at = pres[x]
        act, g, gpre, lower, lower_cot = coupling(pre_ref[at], vd[:k], vd[k:], pj, pt, bo)
        taps_ref, at = taps[x + 1]
        u = taps_ref[at][k : 2 * k, 128 : 128 + wide]
        for y in range(ny + 2):
            cols = slice(128 * y, 128 * (y + 1))
            here = inside * (low_y if y == 0 else high_y if y == ny + 1 else 1.0)
            q_ref[x, y, :k] = u[:, cols]
            q_ref[x, y, k:] = lower[:, cols] * here
        gpre_ref[x] = gpre
        return act, g, lower_cot

    sums[...] = jnp.zeros_like(sums)
    rests[...] = jnp.zeros_like(rests)
    g_sum[...] = jnp.zeros_like(g_sum)

    for x in range(nx):
        a, b = ya_ref[x, 0], yb_ref[x, 0]
        vd = jnp.concatenate([lax.select(even_y, b, a), row_of(vd_ref, x, 0, ny), lax.select(even_y, a, b)], axis=1)
        act, g, lower_cot = forward(x + 1, vd, 1.0)
        low_ref[x] = lower_cot[:, own]
        act_s[x] = act[:, own]
        g_s[x] = g[:, own]
    a, b = row_of(xa_ref, 0, 0, ny + 2), row_of(xb_ref, 0, 0, ny + 2)
    forward(0, lax.select(even_x, b, a), low_x)
    forward(nx + 1, lax.select(even_x, a, b), high_x)

    for x in range(nx):
        patch = jnp.concatenate([ref[at][:, 128 : 128 + wide] for ref, at in taps[x + 1 : x + 4]], axis=0)
        a, b = weight_products(patch, gpre_ref[x + 1][:, own], act_s[x], g_s[x])
        sums[...] += a
        rests[...] += b
        g_sum[...] += lane_sum(g_s[x])
    rows, fold = 9 * k, 9 * k // 2
    conv, bias_in, proj, bias_out = gathered(sums[...], rests[...], g_sum[...], rows, 2 * k, 64)
    grads_ref[:rows] = conv[:, :128] * factor
    second = conv[:, 128:] * factor
    grads_ref[rows : rows + fold] = lanes_from(64, pltpu.roll(second[fold:], 64, 1), second[:fold])
    proj = proj[:, 128:] * factor
    at = rows + fold
    grads_ref[at : at + k] = lanes_from(64, proj[k:], pltpu.roll(proj[:k], 64, 1))
    grads_ref[at + k : at + k + 8] = lanes_from(64, bias_out, bias_in[:, :128]) * factor
    grads_ref[at + k + 8 :] = jnp.zeros((grads_ref.shape[0] - at - k - 8, 128), f32)


def coarse_back_kernel(gpre_ref, low_ref, cot_ref, conv_ref, dq_ref):
    nx, ny, k = low_ref.shape[0], cot_ref.shape[1], low_ref.shape[1]
    wd = back_weight(conv_ref)

    def back(x, _):
        parts = jnp.concatenate([gpre_ref[x + 2], gpre_ref[x + 1], gpre_ref[x]], axis=0)
        s = window(dot(wd, stacked(parts)), 3 * k, ny * 128, True)
        du = s[k : 2 * k] + shifted(s[:k], -1) + shifted(s[2 * k :], 1)
        low = low_ref[x]
        for y in range(ny):
            cols = slice(128 * y, 128 * (y + 1))
            dq_ref[x, y, :k] = cot_ref[x, y] + du[:, cols]
            dq_ref[x, y, k:] = low[:, cols]
        return 0

    lax.fori_loop(0, nx, back, 0, unroll=True)


def finer_rows(field):
    c = field.shape[0] // 4
    a, b, d, e = [field[i * c : (i + 1) * c] for i in range(4)]
    sum_u, sum_l, dif_u, dif_l = a + b, d + e, a - b, d - e
    rows = []
    for p, q in ((sum_u, sum_l), (dif_u, dif_l)):
        even, odd = 0.5 * (p + q), 0.5 * (p - q)
        cols = []
        for k in range(even.shape[1] // 128):
            cols += [even[:, 128 * k : 128 * (k + 1)], odd[:, 128 * k : 128 * (k + 1)]]
        rows.append(jnp.concatenate(cols, axis=1))
    return rows


def fine_kernel(factor, first, count, n_in, n_out, *refs):
    q_ref, dq_ref, conv_ref, in_ref, proj_ref, out_ref = refs[:6]
    before = refs[6:n_in]
    field_ref, cot_ref, gpre_ref, *grads_ref = refs[n_in : n_in + n_out]
    scratch = refs[n_in + n_out :]
    taps, v_s, dz_s = scratch[:3]
    sums, rests, g_sum = scratch[3:] if before else grads_ref
    ny = field_ref.shape[1]
    k = field_ref.shape[2] // 2
    h = conv_ref.shape[2]
    wp = forward_weight(conv_ref, 8)
    pj, pt = projections(proj_ref)
    bi, bo = column(in_ref[...]), column(out_ref[...])
    cy = ny // 2

    for x in range(q_ref.shape[0]):
        wanted = [r for r in (2 * x, 2 * x + 1) if first + 1 <= r <= first + count + 2]
        if wanted:
            pair = finer_rows(row_of(q_ref, x, 0, cy + 2))
        for r in wanted:
            z = pair[r - 2 * x]
            taps[r - 1 - first] = taps_along_z(z[:k, 128 : 128 * (ny + 3)])
            if first + 2 <= r < first + count + 2:
                v_s[r - 2 - first] = z[k:, 256 : 128 * (ny + 2)]
    for x in range(first // 2, (first + count) // 2):
        pair = finer_rows(row_of(dq_ref, x, 0, cy))
        dz_s[2 * x - first] = pair[0]
        dz_s[2 * x + 1 - first] = pair[1]

    if before:
        sums[...], rests[...], g_sum[...] = before[3][...], before[4][...], before[5][...]
        for ref, old in zip((field_ref, cot_ref, gpre_ref), before):
            ref[:first] = old[...]
    else:
        sums[...] = jnp.zeros_like(sums)
        rests[...] = jnp.zeros_like(rests)
        g_sum[...] = jnp.zeros_like(g_sum)
    at = first if before else 0

    for x in range(count):
        patch = jnp.concatenate([taps[x], taps[x + 1], taps[x + 2]], axis=0)
        pre = window(dot(wp, stacked(patch, 8)), h, ny * 128, False) + bi
        dz = dz_s[x]
        act, g, gpre, lower, lower_cot = coupling(pre, v_s[x], dz[k:], pj, pt, bo)
        a, b = weight_products(patch, gpre, act, g)
        sums[...] += a
        rests[...] += b
        g_sum[...] += lane_sum(g)
        field = jnp.concatenate([taps[x + 1][k : 2 * k, 128 : 128 * (ny + 1)], lower], axis=0)
        cot = jnp.concatenate([dz[:k], lower_cot], axis=0)
        for y in range(ny):
            cols = slice(128 * y, 128 * (y + 1))
            field_ref[at + x, y] = field[:, cols]
            cot_ref[at + x, y] = cot[:, cols]
            gpre_ref[at + x, y] = gpre[:, cols]

    if before:
        (grads,) = grads_ref
        conv, bias_in, proj, bias_out = gathered(sums[...], rests[...], g_sum[...], 9 * k, 2 * k, 3 * h)
        spare = jnp.zeros((9 * k - 2 * k - 16, 128), f32)
        others = jnp.concatenate([proj, pltpu.roll(bias_in, h, 1), bias_out, spare], axis=0)
        grads[: 9 * k] = lanes_from(3 * h, others, conv) * factor
        grads[9 * k :] = jnp.zeros((grads.shape[0] - 9 * k, 128), f32)


def fine_back_kernel(gpre_ref, cot_ref, conv_ref, out_ref, columns_ref, rows_ref, gpre_s):
    nx, ny = cot_ref.shape[0], cot_ref.shape[1]
    k = cot_ref.shape[2] // 2
    h = gpre_ref.shape[2]
    wd = back_weight(conv_ref)
    for x in (0, 1, nx + 2, nx + 3):
        gpre_s[x] = jnp.zeros((h, ny * 128), f32)

    def fill(x, _):
        gpre_s[x + 2] = row_of(gpre_ref, x, 0, ny)
        return 0

    lax.fori_loop(0, nx, fill, 0, unroll=True)

    def contributions(x):
        parts = jnp.concatenate([gpre_s[x + 2], gpre_s[x + 1], gpre_s[x]], axis=0)
        o = dot(wd, stacked(parts))
        s = [placed_at(o[b * 3 * k : (b + 1) * 3 * k], b, 2 - b) for b in range(3)]
        s = s[0] + s[1] + s[2]
        du = s[k : 2 * k] + shifted(s[:k], -1) + shifted(s[2 * k :], 1)
        columns_ref[0, x] = du[:, :128]
        columns_ref[1, x] = du[:, 128 * (ny + 1) :]
        return du

    def inner(x, _):
        du = contributions(x + 1)
        for y in range(ny):
            out_ref[x, y, :k] = cot_ref[x, y, :k] + du[:, 128 * (y + 1) : 128 * (y + 2)]
            out_ref[x, y, k:] = cot_ref[x, y, k:]
        return 0

    def outer(i, _):
        du = contributions(i * (nx + 1))
        for y in range(ny):
            rows_ref[i, y] = du[:, 128 * (y + 1) : 128 * (y + 2)]
        return 0

    lax.fori_loop(0, nx, inner, 0, unroll=True)
    lax.fori_loop(0, 2, outer, 0, unroll=True)


def unpack_kernel(at_ref, coarse_ref, coarse_other, fine_ref, fine_other,
                  f_conv, f_in, f_proj, f_out, c_conv, c_in, c_proj, c_out, coarse, fine):
    first = at_ref[1] % 2 == 0
    for whole, mine, other in ((coarse, coarse_ref, coarse_other), (fine, fine_ref, fine_other)):
        rows = mine.shape[0]
        a, b = mine[...], other[...]
        whole[:rows] = lax.select(first, a, b)
        whole[rows:] = lax.select(first, b, a)

    k, h = c_conv.shape[1], c_conv.shape[2]
    rows, fold = 9 * k, 9 * k // 2
    ahead = coarse[:rows]
    second = coarse[rows : rows + fold]
    taps = [ahead, pltpu.roll(ahead, 64, 1), jnp.concatenate([second, pltpu.roll(second, 64, 1)], axis=0)]
    for t in range(27):
        a, b, c = t // 9, t // 3 % 3, t % 3
        c_conv[t] = taps[b][(3 * a + c) * k : (3 * a + c + 1) * k, :h]
    at = rows + fold
    proj = coarse[at : at + k]
    c_proj[:k] = proj[:, :h]
    c_proj[k:] = pltpu.roll(proj, 64, 1)[:, :h]
    biases = coarse[at + k : at + k + 8]
    c_in[...] = biases[:1, :h]
    c_out[...] = pltpu.roll(biases, 64, 1)[:1, : 2 * k]

    k, h = f_conv.shape[1], f_conv.shape[2]
    whole = fine[: 9 * k]
    parts = [whole] + [pltpu.roll(whole, 128 - b * h, 1) for b in (1, 2, 3)]
    for t in range(27):
        a, b, c = t // 9, t // 3 % 3, t % 3
        f_conv[t] = parts[b][(3 * a + c) * k : (3 * a + c + 1) * k, :h]
    f_proj[...] = parts[3][: 2 * k, :h]
    f_in[...] = parts[3][2 * k : 2 * k + 1, :h]
    f_out[...] = parts[3][2 * k + 8 : 2 * k + 9, : 2 * k]


def call(kernel, outs, scratch, flops, *args, scalars=False):
    specs = [pl.BlockSpec(memory_space=pltpu.VMEM)] * len(args)
    if scalars:
        specs[0] = pl.BlockSpec(memory_space=pltpu.SMEM)
    return pl.pallas_call(
        kernel,
        in_specs=specs,
        out_shape=[jax.ShapeDtypeStruct(s, f32) for s in outs],
        scratch_shapes=[pltpu.VMEM(s, f32) for s in scratch],
        compiler_params=pltpu.CompilerParams(vmem_limit_bytes=VMEM_BYTES),
        cost_estimate=pl.CostEstimate(flops=flops, bytes_accessed=1_000_000, transcendentals=0),
    )(*args)


def swapped(axis, one, two):
    size = lax.axis_size(axis)
    inner = [(i, i ^ 1) for i in range(size)]
    outer = []
    for i in range(1, size - 1, 2):
        outer += [(i, i + 1), (i + 1, i)]
    two = lax.ppermute(two, axis, outer)
    one = lax.ppermute(one, axis, inner)
    return one, two


def halos(axis, low, high):
    even = lax.axis_index(axis) % 2 == 0
    one, two = swapped(axis, jnp.where(even, high, low), jnp.where(even, low, high))
    return jnp.where(even, two, one), jnp.where(even, one, two)


def partner(x, mask):
    sizes = [lax.axis_size("gx"), lax.axis_size("gy")]
    pairs = []
    for i in range(sizes[0] * sizes[1]):
        gx, gy = divmod(i, sizes[1])
        pairs.append((i, (gx ^ mask[0]) * sizes[1] + (gy ^ mask[1])))
    return lax.ppermute(x, ("gx", "gy"), pairs)


CORE, X_NEAR, X_FAR, Y_NEAR, Y_FAR = (0, 1), (0, 2), (0, 6), (1, 0), (3, 0)
Z_ONE, Z_TWO, Z_FAR = (4, 0), (8, 0), (12, 8)


def second_half(step):
    gx, gy = lax.axis_index("gx"), lax.axis_index("gy")
    if step == CORE:
        return gy % 2 == 1
    if step == X_NEAR:
        return (gy // 2 + gy // 4) % 2 == 1
    return (gx + gx // 2) % 2 == 1


def half_sum(x, step):
    rows = x.shape[0] // 2
    upper = second_half(step)
    first, second = x[:rows], x[rows:]
    return jnp.where(upper, second, first) + partner(jnp.where(upper, first, second), step)


def in_order(mine, other, step):
    upper = second_half(step)
    return jnp.concatenate([jnp.where(upper, other, mine), jnp.where(upper, mine, other)], axis=0)


def tied(x, *others):
    return lax.optimization_barrier((x, *others))


def pair_sum(coarse, fine, step):
    both = jnp.concatenate([coarse, fine], axis=0)
    both = both + partner(both, step)
    return both[: coarse.shape[0]], both[coarse.shape[0] :]


def pair_whole(coarse, fine, step):
    other = partner(jnp.concatenate([coarse, fine], axis=0), step)
    return in_order(coarse, other[: coarse.shape[0]], step), fine + other[coarse.shape[0] :]


def local(
    coarse_out,
    coarse_cot,
    fine_conv,
    fine_bias_in,
    fine_proj,
    fine_bias_out,
    coarse_conv,
    coarse_bias_in,
    coarse_proj,
    coarse_bias_out,
):
    channels, nx, ny, nz = coarse_out.shape
    k = channels // 2
    h = coarse_conv.shape[1]
    fk, fh = fine_conv.shape[2], fine_conv.shape[1]
    size_x, size_y = lax.axis_size("gx"), lax.axis_size("gy")
    factor = float(4 * nx * ny * nz * size_x * size_y) ** -0.5
    at = jnp.stack([lax.axis_index("gx"), lax.axis_index("gy")]).astype(jnp.int32)
    c_conv, f_conv = jnp.transpose(coarse_conv, (0, 2, 1)), jnp.transpose(fine_conv, (0, 2, 1))

    u, one, two = call(
        ends_kernel, [(nx, ny, k, nz), (nx, 2, k, nz), (nx, 2, k, nz)], [], 500_000_000, at, coarse_out, scalars=True
    )
    u_y = swapped("gy", one, two)
    vd, cot_u, one, two = call(
        ends_vd_kernel,
        [(nx, ny, 2 * k, nz), (nx, ny, k, nz), (nx, 1, 2 * k, nz), (nx, 1, 2 * k, nz)],
        [],
        500_000_000,
        at,
        coarse_out,
        coarse_cot,
        scalars=True,
    )
    vd_y = swapped("gy", one, two)
    u_x = swapped("gx", *call(sides_kernel, [(2, ny + 4, k, nz)] * 2, [], 500_000_000, at, u, *u_y, scalars=True))
    inner, pre_in, wp, b_in = call(
        conv_inner_kernel,
        [(nx, 3 * k, (ny + 4) * nz), (nx - 2, h, (ny + 2) * nz), (3 * h, 27 * k), (h, 1)],
        [],
        2_500_000_000,
        at,
        u,
        *u_y,
        c_conv,
        coarse_bias_in[None, :],
        scalars=True,
    )
    vd_x = swapped("gx", *call(sides_kernel, [(1, ny + 2, 2 * k, nz)] * 2, [], 500_000_000, at, vd, *vd_y, scalars=True))
    outer, pre_out = call(
        conv_outer_kernel,
        [(4, 3 * k, (ny + 4) * nz), (4, h, (ny + 2) * nz)],
        [],
        4_000_000_000,
        at,
        inner,
        *u_x,
        wp,
        b_in,
        scalars=True,
    )
    q, c_gpre, low, coarse_grads = call(
        lambda *refs: coarse_kernel(factor, size_x, size_y, *refs),
        [(nx + 2, ny + 2, 2 * k, nz), (nx + 2, h, (ny + 2) * nz), (nx, k, ny * nz), (16 * k, 128)],
        [
            (nx, h, ny * nz),
            (nx, 2 * k, ny * nz),
            (9 * k + 16 + 2 * k, 4 * h),
            (9 * k + 2 * k, 4 * h),
            (2 * k, 128),
        ],
        6_000_000_000,
        at,
        inner,
        outer,
        pre_in,
        pre_out,
        vd,
        *vd_y,
        *vd_x,
        coarse_proj,
        coarse_bias_out[None, :],
        scalars=True,
    )
    coarse_grads = half_sum(coarse_grads, CORE)
    (dq,) = call(coarse_back_kernel, [(nx, ny, 2 * k, nz)], [], 2_500_000_000, c_gpre, low, cot_u, c_conv)
    coarse_grads, q, dq = tied(coarse_grads, q, dq)
    coarse_grads = half_sum(coarse_grads, Y_NEAR)

    fx, fy = 2 * nx, 2 * ny
    weights = (f_conv, fine_bias_in[None, :], fine_proj, fine_bias_out[None, :])
    sums_shapes = [(9 * fk + 16 + 2 * fk, 4 * fh), (9 * fk + 2 * fk, 4 * fh), (2 * fk, 128)]

    def fine(first, count, rows, last, *before):
        ins = (q, dq, *weights, *before)
        outs = [(rows, fy, 2 * fk, nz), (rows, fy, 2 * fk, nz), (rows, fy, fh, nz), *last]
        scratch = [(count + 2, 3 * fk, (fy + 2) * nz), (count, fk, fy * nz), (count, 2 * fk, fy * nz)]
        return call(
            lambda *refs: fine_kernel(factor, first, count, len(ins), len(outs), *refs),
            outs,
            scratch + (sums_shapes if before else []),
            4_500_000_000,
            *ins,
        )

    part = fine(0, nx, nx, sums_shapes)
    coarse_grads, *part = tied(coarse_grads, *part)
    coarse_grads = half_sum(coarse_grads, X_NEAR)
    field, cot, gpre, fine_grads = fine(nx, nx, fx, [(10 * fk, 128)], *part)
    coarse_grads, fine_grads = tied(coarse_grads, fine_grads)
    fine_grads = half_sum(fine_grads, CORE)

    def far(coarse, fine, steps):
        for step in steps:
            if step[0] < size_x and step[1] < size_y:
                coarse, fine = pair_sum(coarse, fine, step)
        return coarse, fine

    sums = far(coarse_grads, fine_grads, [X_FAR, Y_FAR])
    sums, gpre = tied(sums, gpre)
    cot, columns, rows = call(
        fine_back_kernel,
        [cot.shape, (2, fx + 2, fk, nz), (2, fy, fk, nz)],
        [(fx + 4, fh, fy * nz)],
        4_000_000_000,
        gpre,
        cot,
        f_conv,
    )
    sums = far(*sums, [Z_TWO, Z_ONE])
    sums, columns = tied(sums, columns)
    low, high = halos("gy", columns[0], columns[1])
    rows = jnp.concatenate([rows[:, :1] + low[:: fx + 1, None], rows[:, 1:-1], rows[:, -1:] + high[:: fx + 1, None]], axis=1)
    sums = far(*sums, [Z_FAR])
    sums, rows = tied(sums, rows)
    below, above = halos("gx", rows[0], rows[1])
    du = cot[:, :, :fk]
    du = jnp.concatenate([du[:, :1] + low[1:-1, None], du[:, 1:-1], du[:, -1:] + high[1:-1, None]], axis=1)
    du = jnp.concatenate([du[:1] + below[None], du[1:-1], du[-1:] + above[None]], axis=0)
    cot = jnp.concatenate([du, cot[:, :, fk:]], axis=2)

    coarse_grads, fine_grads = pair_whole(*pair_whole(*sums, X_NEAR), Y_NEAR)
    other = partner(jnp.concatenate([coarse_grads, fine_grads], axis=0), CORE)
    cut = coarse_grads.shape[0]
    sums = (coarse_grads, other[:cut], fine_grads, other[cut:])

    grads = call(
        unpack_kernel,
        [(27, fk, fh), (1, fh), (2 * fk, fh), (1, 2 * fk), (27, k, h), (1, h), (2 * k, h), (1, 2 * k)],
        [(16 * k, 128), (10 * fk, 128)],
        1_000_000,
        at,
        *sums,
        scalars=True,
    )
    f_conv, f_in, f_proj, f_out, c_conv, c_in, c_proj, c_out = grads
    return (
        jnp.transpose(field, (2, 0, 1, 3)),
        jnp.transpose(cot, (2, 0, 1, 3)),
        jnp.transpose(f_conv, (0, 2, 1)),
        f_in[0],
        f_proj,
        f_out[0],
        jnp.transpose(c_conv, (0, 2, 1)),
        c_in[0],
        c_proj,
        c_out[0],
    )


def solution(mesh):
    split_field = P(None, "gx", "gy", None)
    return jax.shard_map(
        local,
        mesh=mesh,
        in_specs=(split_field, split_field) + (P(),) * 8,
        out_specs=(split_field, split_field) + (P(),) * 8,
        check_vma=False,
    )
```

time: 126 us -> 100 us (0.79)
  the two profiles are of different devices: /device:TPU:7 before, /device:TPU:21 now
where the time goes in v2:
time: 100 us
  starting transfers between devices  55.6 us (56%)
  Pallas kernels  22.5 us (22%)
  waiting for transfers between devices  17.1 us (17%)
  local copies, waits for them, and re-layouts  3.11 us (3%)
  between operations  1.34 us (1%)
    ppermute x6, starting transfers between devices, swapped(): two = lax.ppermute(two, axis, outer)  25.8 us
    pallas_call x12, Pallas kernels, call(): pl.pallas_call(kernel, in_specs=specs, out_shape=[jax.ShapeDtypeStruct(s,...  22.5 us
    ppermute x12, starting transfers between devices, partner(): return lax.ppermute(x, ('gx', 'gy'), pairs)  20 us
    ppermute x12, waiting for transfers between devices, partner(): return lax.ppermute(x, ('gx', 'gy'), pairs)  13.5 us
    ppermute x6, starting transfers between devices, swapped(): one = lax.ppermute(one, axis, inner)  9.94 us
    unnamed x24, local copies, waits for them, and re-layouts  3.01 us
    ppermute x6, waiting for transfers between devices, swapped(): two = lax.ppermute(two, axis, outer)  2.46 us
  transfers between devices with their start and end apart: 24, of which 10 were waited for; matrix products, arithmetic and copies ran while one was open for 2% of the time, Pallas kernels for 16%

profile of v2, /device:TPU:21, one launch (start us, length us, event | category | flops | bytes accessed | tf_op | source)
XLA Modules:
  0.0 100.1 jit_solution(18433904787496037464)
XLA Ops:
  0.7 1.0 %copy-done = f32[64,4,4,128]{3,2,1,0:T(4,128)S(1)} copy-done((f32[64,4,4,128]{3,2,1,0:T(4,128)S(1)}, f32[64,4,4,128]{3,2,1,0:T(4,128)}, u32[]{:S(2)}) %copy-start) | copy-done | bytes 524312
  1.8 0.6 shard_map.177
  2.4 0.8 collective-permute-start
  3.1 2.7 %collective-permute-start.1 = (f32[4,2,32,128]{3,2,1,0:T(8,128)S(1)}, f32[4,2,32,128]{3,2,1,0:T(8,128)S(1)}, u32[]{:S(2)}, u32[]{:S(2)}) collective-permute-start(f32[4,2,32,128]{3,2,1,0:T(8,128)S(1)} %get-tuple-element.75), channel_id=1, source_target_pairs={{1,2},{2,1},{3,4},{4,3},{5,6},{6,5},{7,8},{8,7},{9,10},{10,9},{11,... | collective-permute-start | bytes 393224 | tf_op jit(solution)/shard_map/ppermute | solution.py:490
  5.9 0.7 shard_map.181
  6.6 0.1 collective-permute-start.4
  6.7 9.1 %collective-permute-start.5 = (f32[4,1,64,128]{3,2,1,0:T(8,128)S(1)}, f32[4,1,64,128]{3,2,1,0:T(8,128)S(1)}, u32[]{:S(2)}, u32[]{:S(2)}) collective-permute-start(f32[4,1,64,128]{3,2,1,0:T(8,128)S(1)} %get-tuple-element.86), channel_id=1, source_target_pairs={{1,2},{2,1},{3,4},{4,3},{5,6},{6,5},{7,8},{8,7},{9,10},{10,9},{11,... | collective-permute-start | bytes 393224 | tf_op jit(solution)/shard_map/ppermute | solution.py:490
  15.9 0.6 shard_map.179
  16.5 1.1 %collective-permute-start.2 = (f32[2,8,32,128]{3,2,1,0:T(8,128)S(1)}, f32[2,8,32,128]{3,2,1,0:T(8,128)S(1)}, u32[]{:S(2)}, u32[]{:S(2)}) collective-permute-start(f32[2,8,32,128]{3,2,1,0:T(8,128)S(1)} %get-tuple-element.77), channel_id=1, source_target_pairs={{0,16},{16,0},{32,48},{48,32},{64,80},{80,64},{96,112},{112,96},{1... | collective-permute-start | bytes 786440 | tf_op jit(solution)/shard_map/ppermute | solution.py:491
  17.6 1.9 %collective-permute-start.3 = (f32[2,8,32,128]{3,2,1,0:T(8,128)S(1)}, f32[2,8,32,128]{3,2,1,0:T(8,128)S(1)}, u32[]{:S(2)}, u32[]{:S(2)}) collective-permute-start(f32[2,8,32,128]{3,2,1,0:T(8,128)S(1)} %get-tuple-element.78), channel_id=1, source_target_pairs={{16,32},{32,16},{48,64},{64,48},{80,96},{96,80},{112,128},{128,112... | collective-permute-start | bytes 786440 | tf_op jit(solution)/shard_map/ppermute | solution.py:490
  19.6 0.6 shard_map.182
  20.1 1.8 %collective-permute-start.6 = (f32[1,6,64,128]{3,2,1,0:T(8,128)S(1)}, f32[1,6,64,128]{3,2,1,0:T(8,128)S(1)}, u32[]{:S(2)}, u32[]{:S(2)}) collective-permute-start(f32[1,6,64,128]{3,2,1,0:T(8,128)S(1)} %get-tuple-element.87), channel_id=1, source_target_pairs={{0,16},{16,0},{32,48},{48,32},{64,80},{80,64},{96,112},{112,96},{1... | collective-permute-start | bytes 589832 | tf_op jit(solution)/shard_map/ppermute | solution.py:491
  21.9 1.9 %collective-permute-start.7 = (f32[1,6,64,128]{3,2,1,0:T(8,128)S(1)}, f32[1,6,64,128]{3,2,1,0:T(8,128)S(1)}, u32[]{:S(2)}, u32[]{:S(2)}) collective-permute-start(f32[1,6,64,128]{3,2,1,0:T(8,128)S(1)} %get-tuple-element.88), channel_id=1, source_target_pairs={{16,32},{32,16},{48,64},{64,48},{80,96},{96,80},{112,128},{128,112... | collective-permute-start | bytes 589832 | tf_op jit(solution)/shard_map/ppermute | solution.py:490
  23.9 1.9 %shard_map.178 = (f32[4,96,1024]{2,1,0:T(8,128)S(1)}, f32[2,64,768]{2,1,0:T(8,128)S(1)}, f32[192,864]{1,0:T(8,128)S(1)}, f32[64,1]{1,0:T(8,128)S(1)}) custom-call(s32[2]{0:T(128)S(1)} %pad_add_fusion.at_ref.refs_0_, f32[4,4,32,128]{3,2,1,0:T(8,128)S(1)} %get-tuple-element.73.u_ref.f_ref, f32[4,2,32,128]{3,2,1,0:T(8,128)S(1)} %collective-permute-done.ya_ref, ...), custom_call_target="tpu_custom_call" | custom-call | flops 2500000000 | bytes 1000000 | tf_op jit(solution)/shard_map/pallas_call | solution.py:474
  25.8 1.0 %collective-permute-done.3.xb_ref = f32[2,8,32,128]{3,2,1,0:T(8,128)S(1)} collective-permute-done((f32[2,8,32,128]{3,2,1,0:T(8,128)S(1)}, f32[2,8,32,128]{3,2,1,0:T(8,128)S(1)}, u32[]{:S(2)}, u32[]{:S(2)}) %collective-permute-start.3) | collective-permute-done | bytes 262176 | tf_op jit(solution)/shard_map/ppermute | solution.py:490
  26.8 2.5 %shard_map.180 = (f32[4,96,1024]{2,1,0:T(8,128)S(1)}, f32[4,64,768]{2,1,0:T(8,128)S(1)}) custom-call(s32[2]{0:T(128)S(1)} %pad_add_fusion.at_ref.refs_0_, f32[4,96,1024]{2,1,0:T(8,128)S(1)} %get-tuple-element.76.inner_ref.refs_1_, f32[2,8,32,128]{3,2,1,0:T(8,128)S(1)} %collective-permute-done.2.xa_ref, f32[2,8,32,128]{3,2,1,0:T(8,128)S(1)} %collective-permute-done.3.xb_ref, ...), custom_call_target="tpu_custom_call" | custom-call | flops 4000000000 | bytes 1000000 | tf_op jit(solution)/shard_map/pallas_call | solution.py:474
  29.4 4.2 %shard_map.183 = (f32[6,6,64,128]{3,2,1,0:T(8,128)S(1)}, f32[6,64,768]{2,1,0:T(8,128)S(1)}, f32[4,32,512]{2,1,0:T(8,128)S(1)}, f32[512,128]{1,0:T(8,128)S(1)}) custom-call(s32[2]{0:T(128)S(1)} %pad_add_fusion.at_ref.refs_0_, f32[4,96,1024]{2,1,0:T(8,128)S(1)} %get-tuple-element.76.inner_ref.refs_1_, f32[4,96,1024]{2,1,0:T(8,128)S(1)} %get-tuple-element.81.refs_2_, ...), custom_call_target="tpu_custom_call" | custom-call | flops 6000000000 | bytes 1000000 | tf_op jit(solution)/shard_map/pallas_call | solution.py:474
  33.6 0.1 collective-permute-start.8
  33.8 1.9 %shard_map.184.refs_1_ = f32[4,4,64,128]{3,2,1,0:T(8,128)S(1)} custom-call(f32[6,64,768]{2,1,0:T(8,128)S(1)} %get-tuple-element.91.gpre_ref, f32[4,32,512]{2,1,0:T(8,128)S(1)} %get-tuple-element.92.low_ref, f32[4,4,32,128]{3,2,1,0:T(8,128)S(1)} %get-tuple-element.93.cot_ref, f32[27,32,64]{2,1,0:T(8,128)S(1)} %bitcast.53), custom_call_target="tpu_custom_call" | custom-call | flops 2500000000 | bytes 1000000 | tf_op jit(solution)/shard_map/pallas_call | solution.py:474
  35.8 2.3 %collective-permute-start.9 = (f32[128,128]{1,0:T(8,128)S(1)}, f32[128,128]{1,0:T(8,128)S(1)}, u32[]{:S(2)}, u32[]{:S(2)}) collective-permute-start(f32[128,128]{1,0:T(8,128)S(1)} %slice_select_fusion.3), channel_id=1, source_target_pairs={{0,16},{1,17},{2,18},{3,19},{4,20},{5,21},{6,22},{7,23},{8,24},{9,... | collective-permute-start | bytes 196616 | tf_op jit(solution)/shard_map/ppermute | solution.py:507
  38.1 3.2 %shard_map.185 = (f32[4,8,16,128]{3,2,1,0:T(8,128)S(1)}, f32[4,8,16,128]{3,2,1,0:T(8,128)S(1)}, f32[4,8,32,128]{3,2,1,0:T(8,128)S(1)}, f32[104,128]{1,0:T(8,128)...) custom-call(f32[6,6,64,128]{3,2,1,0:T(8,128)S(1)} %get-tuple-element.94.refs_0_, ...), custom_call_target="tpu_custom_call" | custom-call | flops 4499999744 | bytes 1000000 | tf_op jit(solution)/shard_map/pallas_call | solution.py:474
  41.4 6.0 %collective-permute-start.10 = (f32[64,128]{1,0:T(8,128)S(1)}, f32[64,128]{1,0:T(8,128)S(1)}, u32[]{:S(2)}, u32[]{:S(2)}) collective-permute-start(f32[64,128]{1,0:T(8,128)S(1)} %slice_select_fusion.6), channel_id=1, source_target_pairs={{0,2},{1,3},{2,0},{3,1},{4,6},{5,7},{6,4},{7,5},{8,10},{9,11},{10,... | collective-permute-start | bytes 98312 | tf_op jit(solution)/shard_map/ppermute | solution.py:507
  47.4 3.3 %shard_map.186 = (f32[8,8,16,128]{3,2,1,0:T(8,128)S(1)}, f32[8,8,16,128]{3,2,1,0:T(8,128)S(1)}, f32[8,8,32,128]{3,2,1,0:T(8,128)S(1)}, f32[80,128]{1,0:T(8,128)S(1)}) custom-call(f32[6,6,64,128]{3,2,1,0:T(8,128)S(1)} %get-tuple-element.94.refs_0_, f32[4,4,64,128]{3,2,1,0:T(8,128)S(1)} %shard_map.184.refs_1_, f32[27,8,32]{2,1,0:T(8,128)S(1)} %bitcast.55, ...), custom_call_target="tpu_custom_call" | custom-call | flops 4499999744 | bytes 1000000 | tf_op jit(solution)/shard_map/pallas_call | solution.py:474
  50.7 1.1 %collective-permute-start.11 = (f32[40,128]{1,0:T(8,128)S(1)}, f32[40,128]{1,0:T(8,128)S(1)}, u32[]{:S(2)}, u32[]{:S(2)}) collective-permute-start(f32[40,128]{1,0:T(8,128)S(1)} %slice_select_fusion.7), channel_id=1, source_target_pairs={{0,1},{1,0},{2,3},{3,2},{4,5},{5,4},{6,7},{7,6},{8,9},{9,8},{10,11... | collective-permute-start | bytes 61448 | tf_op jit(solution)/shard_map/ppermute | solution.py:507
  51.9 0.8 collective-permute-done.11
  52.8 3.0 %collective-permute-done.12 = f32[104,128]{1,0:T(8,128)S(1)} collective-permute-done((f32[104,128]{1,0:T(8,128)S(1)}, f32[104,128]{1,0:T(8,128)S(1)}, u32[]{:S(2)}, u32[]{:S(2)}) %collective-permute-start.12) | collective-permute-done | bytes 53280 | tf_op jit(solution)/shard_map/ppermute | solution.py:507
  55.8 0.2 collective-permute-start.13
  56.0 2.9 %collective-permute-done.13 = f32[104,128]{1,0:T(8,128)S(1)} collective-permute-done((f32[104,128]{1,0:T(8,128)S(1)}, f32[104,128]{1,0:T(8,128)S(1)}, u32[]{:S(2)}, u32[]{:S(2)}) %collective-permute-start.13) | collective-permute-done | bytes 53280 | tf_op jit(solution)/shard_map/ppermute | solution.py:507
  58.9 2.5 %collective-permute-start.14 = (f32[104,128]{1,0:T(8,128)S(1)}, f32[104,128]{1,0:T(8,128)S(1)}, u32[]{:S(2)}, u32[]{:S(2)}) collective-permute-start(f32[104,128]{1,0:T(8,128)S(1)} %constant_dynamic-update-slice_fusion), channel_id=1, source_target_pairs={{0,128},{1,129},{2,130},{3,131},{4,132},{5,133},{6,134},{7,135},{8... | collective-permute-start | bytes 159752 | tf_op jit(solution)/shard_map/ppermute | solution.py:507
  61.4 1.0 copy.26
  62.4 0.6 collective-permute-done.14
  63.0 1.2 %collective-permute-start.15 = (f32[104,128]{1,0:T(8,128)S(1)}, f32[104,128]{1,0:T(8,128)S(1)}, u32[]{:S(2)}, u32[]{:S(2)}) collective-permute-start(f32[104,128]{1,0:T(8,128)S(1)} %add.90), channel_id=1, source_target_pairs={{0,64},{1,65},{2,66},{3,67},{4,68},{5,69},{6,70},{7,71},{8,72},{9,... | collective-permute-start | bytes 159752 | tf_op jit(solution)/shard_map/ppermute | solution.py:507
  64.2 1.4 %shard_map.187 = (f32[8,8,16,128]{3,2,1,0:T(8,128)S(1)}, f32[2,10,8,128]{3,2,1,0:T(8,128)S(1)}, f32[2,8,8,128]{3,2,1,0:T(8,128)S(1)}) custom-call(f32[8,8,32,128]{3,2,1,0:T(8,128)S(1)} %get-tuple-element.115.gpre_ref, f32[8,8,16,128]{3,2,1,0:T(8,128)S(1)} %get-tuple-element.116.cot_ref, f32[27,8,32]{2,1,0:T(8,128)S(1)} %bitcast.56), custom_call_target="tpu_custom_call" | custom-call | flops 4000000000 | bytes 1000000 | tf_op jit(solution)/shard_map/pallas_call | solution.py:474
  65.7 0.9 collective-permute-done.15
  66.6 7.7 %collective-permute-start.16 = (f32[10,8,128]{2,1,0:T(8,128)S(1)}, f32[10,8,128]{2,1,0:T(8,128)S(1)}, u32[]{:S(2)}, u32[]{:S(2)}) collective-permute-start(f32[10,8,128]{2,1,0:T(8,128)S(1)} %get-tuple-element.156), channel_id=1, source_target_pairs={{1,2},{2,1},{3,4},{4,3},{5,6},{6,5},{7,8},{8,7},{9,10},{10,9},{11,... | collective-permute-start | bytes 122888 | tf_op jit(solution)/shard_map/ppermute | solution.py:490
  74.4 0.1 collective-permute-start.17
  74.5 0.1 collective-permute-start.18
  74.6 1.4 %collective-permute-done.16 = f32[10,8,128]{2,1,0:T(8,128)S(1)} collective-permute-done((f32[10,8,128]{2,1,0:T(8,128)S(1)}, f32[10,8,128]{2,1,0:T(8,128)S(1)}, u32[]{:S(2)}, u32[]{:S(2)}) %collective-permute-start.16) | collective-permute-done | bytes 40992 | tf_op jit(solution)/shard_map/ppermute | solution.py:490
  76.2 2.6 %collective-permute-done.18 = f32[104,128]{1,0:T(8,128)S(1)} collective-permute-done((f32[104,128]{1,0:T(8,128)S(1)}, f32[104,128]{1,0:T(8,128)S(1)}, u32[]{:S(2)}, u32[]{:S(2)}) %collective-permute-start.18) | collective-permute-done | bytes 53280 | tf_op jit(solution)/shard_map/ppermute | solution.py:507
  78.8 3.1 %collective-permute-start.21 = (f32[104,128]{1,0:T(8,128)S(1)}, f32[104,128]{1,0:T(8,128)S(1)}, u32[]{:S(2)}, u32[]{:S(2)}) collective-permute-start(f32[104,128]{1,0:T(8,128)S(1)} %pad_maximum_fusion.7), channel_id=1, source_target_pairs={{0,2},{1,3},{2,0},{3,1},{4,6},{5,7},{6,4},{7,5},{8,10},{9,11},{10,... | collective-permute-start | bytes 159752 | tf_op jit(solution)/shard_map/ppermute | solution.py:507
  81.9 2.4 %collective-permute-start.19 = (f32[8,8,128]{2,1,0:T(8,128)S(1)}, f32[8,8,128]{2,1,0:T(8,128)S(1)}, u32[]{:S(2)}, u32[]{:S(2)}) collective-permute-start(f32[8,8,128]{2,1,0:T(8,128)S(1)} %get-tuple-element.158), channel_id=1, source_target_pairs={{16,32},{32,16},{48,64},{64,48},{80,96},{96,80},{112,128},{128,112... | collective-permute-start | bytes 98312 | tf_op jit(solution)/shard_map/ppermute | solution.py:490
  84.3 6.1 %collective-permute-start.20 = (f32[8,8,128]{2,1,0:T(8,128)S(1)}, f32[8,8,128]{2,1,0:T(8,128)S(1)}, u32[]{:S(2)}, u32[]{:S(2)}) collective-permute-start(f32[8,8,128]{2,1,0:T(8,128)S(1)} %get-tuple-element.159), channel_id=1, source_target_pairs={{0,16},{16,0},{32,48},{48,32},{64,80},{80,64},{96,112},{112,96},{1... | collective-permute-start | bytes 98312 | tf_op jit(solution)/shard_map/ppermute | solution.py:491
  90.5 0.1 collective-permute-start.22
  90.6 1.1 %collective-permute-done.20 = f32[8,8,128]{2,1,0:T(8,128)S(1)} collective-permute-done((f32[8,8,128]{2,1,0:T(8,128)S(1)}, f32[8,8,128]{2,1,0:T(8,128)S(1)}, u32[]{:S(2)}, u32[]{:S(2)}) %collective-permute-start.20) | collective-permute-done | bytes 32800 | tf_op jit(solution)/shard_map/ppermute | solution.py:491
  91.7 2.7 %collective-permute-done.22 = f32[168,128]{1,0:T(8,128)S(1)} collective-permute-done((f32[168,128]{1,0:T(8,128)S(1)}, f32[168,128]{1,0:T(8,128)S(1)}, u32[]{:S(2)}, u32[]{:S(2)}) %collective-permute-start.22) | collective-permute-done | bytes 86048 | tf_op jit(solution)/shard_map/ppermute | solution.py:507
  94.5 3.0 %collective-permute-start.23 = (f32[296,128]{1,0:T(8,128)S(1)}, f32[296,128]{1,0:T(8,128)S(1)}, u32[]{:S(2)}, u32[]{:S(2)}) collective-permute-start(f32[296,128]{1,0:T(8,128)S(1)} %pad_maximum_fusion.1), channel_id=1, source_target_pairs={{0,1},{1,0},{2,3},{3,2},{4,5},{5,4},{6,7},{7,6},{8,9},{9,8},{10,11... | collective-permute-start | bytes 454664 | tf_op jit(solution)/shard_map/ppermute | solution.py:507
  97.6 1.0 copy.27
  98.6 1.5 %shard_map.188 = (f32[27,8,32]{2,1,0:T(8,128)}, f32[1,32]{1,0:T(1,128)}, f32[16,32]{1,0:T(8,128)}, f32[1,16]{1,0:T(1,128)}, f32[27,32,64]{2,1,0:T(8,128)}, /*ind...) custom-call(s32[2]{0:T(128)S(1)} %pad_add_fusion.at_ref.refs_0_, f32[256,128]{1,0:T(8,128)S(1)} %pad_maximum_fusion.2.coarse_ref, ...), custom_call_target="tpu_custom_call" | custom-call | flops 1000000 | bytes 1000000 | tf_op jit(solution)/shard_map/pallas_call | solution.py:474
  (83 shorter events, 0.7 us)
Async XLA Ops:
  0.7 1.0 %copy-start = (f32[64,4,4,128]{3,2,1,0:T(4,128)S(1)}, f32[64,4,4,128]{3,2,1,0:T(4,128)}, u32[]{:S(2)}) copy-start(f32[64,4,4,128]{3,2,1,0:T(4,128)} %w_ref.3) | copy-start | bytes 1572868
  1.8 4.1 %copy-start.1 = (f32[64,4,4,128]{3,2,1,0:T(4,128)S(1)}, f32[64,4,4,128]{3,2,1,0:T(4,128)}, u32[]{:S(2)}) copy-start(f32[64,4,4,128]{3,2,1,0:T(4,128)} %dw_ref.1) | copy-start | bytes 1572868
  2.4 13.5 %collective-permute-start = (f32[4,2,32,128]{3,2,1,0:T(8,128)S(1)}, f32[4,2,32,128]{3,2,1,0:T(8,128)S(1)}, u32[]{:S(2)}, u32[]{:S(2)}) collective-permute-start(f32[4,2,32,128]{3,2,1,0:T(8,128)S(1)} %get-tuple-element.74), channel_id=1, source_target_pairs={{0,1},{1,0},{2,3},{3,2},{4,5},{5,4},{6,7},{7,6},{8,9},{9,8},{10,11... | collective-permute-start | bytes 393224 | tf_op jit(solution)/shard_map/ppermute | solution.py:491
  3.1 12.7 %collective-permute-start.1 = (f32[4,2,32,128]{3,2,1,0:T(8,128)S(1)}, f32[4,2,32,128]{3,2,1,0:T(8,128)S(1)}, u32[]{:S(2)}, u32[]{:S(2)}) collective-permute-start(f32[4,2,32,128]{3,2,1,0:T(8,128)S(1)} %get-tuple-element.75), channel_id=1, source_target_pairs={{1,2},{2,1},{3,4},{4,3},{5,6},{6,5},{7,8},{8,7},{9,10},{10,9},{11,... | collective-permute-start | bytes 393224 | tf_op jit(solution)/shard_map/ppermute | solution.py:490
  6.6 12.9 %collective-permute-start.4 = (f32[4,1,64,128]{3,2,1,0:T(8,128)S(1)}, f32[4,1,64,128]{3,2,1,0:T(8,128)S(1)}, u32[]{:S(2)}, u32[]{:S(2)}) collective-permute-start(f32[4,1,64,128]{3,2,1,0:T(8,128)S(1)} %get-tuple-element.85), channel_id=1, source_target_pairs={{0,1},{1,0},{2,3},{3,2},{4,5},{5,4},{6,7},{7,6},{8,9},{9,8},{10,11... | collective-permute-start | bytes 393224 | tf_op jit(solution)/shard_map/ppermute | solution.py:491
  6.7 12.9 %collective-permute-start.5 = (f32[4,1,64,128]{3,2,1,0:T(8,128)S(1)}, f32[4,1,64,128]{3,2,1,0:T(8,128)S(1)}, u32[]{:S(2)}, u32[]{:S(2)}) collective-permute-start(f32[4,1,64,128]{3,2,1,0:T(8,128)S(1)} %get-tuple-element.86), channel_id=1, source_target_pairs={{1,2},{2,1},{3,4},{4,3},{5,6},{6,5},{7,8},{8,7},{9,10},{10,9},{11,... | collective-permute-start | bytes 393224 | tf_op jit(solution)/shard_map/ppermute | solution.py:490
  15.9 8.0 %copy-start.2 = (f32[27,64,32]{1,2,0:T(8,128)S(1)}, f32[27,64,32]{1,2,0:T(8,128)}, u32[]{:S(2)}) copy-start(f32[27,64,32]{1,2,0:T(8,128)} %param.16) | copy-start | bytes 663556
  15.9 8.0 %copy-start.6 = (f32[64]{0:T(128)S(1)}, f32[64]{0:T(128)}, u32[]{:S(2)}) copy-start(f32[64]{0:T(128)} %param.17) | copy-start | bytes 772
  16.5 9.3 %collective-permute-start.2 = (f32[2,8,32,128]{3,2,1,0:T(8,128)S(1)}, f32[2,8,32,128]{3,2,1,0:T(8,128)S(1)}, u32[]{:S(2)}, u32[]{:S(2)}) collective-permute-start(f32[2,8,32,128]{3,2,1,0:T(8,128)S(1)} %get-tuple-element.77), channel_id=1, source_target_pairs={{0,16},{16,0},{32,48},{48,32},{64,80},{80,64},{96,112},{112,96},{1... | collective-permute-start | bytes 786440 | tf_op jit(solution)/shard_map/ppermute | solution.py:491
  17.6 9.2 %collective-permute-start.3 = (f32[2,8,32,128]{3,2,1,0:T(8,128)S(1)}, f32[2,8,32,128]{3,2,1,0:T(8,128)S(1)}, u32[]{:S(2)}, u32[]{:S(2)}) collective-permute-start(f32[2,8,32,128]{3,2,1,0:T(8,128)S(1)} %get-tuple-element.78), channel_id=1, source_target_pairs={{16,32},{32,16},{48,64},{64,48},{80,96},{96,80},{112,128},{128,112... | collective-permute-start | bytes 786440 | tf_op jit(solution)/shard_map/ppermute | solution.py:490
  20.1 9.2 %collective-permute-start.6 = (f32[1,6,64,128]{3,2,1,0:T(8,128)S(1)}, f32[1,6,64,128]{3,2,1,0:T(8,128)S(1)}, u32[]{:S(2)}, u32[]{:S(2)}) collective-permute-start(f32[1,6,64,128]{3,2,1,0:T(8,128)S(1)} %get-tuple-element.87), channel_id=1, source_target_pairs={{0,16},{16,0},{32,48},{48,32},{64,80},{80,64},{96,112},{112,96},{1... | collective-permute-start | bytes 589832 | tf_op jit(solution)/shard_map/ppermute | solution.py:491
  21.9 7.4 %collective-permute-start.7 = (f32[1,6,64,128]{3,2,1,0:T(8,128)S(1)}, f32[1,6,64,128]{3,2,1,0:T(8,128)S(1)}, u32[]{:S(2)}, u32[]{:S(2)}) collective-permute-start(f32[1,6,64,128]{3,2,1,0:T(8,128)S(1)} %get-tuple-element.88), channel_id=1, source_target_pairs={{16,32},{32,16},{48,64},{64,48},{80,96},{96,80},{112,128},{128,112... | collective-permute-start | bytes 589832 | tf_op jit(solution)/shard_map/ppermute | solution.py:490
  26.8 2.5 %copy-start.4 = (f32[64,64]{1,0:T(8,128)S(1)}, f32[64,64]{1,0:T(8,128)}, u32[]{:S(2)}) copy-start(f32[64,64]{1,0:T(8,128)} %refs_10_.1) | copy-start | bytes 49156
  26.8 2.6 %copy-start.7 = (f32[64]{0:T(128)S(1)}, f32[64]{0:T(128)}, u32[]{:S(2)}) copy-start(f32[64]{0:T(128)} %param.19) | copy-start | bytes 772
  33.6 2.1 %collective-permute-start.8 = (f32[256,128]{1,0:T(8,128)S(1)}, f32[256,128]{1,0:T(8,128)S(1)}, u32[]{:S(2)}, u32[]{:S(2)}) collective-permute-start(f32[256,128]{1,0:T(8,128)S(1)} %slice_select_fusion), channel_id=1, source_target_pairs={{0,1},{1,0},{2,3},{3,2},{4,5},{5,4},{6,7},{7,6},{8,9},{9,8},{10,11... | collective-permute-start | bytes 393224 | tf_op jit(solution)/shard_map/ppermute | solution.py:507
  33.7 4.4 %copy-start.3 = (f32[27,32,8]{1,2,0:T(8,128)S(1)}, f32[27,32,8]{1,2,0:T(8,128)}, u32[]{:S(2)}) copy-start(f32[27,32,8]{1,2,0:T(8,128)} %param.12) | copy-start | bytes 82948
  33.7 4.4 %copy-start.5 = (f32[16,32]{1,0:T(8,128)S(1)}, f32[16,32]{1,0:T(8,128)}, u32[]{:S(2)}) copy-start(f32[16,32]{1,0:T(8,128)} %refs_4_.3) | copy-start | bytes 6148
  33.8 4.4 %copy-start.8 = (f32[32]{0:T(128)S(1)}, f32[32]{0:T(128)}, u32[]{:S(2)}) copy-start(f32[32]{0:T(128)} %param.13) | copy-start | bytes 388
  33.8 4.4 %copy-start.9 = (f32[16]{0:T(128)S(1)}, f32[16]{0:T(128)}, u32[]{:S(2)}) copy-start(f32[16]{0:T(128)} %param.15) | copy-start | bytes 196
  35.8 5.6 %collective-permute-start.9 = (f32[128,128]{1,0:T(8,128)S(1)}, f32[128,128]{1,0:T(8,128)S(1)}, u32[]{:S(2)}, u32[]{:S(2)}) collective-permute-start(f32[128,128]{1,0:T(8,128)S(1)} %slice_select_fusion.3), channel_id=1, source_target_pairs={{0,16},{1,17},{2,18},{3,19},{4,20},{5,21},{6,22},{7,23},{8,24},{9,... | collective-permute-start | bytes 196616 | tf_op jit(solution)/shard_map/ppermute | solution.py:507
  41.4 9.3 %collective-permute-start.10 = (f32[64,128]{1,0:T(8,128)S(1)}, f32[64,128]{1,0:T(8,128)S(1)}, u32[]{:S(2)}, u32[]{:S(2)}) collective-permute-start(f32[64,128]{1,0:T(8,128)S(1)} %slice_select_fusion.6), channel_id=1, source_target_pairs={{0,2},{1,3},{2,0},{3,1},{4,6},{5,7},{6,4},{7,5},{8,10},{9,11},{10,... | collective-permute-start | bytes 98312 | tf_op jit(solution)/shard_map/ppermute | solution.py:507
  50.7 2.0 %collective-permute-start.11 = (f32[40,128]{1,0:T(8,128)S(1)}, f32[40,128]{1,0:T(8,128)S(1)}, u32[]{:S(2)}, u32[]{:S(2)}) collective-permute-start(f32[40,128]{1,0:T(8,128)S(1)} %slice_select_fusion.7), channel_id=1, source_target_pairs={{0,1},{1,0},{2,3},{3,2},{4,5},{5,4},{6,7},{7,6},{8,9},{9,8},{10,11... | collective-permute-start | bytes 61448 | tf_op jit(solution)/shard_map/ppermute | solution.py:507
  52.7 3.1 %collective-permute-start.12 = (f32[104,128]{1,0:T(8,128)S(1)}, f32[104,128]{1,0:T(8,128)S(1)}, u32[]{:S(2)}, u32[]{:S(2)}) collective-permute-start(f32[104,128]{1,0:T(8,128)S(1)} %pad_maximum_fusion.6), channel_id=1, source_target_pairs={{0,6},{1,7},{2,4},{3,5},{4,2},{5,3},{6,0},{7,1},{8,14},{9,15},{10,... | collective-permute-start | bytes 159752 | tf_op jit(solution)/shard_map/ppermute | solution.py:507
  55.8 3.1 %collective-permute-start.13 = (f32[104,128]{1,0:T(8,128)S(1)}, f32[104,128]{1,0:T(8,128)S(1)}, u32[]{:S(2)}, u32[]{:S(2)}) collective-permute-start(f32[104,128]{1,0:T(8,128)S(1)} %fusion.5), channel_id=1, source_target_pairs={{0,48},{1,49},{2,50},{3,51},{4,52},{5,53},{6,54},{7,55},{8,56},{9,... | collective-permute-start | bytes 159752 | tf_op jit(solution)/shard_map/ppermute | solution.py:507
  58.9 4.0 %collective-permute-start.14 = (f32[104,128]{1,0:T(8,128)S(1)}, f32[104,128]{1,0:T(8,128)S(1)}, u32[]{:S(2)}, u32[]{:S(2)}) collective-permute-start(f32[104,128]{1,0:T(8,128)S(1)} %constant_dynamic-update-slice_fusion), channel_id=1, source_target_pairs={{0,128},{1,129},{2,130},{3,131},{4,132},{5,133},{6,134},{7,135},{8... | collective-permute-start | bytes 159752 | tf_op jit(solution)/shard_map/ppermute | solution.py:507
  63.0 3.6 %collective-permute-start.15 = (f32[104,128]{1,0:T(8,128)S(1)}, f32[104,128]{1,0:T(8,128)S(1)}, u32[]{:S(2)}, u32[]{:S(2)}) collective-permute-start(f32[104,128]{1,0:T(8,128)S(1)} %add.90), channel_id=1, source_target_pairs={{0,64},{1,65},{2,66},{3,67},{4,68},{5,69},{6,70},{7,71},{8,72},{9,... | collective-permute-start | bytes 159752 | tf_op jit(solution)/shard_map/ppermute | solution.py:507
  66.6 9.4 %collective-permute-start.16 = (f32[10,8,128]{2,1,0:T(8,128)S(1)}, f32[10,8,128]{2,1,0:T(8,128)S(1)}, u32[]{:S(2)}, u32[]{:S(2)}) collective-permute-start(f32[10,8,128]{2,1,0:T(8,128)S(1)} %get-tuple-element.156), channel_id=1, source_target_pairs={{1,2},{2,1},{3,4},{4,3},{5,6},{6,5},{7,8},{8,7},{9,10},{10,9},{11,... | collective-permute-start | bytes 122888 | tf_op jit(solution)/shard_map/ppermute | solution.py:490
  74.4 1.7 %collective-permute-start.17 = (f32[10,8,128]{2,1,0:T(8,128)S(1)}, f32[10,8,128]{2,1,0:T(8,128)S(1)}, u32[]{:S(2)}, u32[]{:S(2)}) collective-permute-start(f32[10,8,128]{2,1,0:T(8,128)S(1)} %get-tuple-element.157), channel_id=1, source_target_pairs={{0,1},{1,0},{2,3},{3,2},{4,5},{5,4},{6,7},{7,6},{8,9},{9,8},{10,11... | collective-permute-start | bytes 122888 | tf_op jit(solution)/shard_map/ppermute | solution.py:491
  74.5 4.3 %collective-permute-start.18 = (f32[104,128]{1,0:T(8,128)S(1)}, f32[104,128]{1,0:T(8,128)S(1)}, u32[]{:S(2)}, u32[]{:S(2)}) collective-permute-start(f32[104,128]{1,0:T(8,128)S(1)} %constant_dynamic-update-slice_fusion.2), channel_id=1, source_target_pairs={{0,200},{1,201},{2,202},{3,203},{4,204},{5,205},{6,206},{7,207},{8... | collective-permute-start | bytes 159752 | tf_op jit(solution)/shard_map/ppermute | solution.py:507
  78.8 11.6 %collective-permute-start.21 = (f32[104,128]{1,0:T(8,128)S(1)}, f32[104,128]{1,0:T(8,128)S(1)}, u32[]{:S(2)}, u32[]{:S(2)}) collective-permute-start(f32[104,128]{1,0:T(8,128)S(1)} %pad_maximum_fusion.7), channel_id=1, source_target_pairs={{0,2},{1,3},{2,0},{3,1},{4,6},{5,7},{6,4},{7,5},{8,10},{9,11},{10,... | collective-permute-start | bytes 159752 | tf_op jit(solution)/shard_map/ppermute | solution.py:507
  81.9 8.6 %collective-permute-start.19 = (f32[8,8,128]{2,1,0:T(8,128)S(1)}, f32[8,8,128]{2,1,0:T(8,128)S(1)}, u32[]{:S(2)}, u32[]{:S(2)}) collective-permute-start(f32[8,8,128]{2,1,0:T(8,128)S(1)} %get-tuple-element.158), channel_id=1, source_target_pairs={{16,32},{32,16},{48,64},{64,48},{80,96},{96,80},{112,128},{128,112... | collective-permute-start | bytes 98312 | tf_op jit(solution)/shard_map/ppermute | solution.py:490
  84.3 7.4 %collective-permute-start.20 = (f32[8,8,128]{2,1,0:T(8,128)S(1)}, f32[8,8,128]{2,1,0:T(8,128)S(1)}, u32[]{:S(2)}, u32[]{:S(2)}) collective-permute-start(f32[8,8,128]{2,1,0:T(8,128)S(1)} %get-tuple-element.159), channel_id=1, source_target_pairs={{0,16},{16,0},{32,48},{48,32},{64,80},{80,64},{96,112},{112,96},{1... | collective-permute-start | bytes 98312 | tf_op jit(solution)/shard_map/ppermute | solution.py:491
  90.5 4.0 %collective-permute-start.22 = (f32[168,128]{1,0:T(8,128)S(1)}, f32[168,128]{1,0:T(8,128)S(1)}, u32[]{:S(2)}, u32[]{:S(2)}) collective-permute-start(f32[168,128]{1,0:T(8,128)S(1)} %pad_maximum_fusion.3), channel_id=1, source_target_pairs={{0,16},{1,17},{2,18},{3,19},{4,20},{5,21},{6,22},{7,23},{8,24},{9,... | collective-permute-start | bytes 258056 | tf_op jit(solution)/shard_map/ppermute | solution.py:507
  94.5 4.1 %collective-permute-start.23 = (f32[296,128]{1,0:T(8,128)S(1)}, f32[296,128]{1,0:T(8,128)S(1)}, u32[]{:S(2)}, u32[]{:S(2)}) collective-permute-start(f32[296,128]{1,0:T(8,128)S(1)} %pad_maximum_fusion.1), channel_id=1, source_target_pairs={{0,1},{1,0},{2,3},{3,2},{4,5},{5,4},{6,7},{7,6},{8,9},{9,8},{10,11... | collective-permute-start | bytes 454664 | tf_op jit(solution)/shard_map/ppermute | solution.py:507

commit v3 on v2

--- a/solution.py
+++ b/solution.py
@@ -101,8 +101,11 @@
     first = jnp.concatenate([p_top, ones, g_top], axis=0).astype(bf16)
     second = jnp.concatenate([p_rest, g_rest], axis=0).astype(bf16)
     wide = right.shape[0] // 2
-    a = dot_cells(first, right)
-    b = dot_cells(second, right[:wide])
+    if wide < 256:
+        both = dot_cells(jnp.concatenate([first, second], axis=0), right)
+        a, b = both[: first.shape[0]], both[first.shape[0] :, :wide]
+    else:
+        a, b = dot_cells(first, right), dot_cells(second, right[:wide])
     return a[:, :wide] + a[:, wide:], b
 
 
@@ -431,6 +434,30 @@
     lax.fori_loop(0, 2, outer, 0, unroll=True)
 
 
+def corners_kernel(rows_ref, low_ref, high_ref, out_ref):
+    count = out_ref.shape[1]
+    for i, x in ((0, 0), (1, low_ref.shape[0] - 1)):
+        for y in range(count):
+            more = [ref[x] for ref, at in ((low_ref, 0), (high_ref, count - 1)) if at == y]
+            out_ref[i, y] = sum(more, rows_ref[i, y])
+
+
+def rims_kernel(cot_ref, low_ref, high_ref, below_ref, above_ref, out_ref):
+    nx, ny, k = cot_ref.shape[0], cot_ref.shape[1], low_ref.shape[1]
+    for x in range(nx):
+        cells = []
+        for y in range(ny):
+            du = cot_ref[x, y, :k]
+            for ref, at in ((low_ref, y == 0), (high_ref, y == ny - 1)):
+                if at:
+                    du = du + ref[x + 1]
+            for ref, at in ((below_ref, x == 0), (above_ref, x == nx - 1)):
+                if at:
+                    du = du + ref[y]
+            cells.append(jnp.concatenate([du, cot_ref[x, y, k:]], axis=0))
+        out_ref[:, x] = jnp.swapaxes(jnp.stack(cells, axis=0), 0, 1)
+
+
 def unpack_kernel(at_ref, coarse_ref, coarse_other, fine_ref, fine_other,
                   f_conv, f_in, f_proj, f_out, c_conv, c_in, c_proj, c_out, coarse, fine):
     first = at_ref[1] % 2 == 0
@@ -503,7 +530,9 @@
     pairs = []
     for i in range(sizes[0] * sizes[1]):
         gx, gy = divmod(i, sizes[1])
-        pairs.append((i, (gx ^ mask[0]) * sizes[1] + (gy ^ mask[1])))
+        to = (gx ^ mask[0], gy ^ mask[1])
+        if to[0] < sizes[0] and to[1] < sizes[1]:
+            pairs.append((i, to[0] * sizes[1] + to[1]))
     return lax.ppermute(x, ("gx", "gy"), pairs)
 
 
@@ -536,15 +565,29 @@
     return lax.optimization_barrier((x, *others))
 
 
+def partners(x, first, second):
+    both = (first[0] ^ second[0], first[1] ^ second[1])
+    return partner(x, first), partner(x, second), partner(x, both)
+
+
+def four_sum(coarse, fine, first, second):
+    both = jnp.concatenate([coarse, fine], axis=0)
+    a, b, c = partners(both, first, second)
+    both = (both + a) + (b + c)
+    return both[: coarse.shape[0]], both[coarse.shape[0] :]
+
+
 def pair_sum(coarse, fine, step):
     both = jnp.concatenate([coarse, fine], axis=0)
     both = both + partner(both, step)
     return both[: coarse.shape[0]], both[coarse.shape[0] :]
 
 
-def pair_whole(coarse, fine, step):
-    other = partner(jnp.concatenate([coarse, fine], axis=0), step)
-    return in_order(coarse, other[: coarse.shape[0]], step), fine + other[coarse.shape[0] :]
+def four_whole(coarse, fine, first, second):
+    cut = coarse.shape[0]
+    a, b, c = partners(jnp.concatenate([coarse, fine], axis=0), first, second)
+    mine, other = in_order(coarse, a[:cut], first), in_order(b[:cut], c[:cut], first)
+    return in_order(mine, other, second), (fine + a[cut:]) + (b[cut:] + c[cut:])
 
 
 def local(
@@ -660,13 +703,7 @@
     coarse_grads, fine_grads = tied(coarse_grads, fine_grads)
     fine_grads = half_sum(fine_grads, CORE)
 
-    def far(coarse, fine, steps):
-        for step in steps:
-            if step[0] < size_x and step[1] < size_y:
-                coarse, fine = pair_sum(coarse, fine, step)
-        return coarse, fine
-
-    sums = far(coarse_grads, fine_grads, [X_FAR, Y_FAR])
+    sums = four_sum(coarse_grads, fine_grads, X_FAR, Y_FAR)
     sums, gpre = tied(sums, gpre)
     cot, columns, rows = call(
         fine_back_kernel,
@@ -677,19 +714,14 @@
         cot,
         f_conv,
     )
-    sums = far(*sums, [Z_TWO, Z_ONE])
-    sums, columns = tied(sums, columns)
     low, high = halos("gy", columns[0], columns[1])
-    rows = jnp.concatenate([rows[:, :1] + low[:: fx + 1, None], rows[:, 1:-1], rows[:, -1:] + high[:: fx + 1, None]], axis=1)
-    sums = far(*sums, [Z_FAR])
-    sums, rows = tied(sums, rows)
+    sums = four_sum(*sums, Z_ONE, Z_TWO)
+    sums, low, high = tied(sums, low, high)
+    (rows,) = call(corners_kernel, [rows.shape], [], 6_000_000_000, rows, low, high)
     below, above = halos("gx", rows[0], rows[1])
-    du = cot[:, :, :fk]
-    du = jnp.concatenate([du[:, :1] + low[1:-1, None], du[:, 1:-1], du[:, -1:] + high[1:-1, None]], axis=1)
-    du = jnp.concatenate([du[:1] + below[None], du[1:-1], du[-1:] + above[None]], axis=0)
-    cot = jnp.concatenate([du, cot[:, :, fk:]], axis=2)
-
-    coarse_grads, fine_grads = pair_whole(*pair_whole(*sums, X_NEAR), Y_NEAR)
+    sums = pair_sum(*sums, Z_FAR)
+    (cot,) = call(rims_kernel, [(2 * fk, fx, fy, nz)], [], 2_000_000_000, cot, low, high, below, above)
+    coarse_grads, fine_grads = four_whole(*sums, X_NEAR, Y_NEAR)
     other = partner(jnp.concatenate([coarse_grads, fine_grads], axis=0), CORE)
     cut = coarse_grads.shape[0]
     sums = (coarse_grads, other[:cut], fine_grads, other[cut:])
@@ -706,7 +738,7 @@
     f_conv, f_in, f_proj, f_out, c_conv, c_in, c_proj, c_out = grads
     return (
         jnp.transpose(field, (2, 0, 1, 3)),
-        jnp.transpose(cot, (2, 0, 1, 3)),
+        cot,
         jnp.transpose(f_conv, (0, 2, 1)),
         f_in[0],
         f_proj,

time: 100 us -> 97.6 us (0.976)
  the two profiles are of different devices: /device:TPU:21 before, /device:TPU:33 now
where the time goes in v3:
time: 97.6 us; the launch traced here: 97.3 us
  starting transfers between devices  45.4 us (47%)
  waiting for transfers between devices  26 us (27%)
  Pallas kernels  22.3 us (23%)
  local copies, waits for them, and re-layouts  2.08 us (2%)
  between operations  1.21 us (1%)
    ppermute x15, starting transfers between devices, partner(): return lax.ppermute(x, ('gx', 'gy'), pairs)  24.4 us
    pallas_call x14, Pallas kernels, call(): pl.pallas_call(kernel, in_specs=specs, out_shape=[jax.ShapeDtypeStruct(s,...  22.3 us
    ppermute x15, waiting for transfers between devices, partner(): return lax.ppermute(x, ('gx', 'gy'), pairs)  17.4 us
    ppermute x6, starting transfers between devices, swapped(): two = lax.ppermute(two, axis, outer)  17.3 us
    ppermute x6, waiting for transfers between devices, swapped(): two = lax.ppermute(two, axis, outer)  8.53 us
    ppermute x6, starting transfers between devices, swapped(): one = lax.ppermute(one, axis, inner)  3.73 us
    unnamed x23, local copies, waits for them, and re-layouts  2.04 us
  transfers between devices with their start and end apart: 27, of which 13 were waited for; matrix products, arithmetic and copies ran while one was open for 1% of the time, Pallas kernels for 15%

profile of v3, /device:TPU:33, one launch (start us, length us, event | category | flops | bytes accessed | tf_op | source)
XLA Modules:
  0.0 97.3 jit_solution(10073347165882260402)
XLA Ops:
  0.7 1.0 %copy-done = f32[64,4,4,128]{3,2,1,0:T(4,128)S(1)} copy-done((f32[64,4,4,128]{3,2,1,0:T(4,128)S(1)}, f32[64,4,4,128]{3,2,1,0:T(4,128)}, u32[]{:S(2)}) %copy-start) | copy-done | bytes 524312
  1.8 0.6 shard_map.177
  2.4 0.8 collective-permute-start
  3.1 3.0 %collective-permute-start.1 = (f32[4,2,32,128]{3,2,1,0:T(8,128)S(1)}, f32[4,2,32,128]{3,2,1,0:T(8,128)S(1)}, u32[]{:S(2)}, u32[]{:S(2)}) collective-permute-start(f32[4,2,32,128]{3,2,1,0:T(8,128)S(1)} %get-tuple-element.73), channel_id=1, source_target_pairs={{1,2},{2,1},{3,4},{4,3},{5,6},{6,5},{7,8},{8,7},{9,10},{10,9},{11,... | collective-permute-start | bytes 393224 | tf_op jit(solution)/shard_map/ppermute | solution.py:517
  6.2 0.7 shard_map.181
  7.0 3.5 %collective-permute-start.5 = (f32[4,1,64,128]{3,2,1,0:T(8,128)S(1)}, f32[4,1,64,128]{3,2,1,0:T(8,128)S(1)}, u32[]{:S(2)}, u32[]{:S(2)}) collective-permute-start(f32[4,1,64,128]{3,2,1,0:T(8,128)S(1)} %get-tuple-element.84), channel_id=1, source_target_pairs={{1,2},{2,1},{3,4},{4,3},{5,6},{6,5},{7,8},{8,7},{9,10},{10,9},{11,... | collective-permute-start | bytes 393224 | tf_op jit(solution)/shard_map/ppermute | solution.py:517
  10.6 0.6 shard_map.179
  11.2 1.4 %collective-permute-start.2 = (f32[2,8,32,128]{3,2,1,0:T(8,128)S(1)}, f32[2,8,32,128]{3,2,1,0:T(8,128)S(1)}, u32[]{:S(2)}, u32[]{:S(2)}) collective-permute-start(f32[2,8,32,128]{3,2,1,0:T(8,128)S(1)} %get-tuple-element.75), channel_id=1, source_target_pairs={{0,16},{16,0},{32,48},{48,32},{64,80},{80,64},{96,112},{112,96},{1... | collective-permute-start | bytes 786440 | tf_op jit(solution)/shard_map/ppermute | solution.py:518
  12.6 3.3 %collective-permute-start.3 = (f32[2,8,32,128]{3,2,1,0:T(8,128)S(1)}, f32[2,8,32,128]{3,2,1,0:T(8,128)S(1)}, u32[]{:S(2)}, u32[]{:S(2)}) collective-permute-start(f32[2,8,32,128]{3,2,1,0:T(8,128)S(1)} %get-tuple-element.76), channel_id=1, source_target_pairs={{16,32},{32,16},{48,64},{64,48},{80,96},{96,80},{112,128},{128,112... | collective-permute-start | bytes 786440 | tf_op jit(solution)/shard_map/ppermute | solution.py:517
  16.0 0.6 shard_map.182
  16.6 0.9 collective-permute-start.6
  17.5 3.2 %collective-permute-start.7 = (f32[1,6,64,128]{3,2,1,0:T(8,128)S(1)}, f32[1,6,64,128]{3,2,1,0:T(8,128)S(1)}, u32[]{:S(2)}, u32[]{:S(2)}) collective-permute-start(f32[1,6,64,128]{3,2,1,0:T(8,128)S(1)} %get-tuple-element.86), channel_id=1, source_target_pairs={{16,32},{32,16},{48,64},{64,48},{80,96},{96,80},{112,128},{128,112... | collective-permute-start | bytes 589832 | tf_op jit(solution)/shard_map/ppermute | solution.py:517
  20.7 1.9 %shard_map.178 = (f32[4,96,1024]{2,1,0:T(8,128)S(1)}, f32[2,64,768]{2,1,0:T(8,128)S(1)}, f32[192,864]{1,0:T(8,128)S(1)}, f32[64,1]{1,0:T(8,128)S(1)}) custom-call(s32[2]{0:T(128)S(1)} %pad_add_fusion.at_ref.refs_0_, f32[4,4,32,128]{3,2,1,0:T(8,128)S(1)} %get-tuple-element.71.u_ref.f_ref, f32[4,2,32,128]{3,2,1,0:T(8,128)S(1)} %collective-permute-done.ya_ref, ...), custom_call_target="tpu_custom_call" | custom-call | flops 2500000000 | bytes 1000000 | tf_op jit(solution)/shard_map/pallas_call | solution.py:501
  22.7 2.3 %collective-permute-done.3.xb_ref = f32[2,8,32,128]{3,2,1,0:T(8,128)S(1)} collective-permute-done((f32[2,8,32,128]{3,2,1,0:T(8,128)S(1)}, f32[2,8,32,128]{3,2,1,0:T(8,128)S(1)}, u32[]{:S(2)}, u32[]{:S(2)}) %collective-permute-start.3) | collective-permute-done | bytes 262176 | tf_op jit(solution)/shard_map/ppermute | solution.py:517
  24.9 2.5 %shard_map.180 = (f32[4,96,1024]{2,1,0:T(8,128)S(1)}, f32[4,64,768]{2,1,0:T(8,128)S(1)}) custom-call(s32[2]{0:T(128)S(1)} %pad_add_fusion.at_ref.refs_0_, f32[4,96,1024]{2,1,0:T(8,128)S(1)} %get-tuple-element.74.inner_ref.refs_1_, f32[2,8,32,128]{3,2,1,0:T(8,128)S(1)} %collective-permute-done.2.xa_ref, f32[2,8,32,128]{3,2,1,0:T(8,128)S(1)} %collective-permute-done.3.xb_ref, ...), custom_call_target="tpu_custom_call" | custom-call | flops 4000000000 | bytes 1000000 | tf_op jit(solution)/shard_map/pallas_call | solution.py:501
  27.5 2.6 %collective-permute-done.7.refs_9_ = f32[1,6,64,128]{3,2,1,0:T(8,128)S(1)} collective-permute-done((f32[1,6,64,128]{3,2,1,0:T(8,128)S(1)}, f32[1,6,64,128]{3,2,1,0:T(8,128)S(1)}, u32[]{:S(2)}, u32[]{:S(2)}) %collective-permute-start.7) | collective-permute-done | bytes 196640 | tf_op jit(solution)/shard_map/ppermute | solution.py:517
  30.1 4.2 %shard_map.183 = (f32[6,6,64,128]{3,2,1,0:T(8,128)S(1)}, f32[6,64,768]{2,1,0:T(8,128)S(1)}, f32[4,32,512]{2,1,0:T(8,128)S(1)}, f32[512,128]{1,0:T(8,128)S(1)}) custom-call(s32[2]{0:T(128)S(1)} %pad_add_fusion.at_ref.refs_0_, f32[4,96,1024]{2,1,0:T(8,128)S(1)} %get-tuple-element.74.inner_ref.refs_1_, f32[4,96,1024]{2,1,0:T(8,128)S(1)} %get-tuple-element.79.refs_2_, ...), custom_call_target="tpu_custom_call" | custom-call | flops 6000000000 | bytes 1000000 | tf_op jit(solution)/shard_map/pallas_call | solution.py:501
  34.3 0.5 collective-permute-start.8
  34.8 1.9 %shard_map.184.refs_1_ = f32[4,4,64,128]{3,2,1,0:T(8,128)S(1)} custom-call(f32[6,64,768]{2,1,0:T(8,128)S(1)} %get-tuple-element.89.gpre_ref, f32[4,32,512]{2,1,0:T(8,128)S(1)} %get-tuple-element.90.low_ref, f32[4,4,32,128]{3,2,1,0:T(8,128)S(1)} %get-tuple-element.91.cot_ref, f32[27,32,64]{2,1,0:T(8,128)S(1)} %bitcast.25), custom_call_target="tpu_custom_call" | custom-call | flops 2500000000 | bytes 1000000 | tf_op jit(solution)/shard_map/pallas_call | solution.py:501
  36.8 0.3 collective-permute-start.9
  37.1 2.9 %shard_map.185 = (f32[4,8,16,128]{3,2,1,0:T(8,128)S(1)}, f32[4,8,16,128]{3,2,1,0:T(8,128)S(1)}, f32[4,8,32,128]{3,2,1,0:T(8,128)S(1)}, f32[104,128]{1,0:T(8,128)...) custom-call(f32[6,6,64,128]{3,2,1,0:T(8,128)S(1)} %get-tuple-element.92.refs_0_, ...), custom_call_target="tpu_custom_call" | custom-call | flops 4499999744 | bytes 1000000 | tf_op jit(solution)/shard_map/pallas_call | solution.py:501
  40.1 0.7 collective-permute-done.9
  40.8 2.5 %shard_map.186 = (f32[8,8,16,128]{3,2,1,0:T(8,128)S(1)}, f32[8,8,16,128]{3,2,1,0:T(8,128)S(1)}, f32[8,8,32,128]{3,2,1,0:T(8,128)S(1)}, f32[80,128]{1,0:T(8,128)S(1)}) custom-call(f32[6,6,64,128]{3,2,1,0:T(8,128)S(1)} %get-tuple-element.92.refs_0_, f32[4,4,64,128]{3,2,1,0:T(8,128)S(1)} %shard_map.184.refs_1_, f32[27,8,32]{2,1,0:T(8,128)S(1)} %bitcast.27, ...), custom_call_target="tpu_custom_call" | custom-call | flops 4499999744 | bytes 1000000 | tf_op jit(solution)/shard_map/pallas_call | solution.py:501
  43.3 0.3 collective-permute-done.10
  43.6 2.1 %collective-permute-start.11 = (f32[40,128]{1,0:T(8,128)S(1)}, f32[40,128]{1,0:T(8,128)S(1)}, u32[]{:S(2)}, u32[]{:S(2)}) collective-permute-start(f32[40,128]{1,0:T(8,128)S(1)} %slice_select_fusion.7), channel_id=1, source_target_pairs={{0,1},{1,0},{2,3},{3,2},{4,5},{5,4},{6,7},{7,6},{8,9},{9,8},{10,11... | collective-permute-start | bytes 61448 | tf_op jit(solution)/shard_map/ppermute | solution.py:536
  45.7 0.8 collective-permute-done.11
  46.6 8.3 %collective-permute-start.12 = (f32[104,128]{1,0:T(8,128)S(1)}, f32[104,128]{1,0:T(8,128)S(1)}, u32[]{:S(2)}, u32[]{:S(2)}) collective-permute-start(f32[104,128]{1,0:T(8,128)S(1)} %pad_maximum_fusion.4), channel_id=1, source_target_pairs={{0,6},{1,7},{2,4},{3,5},{4,2},{5,3},{6,0},{7,1},{8,14},{9,15},{10,... | collective-permute-start | bytes 159752 | tf_op jit(solution)/shard_map/ppermute | solution.py:536
  54.8 1.9 %collective-permute-start.13 = (f32[104,128]{1,0:T(8,128)S(1)}, f32[104,128]{1,0:T(8,128)S(1)}, u32[]{:S(2)}, u32[]{:S(2)}) collective-permute-start(f32[104,128]{1,0:T(8,128)S(1)} %pad_maximum_fusion.4), channel_id=1, source_target_pairs={{0,48},{1,49},{2,50},{3,51},{4,52},{5,53},{6,54},{7,55},{8,56},{9,... | collective-permute-start | bytes 159752 | tf_op jit(solution)/shard_map/ppermute | solution.py:536
  56.7 0.6 collective-permute-start.14
  57.3 1.7 %collective-permute-done.13 = f32[104,128]{1,0:T(8,128)S(1)} collective-permute-done((f32[104,128]{1,0:T(8,128)S(1)}, f32[104,128]{1,0:T(8,128)S(1)}, u32[]{:S(2)}, u32[]{:S(2)}) %collective-permute-start.13) | collective-permute-done | bytes 53280 | tf_op jit(solution)/shard_map/ppermute | solution.py:536
  59.0 4.0 %collective-permute-done.14 = f32[104,128]{1,0:T(8,128)S(1)} collective-permute-done((f32[104,128]{1,0:T(8,128)S(1)}, f32[104,128]{1,0:T(8,128)S(1)}, u32[]{:S(2)}, u32[]{:S(2)}) %collective-permute-start.14) | collective-permute-done | bytes 53280 | tf_op jit(solution)/shard_map/ppermute | solution.py:536
  63.1 1.4 %shard_map.187 = (f32[8,8,16,128]{3,2,1,0:T(8,128)S(1)}, f32[2,10,8,128]{3,2,1,0:T(8,128)S(1)}, f32[2,8,8,128]{3,2,1,0:T(8,128)S(1)}) custom-call(f32[8,8,32,128]{3,2,1,0:T(8,128)S(1)} %get-tuple-element.113.gpre_ref, f32[8,8,16,128]{3,2,1,0:T(8,128)S(1)} %get-tuple-element.114.cot_ref, f32[27,8,32]{2,1,0:T(8,128)S(1)} %bitcast.28), custom_call_target="tpu_custom_call" | custom-call | flops 4000000000 | bytes 1000000 | tf_op jit(solution)/shard_map/pallas_call | solution.py:501
  64.5 2.3 %collective-permute-start.18 = (f32[10,8,128]{2,1,0:T(8,128)S(1)}, f32[10,8,128]{2,1,0:T(8,128)S(1)}, u32[]{:S(2)}, u32[]{:S(2)}) collective-permute-start(f32[10,8,128]{2,1,0:T(8,128)S(1)} %get-tuple-element.151), channel_id=1, source_target_pairs={{1,2},{2,1},{3,4},{4,3},{5,6},{6,5},{7,8},{8,7},{9,10},{10,9},{11,... | collective-permute-start | bytes 122888 | tf_op jit(solution)/shard_map/ppermute | solution.py:517
  66.9 0.5 collective-permute-start.19
  67.3 0.3 collective-permute-start.15
  67.6 2.4 %collective-permute-start.16 = (f32[104,128]{1,0:T(8,128)S(1)}, f32[104,128]{1,0:T(8,128)S(1)}, u32[]{:S(2)}, u32[]{:S(2)}) collective-permute-start(f32[104,128]{1,0:T(8,128)S(1)} %constant_dynamic-update-slice_fusion), channel_id=1, source_target_pairs={{0,128},{1,129},{2,130},{3,131},{4,132},{5,133},{6,134},{7,135},{8... | collective-permute-start | bytes 159752 | tf_op jit(solution)/shard_map/ppermute | solution.py:536
  70.1 0.3 collective-permute-done.15
  70.3 3.7 %collective-permute-done.16 = f32[104,128]{1,0:T(8,128)S(1)} collective-permute-done((f32[104,128]{1,0:T(8,128)S(1)}, f32[104,128]{1,0:T(8,128)S(1)}, u32[]{:S(2)}, u32[]{:S(2)}) %collective-permute-start.16) | collective-permute-done | bytes 53280 | tf_op jit(solution)/shard_map/ppermute | solution.py:536
  74.0 2.2 %collective-permute-done.17 = f32[104,128]{1,0:T(8,128)S(1)} collective-permute-done((f32[104,128]{1,0:T(8,128)S(1)}, f32[104,128]{1,0:T(8,128)S(1)}, u32[]{:S(2)}, u32[]{:S(2)}) %collective-permute-start.17) | collective-permute-done | bytes 53280 | tf_op jit(solution)/shard_map/ppermute | solution.py:536
  76.2 4.6 %collective-permute-start.22 = (f32[104,128]{1,0:T(8,128)S(1)}, f32[104,128]{1,0:T(8,128)S(1)}, u32[]{:S(2)}, u32[]{:S(2)}) collective-permute-start(f32[104,128]{1,0:T(8,128)S(1)} %constant_dynamic-update-slice_fusion.2), channel_id=1, source_target_pairs={{0,200},{1,201},{2,202},{3,203},{4,204},{5,205},{6,206},{7,207},{8... | collective-permute-start | bytes 159752 | tf_op jit(solution)/shard_map/ppermute | solution.py:536
  80.8 1.9 %collective-permute-start.20 = (f32[8,8,128]{2,1,0:T(8,128)S(1)}, f32[8,8,128]{2,1,0:T(8,128)S(1)}, u32[]{:S(2)}, u32[]{:S(2)}) collective-permute-start(f32[8,8,128]{2,1,0:T(8,128)S(1)} %get-tuple-element.155), channel_id=1, source_target_pairs={{16,32},{32,16},{48,64},{64,48},{80,96},{96,80},{112,128},{128,112... | collective-permute-start | bytes 98312 | tf_op jit(solution)/shard_map/ppermute | solution.py:517
  82.8 1.0 copy.20
  83.9 3.7 %collective-permute-done.20 = f32[8,8,128]{2,1,0:T(8,128)S(1)} collective-permute-done((f32[8,8,128]{2,1,0:T(8,128)S(1)}, f32[8,8,128]{2,1,0:T(8,128)S(1)}, u32[]{:S(2)}, u32[]{:S(2)}) %collective-permute-start.20) | collective-permute-done | bytes 32800 | tf_op jit(solution)/shard_map/ppermute | solution.py:517
  87.8 3.7 %collective-permute-done.23 = f32[104,128]{1,0:T(8,128)S(1)} collective-permute-done((f32[104,128]{1,0:T(8,128)S(1)}, f32[104,128]{1,0:T(8,128)S(1)}, u32[]{:S(2)}, u32[]{:S(2)}) %collective-permute-start.23) | collective-permute-done | bytes 53280 | tf_op jit(solution)/shard_map/ppermute | solution.py:536
  91.6 3.1 %collective-permute-start.26 = (f32[296,128]{1,0:T(8,128)S(1)}, f32[296,128]{1,0:T(8,128)S(1)}, u32[]{:S(2)}, u32[]{:S(2)}) collective-permute-start(f32[296,128]{1,0:T(8,128)S(1)} %pad_maximum_fusion), channel_id=1, source_target_pairs={{0,1},{1,0},{2,3},{3,2},{4,5},{5,4},{6,7},{7,6},{8,9},{9,8},{10,11... | collective-permute-start | bytes 454664 | tf_op jit(solution)/shard_map/ppermute | solution.py:536
  94.8 0.9 shard_map.189
  95.7 0.1 collective-permute-done.26
  95.8 1.5 %shard_map.190 = (f32[27,8,32]{2,1,0:T(8,128)}, f32[1,32]{1,0:T(1,128)}, f32[16,32]{1,0:T(8,128)}, f32[1,16]{1,0:T(1,128)}, f32[27,32,64]{2,1,0:T(8,128)}, /*ind...) custom-call(s32[2]{0:T(128)S(1)} %pad_add_fusion.at_ref.refs_0_, f32[256,128]{1,0:T(8,128)S(1)} %pad_maximum_fusion.1.coarse_ref, ...), custom_call_target="tpu_custom_call" | custom-call | flops 1000000 | bytes 1000000 | tf_op jit(solution)/shard_map/pallas_call | solution.py:501
  (74 shorter events, 1.0 us)
Async XLA Ops:
  0.7 1.0 %copy-start = (f32[64,4,4,128]{3,2,1,0:T(4,128)S(1)}, f32[64,4,4,128]{3,2,1,0:T(4,128)}, u32[]{:S(2)}) copy-start(f32[64,4,4,128]{3,2,1,0:T(4,128)} %w_ref.3) | copy-start | bytes 1572868
  1.8 4.4 %copy-start.1 = (f32[64,4,4,128]{3,2,1,0:T(4,128)S(1)}, f32[64,4,4,128]{3,2,1,0:T(4,128)}, u32[]{:S(2)}) copy-start(f32[64,4,4,128]{3,2,1,0:T(4,128)} %dw_ref.1) | copy-start | bytes 1572868
  2.4 8.2 %collective-permute-start = (f32[4,2,32,128]{3,2,1,0:T(8,128)S(1)}, f32[4,2,32,128]{3,2,1,0:T(8,128)S(1)}, u32[]{:S(2)}, u32[]{:S(2)}) collective-permute-start(f32[4,2,32,128]{3,2,1,0:T(8,128)S(1)} %get-tuple-element.72), channel_id=1, source_target_pairs={{0,1},{1,0},{2,3},{3,2},{4,5},{5,4},{6,7},{7,6},{8,9},{9,8},{10,11... | collective-permute-start | bytes 393224 | tf_op jit(solution)/shard_map/ppermute | solution.py:518
  3.1 7.4 %collective-permute-start.1 = (f32[4,2,32,128]{3,2,1,0:T(8,128)S(1)}, f32[4,2,32,128]{3,2,1,0:T(8,128)S(1)}, u32[]{:S(2)}, u32[]{:S(2)}) collective-permute-start(f32[4,2,32,128]{3,2,1,0:T(8,128)S(1)} %get-tuple-element.73), channel_id=1, source_target_pairs={{1,2},{2,1},{3,4},{4,3},{5,6},{6,5},{7,8},{8,7},{9,10},{10,9},{11,... | collective-permute-start | bytes 393224 | tf_op jit(solution)/shard_map/ppermute | solution.py:517
  6.9 9.1 %collective-permute-start.4 = (f32[4,1,64,128]{3,2,1,0:T(8,128)S(1)}, f32[4,1,64,128]{3,2,1,0:T(8,128)S(1)}, u32[]{:S(2)}, u32[]{:S(2)}) collective-permute-start(f32[4,1,64,128]{3,2,1,0:T(8,128)S(1)} %get-tuple-element.83), channel_id=1, source_target_pairs={{0,1},{1,0},{2,3},{3,2},{4,5},{5,4},{6,7},{7,6},{8,9},{9,8},{10,11... | collective-permute-start | bytes 393224 | tf_op jit(solution)/shard_map/ppermute | solution.py:518
  7.0 9.0 %collective-permute-start.5 = (f32[4,1,64,128]{3,2,1,0:T(8,128)S(1)}, f32[4,1,64,128]{3,2,1,0:T(8,128)S(1)}, u32[]{:S(2)}, u32[]{:S(2)}) collective-permute-start(f32[4,1,64,128]{3,2,1,0:T(8,128)S(1)} %get-tuple-element.84), channel_id=1, source_target_pairs={{1,2},{2,1},{3,4},{4,3},{5,6},{6,5},{7,8},{8,7},{9,10},{10,9},{11,... | collective-permute-start | bytes 393224 | tf_op jit(solution)/shard_map/ppermute | solution.py:517
  10.6 10.1 %copy-start.2 = (f32[27,64,32]{1,2,0:T(8,128)S(1)}, f32[27,64,32]{1,2,0:T(8,128)}, u32[]{:S(2)}) copy-start(f32[27,64,32]{1,2,0:T(8,128)} %param.16) | copy-start | bytes 663556
  10.6 10.1 %copy-start.6 = (f32[64]{0:T(128)S(1)}, f32[64]{0:T(128)}, u32[]{:S(2)}) copy-start(f32[64]{0:T(128)} %param.17) | copy-start | bytes 772
  11.2 11.4 %collective-permute-start.2 = (f32[2,8,32,128]{3,2,1,0:T(8,128)S(1)}, f32[2,8,32,128]{3,2,1,0:T(8,128)S(1)}, u32[]{:S(2)}, u32[]{:S(2)}) collective-permute-start(f32[2,8,32,128]{3,2,1,0:T(8,128)S(1)} %get-tuple-element.75), channel_id=1, source_target_pairs={{0,16},{16,0},{32,48},{48,32},{64,80},{80,64},{96,112},{112,96},{1... | collective-permute-start | bytes 786440 | tf_op jit(solution)/shard_map/ppermute | solution.py:518
  12.6 12.3 %collective-permute-start.3 = (f32[2,8,32,128]{3,2,1,0:T(8,128)S(1)}, f32[2,8,32,128]{3,2,1,0:T(8,128)S(1)}, u32[]{:S(2)}, u32[]{:S(2)}) collective-permute-start(f32[2,8,32,128]{3,2,1,0:T(8,128)S(1)} %get-tuple-element.76), channel_id=1, source_target_pairs={{16,32},{32,16},{48,64},{64,48},{80,96},{96,80},{112,128},{128,112... | collective-permute-start | bytes 786440 | tf_op jit(solution)/shard_map/ppermute | solution.py:517
  16.6 10.9 %collective-permute-start.6 = (f32[1,6,64,128]{3,2,1,0:T(8,128)S(1)}, f32[1,6,64,128]{3,2,1,0:T(8,128)S(1)}, u32[]{:S(2)}, u32[]{:S(2)}) collective-permute-start(f32[1,6,64,128]{3,2,1,0:T(8,128)S(1)} %get-tuple-element.85), channel_id=1, source_target_pairs={{0,16},{16,0},{32,48},{48,32},{64,80},{80,64},{96,112},{112,96},{1... | collective-permute-start | bytes 589832 | tf_op jit(solution)/shard_map/ppermute | solution.py:518
  17.5 12.6 %collective-permute-start.7 = (f32[1,6,64,128]{3,2,1,0:T(8,128)S(1)}, f32[1,6,64,128]{3,2,1,0:T(8,128)S(1)}, u32[]{:S(2)}, u32[]{:S(2)}) collective-permute-start(f32[1,6,64,128]{3,2,1,0:T(8,128)S(1)} %get-tuple-element.86), channel_id=1, source_target_pairs={{16,32},{32,16},{48,64},{64,48},{80,96},{96,80},{112,128},{128,112... | collective-permute-start | bytes 589832 | tf_op jit(solution)/shard_map/ppermute | solution.py:517
  24.9 5.1 %copy-start.4 = (f32[64,64]{1,0:T(8,128)S(1)}, f32[64,64]{1,0:T(8,128)}, u32[]{:S(2)}) copy-start(f32[64,64]{1,0:T(8,128)} %refs_10_.1) | copy-start | bytes 49156
  24.9 5.1 %copy-start.7 = (f32[64]{0:T(128)S(1)}, f32[64]{0:T(128)}, u32[]{:S(2)}) copy-start(f32[64]{0:T(128)} %param.19) | copy-start | bytes 772
  34.3 2.4 %collective-permute-start.8 = (f32[256,128]{1,0:T(8,128)S(1)}, f32[256,128]{1,0:T(8,128)S(1)}, u32[]{:S(2)}, u32[]{:S(2)}) collective-permute-start(f32[256,128]{1,0:T(8,128)S(1)} %slice_select_fusion), channel_id=1, source_target_pairs={{0,1},{1,0},{2,3},{3,2},{4,5},{5,4},{6,7},{7,6},{8,9},{9,8},{10,11... | collective-permute-start | bytes 393224 | tf_op jit(solution)/shard_map/ppermute | solution.py:536
  34.8 2.3 %copy-start.3 = (f32[27,32,8]{1,2,0:T(8,128)S(1)}, f32[27,32,8]{1,2,0:T(8,128)}, u32[]{:S(2)}) copy-start(f32[27,32,8]{1,2,0:T(8,128)} %param.12) | copy-start | bytes 82948
  34.8 2.3 %copy-start.5 = (f32[16,32]{1,0:T(8,128)S(1)}, f32[16,32]{1,0:T(8,128)}, u32[]{:S(2)}) copy-start(f32[16,32]{1,0:T(8,128)} %refs_4_.3) | copy-start | bytes 6148
  34.8 2.3 %copy-start.8 = (f32[32]{0:T(128)S(1)}, f32[32]{0:T(128)}, u32[]{:S(2)}) copy-start(f32[32]{0:T(128)} %param.13) | copy-start | bytes 388
  34.8 2.3 %copy-start.9 = (f32[16]{0:T(128)S(1)}, f32[16]{0:T(128)}, u32[]{:S(2)}) copy-start(f32[16]{0:T(128)} %param.15) | copy-start | bytes 196
  36.8 3.9 %collective-permute-start.9 = (f32[128,128]{1,0:T(8,128)S(1)}, f32[128,128]{1,0:T(8,128)S(1)}, u32[]{:S(2)}, u32[]{:S(2)}) collective-permute-start(f32[128,128]{1,0:T(8,128)S(1)} %slice_select_fusion.1), channel_id=1, source_target_pairs={{0,16},{1,17},{2,18},{3,19},{4,20},{5,21},{6,22},{7,23},{8,24},{9,... | collective-permute-start | bytes 196616 | tf_op jit(solution)/shard_map/ppermute | solution.py:536
  40.7 2.9 %collective-permute-start.10 = (f32[64,128]{1,0:T(8,128)S(1)}, f32[64,128]{1,0:T(8,128)S(1)}, u32[]{:S(2)}, u32[]{:S(2)}) collective-permute-start(f32[64,128]{1,0:T(8,128)S(1)} %slice_select_fusion.6), channel_id=1, source_target_pairs={{0,2},{1,3},{2,0},{3,1},{4,6},{5,7},{6,4},{7,5},{8,10},{9,11},{10,... | collective-permute-start | bytes 98312 | tf_op jit(solution)/shard_map/ppermute | solution.py:536
  43.6 2.9 %collective-permute-start.11 = (f32[40,128]{1,0:T(8,128)S(1)}, f32[40,128]{1,0:T(8,128)S(1)}, u32[]{:S(2)}, u32[]{:S(2)}) collective-permute-start(f32[40,128]{1,0:T(8,128)S(1)} %slice_select_fusion.7), channel_id=1, source_target_pairs={{0,1},{1,0},{2,3},{3,2},{4,5},{5,4},{6,7},{7,6},{8,9},{9,8},{10,11... | collective-permute-start | bytes 61448 | tf_op jit(solution)/shard_map/ppermute | solution.py:536
  46.6 10.8 %collective-permute-start.12 = (f32[104,128]{1,0:T(8,128)S(1)}, f32[104,128]{1,0:T(8,128)S(1)}, u32[]{:S(2)}, u32[]{:S(2)}) collective-permute-start(f32[104,128]{1,0:T(8,128)S(1)} %pad_maximum_fusion.4), channel_id=1, source_target_pairs={{0,6},{1,7},{2,4},{3,5},{4,2},{5,3},{6,0},{7,1},{8,14},{9,15},{10,... | collective-permute-start | bytes 159752 | tf_op jit(solution)/shard_map/ppermute | solution.py:536
  54.8 4.2 %collective-permute-start.13 = (f32[104,128]{1,0:T(8,128)S(1)}, f32[104,128]{1,0:T(8,128)S(1)}, u32[]{:S(2)}, u32[]{:S(2)}) collective-permute-start(f32[104,128]{1,0:T(8,128)S(1)} %pad_maximum_fusion.4), channel_id=1, source_target_pairs={{0,48},{1,49},{2,50},{3,51},{4,52},{5,53},{6,54},{7,55},{8,56},{9,... | collective-permute-start | bytes 159752 | tf_op jit(solution)/shard_map/ppermute | solution.py:536
  56.7 6.3 %collective-permute-start.14 = (f32[104,128]{1,0:T(8,128)S(1)}, f32[104,128]{1,0:T(8,128)S(1)}, u32[]{:S(2)}, u32[]{:S(2)}) collective-permute-start(f32[104,128]{1,0:T(8,128)S(1)} %pad_maximum_fusion.4), channel_id=1, source_target_pairs={{0,54},{1,55},{2,52},{3,53},{4,50},{5,51},{6,48},{7,49},{8,62},{9,... | collective-permute-start | bytes 159752 | tf_op jit(solution)/shard_map/ppermute | solution.py:536
  64.5 5.5 %collective-permute-start.18 = (f32[10,8,128]{2,1,0:T(8,128)S(1)}, f32[10,8,128]{2,1,0:T(8,128)S(1)}, u32[]{:S(2)}, u32[]{:S(2)}) collective-permute-start(f32[10,8,128]{2,1,0:T(8,128)S(1)} %get-tuple-element.151), channel_id=1, source_target_pairs={{1,2},{2,1},{3,4},{4,3},{5,6},{6,5},{7,8},{8,7},{9,10},{10,9},{11,... | collective-permute-start | bytes 122888 | tf_op jit(solution)/shard_map/ppermute | solution.py:517
  66.9 3.2 %collective-permute-start.19 = (f32[10,8,128]{2,1,0:T(8,128)S(1)}, f32[10,8,128]{2,1,0:T(8,128)S(1)}, u32[]{:S(2)}, u32[]{:S(2)}) collective-permute-start(f32[10,8,128]{2,1,0:T(8,128)S(1)} %get-tuple-element.150), channel_id=1, source_target_pairs={{0,1},{1,0},{2,3},{3,2},{4,5},{5,4},{6,7},{7,6},{8,9},{9,8},{10,11... | collective-permute-start | bytes 122888 | tf_op jit(solution)/shard_map/ppermute | solution.py:518
  67.3 3.0 %collective-permute-start.15 = (f32[104,128]{1,0:T(8,128)S(1)}, f32[104,128]{1,0:T(8,128)S(1)}, u32[]{:S(2)}, u32[]{:S(2)}) collective-permute-start(f32[104,128]{1,0:T(8,128)S(1)} %constant_dynamic-update-slice_fusion), channel_id=1, source_target_pairs={{0,64},{1,65},{2,66},{3,67},{4,68},{5,69},{6,70},{7,71},{8,72},{9,... | collective-permute-start | bytes 159752 | tf_op jit(solution)/shard_map/ppermute | solution.py:536
  67.6 6.4 %collective-permute-start.16 = (f32[104,128]{1,0:T(8,128)S(1)}, f32[104,128]{1,0:T(8,128)S(1)}, u32[]{:S(2)}, u32[]{:S(2)}) collective-permute-start(f32[104,128]{1,0:T(8,128)S(1)} %constant_dynamic-update-slice_fusion), channel_id=1, source_target_pairs={{0,128},{1,129},{2,130},{3,131},{4,132},{5,133},{6,134},{7,135},{8... | collective-permute-start | bytes 159752 | tf_op jit(solution)/shard_map/ppermute | solution.py:536
  70.0 6.1 %collective-permute-start.17 = (f32[104,128]{1,0:T(8,128)S(1)}, f32[104,128]{1,0:T(8,128)S(1)}, u32[]{:S(2)}, u32[]{:S(2)}) collective-permute-start(f32[104,128]{1,0:T(8,128)S(1)} %constant_dynamic-update-slice_fusion), channel_id=1, source_target_pairs={{0,192},{1,193},{2,194},{3,195},{4,196},{5,197},{6,198},{7,199},{8... | collective-permute-start | bytes 159752 | tf_op jit(solution)/shard_map/ppermute | solution.py:536
  76.2 7.6 %collective-permute-start.22 = (f32[104,128]{1,0:T(8,128)S(1)}, f32[104,128]{1,0:T(8,128)S(1)}, u32[]{:S(2)}, u32[]{:S(2)}) collective-permute-start(f32[104,128]{1,0:T(8,128)S(1)} %constant_dynamic-update-slice_fusion.2), channel_id=1, source_target_pairs={{0,200},{1,201},{2,202},{3,203},{4,204},{5,205},{6,206},{7,207},{8... | collective-permute-start | bytes 159752 | tf_op jit(solution)/shard_map/ppermute | solution.py:536
  80.8 6.8 %collective-permute-start.20 = (f32[8,8,128]{2,1,0:T(8,128)S(1)}, f32[8,8,128]{2,1,0:T(8,128)S(1)}, u32[]{:S(2)}, u32[]{:S(2)}) collective-permute-start(f32[8,8,128]{2,1,0:T(8,128)S(1)} %get-tuple-element.155), channel_id=1, source_target_pairs={{16,32},{32,16},{48,64},{64,48},{80,96},{96,80},{112,128},{128,112... | collective-permute-start | bytes 98312 | tf_op jit(solution)/shard_map/ppermute | solution.py:517
  82.7 4.8 %collective-permute-start.21 = (f32[8,8,128]{2,1,0:T(8,128)S(1)}, f32[8,8,128]{2,1,0:T(8,128)S(1)}, u32[]{:S(2)}, u32[]{:S(2)}) collective-permute-start(f32[8,8,128]{2,1,0:T(8,128)S(1)} %get-tuple-element.154), channel_id=1, source_target_pairs={{0,16},{16,0},{32,48},{48,32},{64,80},{80,64},{96,112},{112,96},{1... | collective-permute-start | bytes 98312 | tf_op jit(solution)/shard_map/ppermute | solution.py:518
  83.8 4.0 %collective-permute-start.25 = (f32[104,128]{1,0:T(8,128)S(1)}, f32[104,128]{1,0:T(8,128)S(1)}, u32[]{:S(2)}, u32[]{:S(2)}) collective-permute-start(f32[104,128]{1,0:T(8,128)S(1)} %add.88), channel_id=1, source_target_pairs={{0,2},{1,3},{2,0},{3,1},{4,6},{5,7},{6,4},{7,5},{8,10},{9,11},{10,... | collective-permute-start | bytes 159752 | tf_op jit(solution)/shard_map/ppermute | solution.py:536
  87.6 4.0 %collective-permute-start.23 = (f32[104,128]{1,0:T(8,128)S(1)}, f32[104,128]{1,0:T(8,128)S(1)}, u32[]{:S(2)}, u32[]{:S(2)}) collective-permute-start(f32[104,128]{1,0:T(8,128)S(1)} %add.88), channel_id=1, source_target_pairs={{0,18},{1,19},{2,16},{3,17},{4,22},{5,23},{6,20},{7,21},{8,26},{9,... | collective-permute-start | bytes 159752 | tf_op jit(solution)/shard_map/ppermute | solution.py:536
  87.7 3.9 %collective-permute-start.24 = (f32[104,128]{1,0:T(8,128)S(1)}, f32[104,128]{1,0:T(8,128)S(1)}, u32[]{:S(2)}, u32[]{:S(2)}) collective-permute-start(f32[104,128]{1,0:T(8,128)S(1)} %add.88), channel_id=1, source_target_pairs={{0,16},{1,17},{2,18},{3,19},{4,20},{5,21},{6,22},{7,23},{8,24},{9,... | collective-permute-start | bytes 159752 | tf_op jit(solution)/shard_map/ppermute | solution.py:536
  91.6 4.2 %collective-permute-start.26 = (f32[296,128]{1,0:T(8,128)S(1)}, f32[296,128]{1,0:T(8,128)S(1)}, u32[]{:S(2)}, u32[]{:S(2)}) collective-permute-start(f32[296,128]{1,0:T(8,128)S(1)} %pad_maximum_fusion), channel_id=1, source_target_pairs={{0,1},{1,0},{2,3},{3,2},{4,5},{5,4},{6,7},{7,6},{8,9},{9,8},{10,11... | collective-permute-start | bytes 454664 | tf_op jit(solution)/shard_map/ppermute | solution.py:536

commit v4 on v3

--- a/solution.py
+++ b/solution.py
@@ -328,14 +328,9 @@
     return rows
 
 
-def fine_kernel(factor, first, count, n_in, n_out, *refs):
-    q_ref, dq_ref, conv_ref, in_ref, proj_ref, out_ref = refs[:6]
-    before = refs[6:n_in]
-    field_ref, cot_ref, gpre_ref, *grads_ref = refs[n_in : n_in + n_out]
-    scratch = refs[n_in + n_out :]
-    taps, v_s, dz_s = scratch[:3]
-    sums, rests, g_sum = scratch[3:] if before else grads_ref
-    ny = field_ref.shape[1]
+def fine_kernel(factor, q_ref, dq_ref, conv_ref, in_ref, proj_ref, out_ref,
+                field_ref, cot_ref, gpre_ref, grads_ref, taps, v_s, dz_s, sums, rests, g_sum):
+    nx, ny = field_ref.shape[0], field_ref.shape[1]
     k = field_ref.shape[2] // 2
     h = conv_ref.shape[2]
     wp = forward_weight(conv_ref, 8)
@@ -344,30 +339,21 @@
     cy = ny // 2
 
     for x in range(q_ref.shape[0]):
-        wanted = [r for r in (2 * x, 2 * x + 1) if first + 1 <= r <= first + count + 2]
-        if wanted:
-            pair = finer_rows(row_of(q_ref, x, 0, cy + 2))
-        for r in wanted:
-            z = pair[r - 2 * x]
-            taps[r - 1 - first] = taps_along_z(z[:k, 128 : 128 * (ny + 3)])
-            if first + 2 <= r < first + count + 2:
-                v_s[r - 2 - first] = z[k:, 256 : 128 * (ny + 2)]
-    for x in range(first // 2, (first + count) // 2):
-        pair = finer_rows(row_of(dq_ref, x, 0, cy))
-        dz_s[2 * x - first] = pair[0]
-        dz_s[2 * x + 1 - first] = pair[1]
-
-    if before:
-        sums[...], rests[...], g_sum[...] = before[3][...], before[4][...], before[5][...]
-        for ref, old in zip((field_ref, cot_ref, gpre_ref), before):
-            ref[:first] = old[...]
-    else:
-        sums[...] = jnp.zeros_like(sums)
-        rests[...] = jnp.zeros_like(rests)
-        g_sum[...] = jnp.zeros_like(g_sum)
-    at = first if before else 0
-
-    for x in range(count):
+        pair = finer_rows(row_of(q_ref, x, 0, cy + 2))
+        for r in (2 * x, 2 * x + 1):
+            if 1 <= r <= nx + 2:
+                z = pair[r - 2 * x]
+                taps[r - 1] = taps_along_z(z[:k, 128 : 128 * (ny + 3)])
+                if 2 <= r < nx + 2:
+                    v_s[r - 2] = z[k:, 256 : 128 * (ny + 2)]
+    for x in range(nx // 2):
+        dz_s[2 * x], dz_s[2 * x + 1] = finer_rows(row_of(dq_ref, x, 0, cy))
+
+    sums[...] = jnp.zeros_like(sums)
+    rests[...] = jnp.zeros_like(rests)
+    g_sum[...] = jnp.zeros_like(g_sum)
+
+    for x in range(nx):
         patch = jnp.concatenate([taps[x], taps[x + 1], taps[x + 2]], axis=0)
         pre = window(dot(wp, stacked(patch, 8)), h, ny * 128, False) + bi
         dz = dz_s[x]
@@ -380,17 +366,15 @@
         cot = jnp.concatenate([dz[:k], lower_cot], axis=0)
         for y in range(ny):
             cols = slice(128 * y, 128 * (y + 1))
-            field_ref[at + x, y] = field[:, cols]
-            cot_ref[at + x, y] = cot[:, cols]
-            gpre_ref[at + x, y] = gpre[:, cols]
-
-    if before:
-        (grads,) = grads_ref
-        conv, bias_in, proj, bias_out = gathered(sums[...], rests[...], g_sum[...], 9 * k, 2 * k, 3 * h)
-        spare = jnp.zeros((9 * k - 2 * k - 16, 128), f32)
-        others = jnp.concatenate([proj, pltpu.roll(bias_in, h, 1), bias_out, spare], axis=0)
-        grads[: 9 * k] = lanes_from(3 * h, others, conv) * factor
-        grads[9 * k :] = jnp.zeros((grads.shape[0] - 9 * k, 128), f32)
+            field_ref[x, y] = field[:, cols]
+            cot_ref[x, y] = cot[:, cols]
+            gpre_ref[x, y] = gpre[:, cols]
+
+    conv, bias_in, proj, bias_out = gathered(sums[...], rests[...], g_sum[...], 9 * k, 2 * k, 3 * h)
+    spare = jnp.zeros((9 * k - 2 * k - 16, 128), f32)
+    others = jnp.concatenate([proj, pltpu.roll(bias_in, h, 1), bias_out, spare], axis=0)
+    grads_ref[: 9 * k] = lanes_from(3 * h, others, conv) * factor
+    grads_ref[9 * k :] = jnp.zeros((grads_ref.shape[0] - 9 * k, 128), f32)
 
 
 def fine_back_kernel(gpre_ref, cot_ref, conv_ref, out_ref, columns_ref, rows_ref, gpre_s):
@@ -570,11 +554,25 @@
     return partner(x, first), partner(x, second), partner(x, both)
 
 
-def four_sum(coarse, fine, first, second):
+def quarter_sum(x, first, second):
+    rows = x.shape[0] // 4
+    one, two = second_half(first), second_half(second)
+    mine, other = (jnp.where(two, x[a:b], x[c:d]) for a, b, c, d in
+                   ((2 * rows, 4 * rows, 0, 2 * rows), (0, 2 * rows, 2 * rows, 4 * rows)))
+    both = (first[0] ^ second[0], first[1] ^ second[1])
+    kept = jnp.where(one, mine[rows:], mine[:rows])
+    a = partner(jnp.where(one, mine[:rows], mine[rows:]), first)
+    b = partner(jnp.where(one, other[rows:], other[:rows]), second)
+    c = partner(jnp.where(one, other[:rows], other[rows:]), both)
+    return (kept + a) + (b + c)
+
+
+def four_sum(coarse, fine, first, second, *later):
     both = jnp.concatenate([coarse, fine], axis=0)
     a, b, c = partners(both, first, second)
+    a, *later = tied(a, *later)
     both = (both + a) + (b + c)
-    return both[: coarse.shape[0]], both[coarse.shape[0] :]
+    return both[: coarse.shape[0]], both[coarse.shape[0] :], *later
 
 
 def pair_sum(coarse, fine, step):
@@ -678,33 +676,33 @@
     coarse_grads = half_sum(coarse_grads, CORE)
     (dq,) = call(coarse_back_kernel, [(nx, ny, 2 * k, nz)], [], 2_500_000_000, c_gpre, low, cot_u, c_conv)
     coarse_grads, q, dq = tied(coarse_grads, q, dq)
-    coarse_grads = half_sum(coarse_grads, Y_NEAR)
+    coarse_grads = quarter_sum(coarse_grads, X_NEAR, Y_NEAR)
 
     fx, fy = 2 * nx, 2 * ny
-    weights = (f_conv, fine_bias_in[None, :], fine_proj, fine_bias_out[None, :])
-    sums_shapes = [(9 * fk + 16 + 2 * fk, 4 * fh), (9 * fk + 2 * fk, 4 * fh), (2 * fk, 128)]
-
-    def fine(first, count, rows, last, *before):
-        ins = (q, dq, *weights, *before)
-        outs = [(rows, fy, 2 * fk, nz), (rows, fy, 2 * fk, nz), (rows, fy, fh, nz), *last]
-        scratch = [(count + 2, 3 * fk, (fy + 2) * nz), (count, fk, fy * nz), (count, 2 * fk, fy * nz)]
-        return call(
-            lambda *refs: fine_kernel(factor, first, count, len(ins), len(outs), *refs),
-            outs,
-            scratch + (sums_shapes if before else []),
-            4_500_000_000,
-            *ins,
-        )
-
-    part = fine(0, nx, nx, sums_shapes)
-    coarse_grads, *part = tied(coarse_grads, *part)
-    coarse_grads = half_sum(coarse_grads, X_NEAR)
-    field, cot, gpre, fine_grads = fine(nx, nx, fx, [(10 * fk, 128)], *part)
+    field, cot, gpre, fine_grads = call(
+        lambda *refs: fine_kernel(factor, *refs),
+        [(fx, fy, 2 * fk, nz), (fx, fy, 2 * fk, nz), (fx, fy, fh, nz), (10 * fk, 128)],
+        [
+            (fx + 2, 3 * fk, (fy + 2) * nz),
+            (fx, fk, fy * nz),
+            (fx, 2 * fk, fy * nz),
+            (9 * fk + 16 + 2 * fk, 4 * fh),
+            (9 * fk + 2 * fk, 4 * fh),
+            (2 * fk, 128),
+        ],
+        9_000_000_000,
+        q,
+        dq,
+        f_conv,
+        fine_bias_in[None, :],
+        fine_proj,
+        fine_bias_out[None, :],
+    )
     coarse_grads, fine_grads = tied(coarse_grads, fine_grads)
     fine_grads = half_sum(fine_grads, CORE)
 
     sums = four_sum(coarse_grads, fine_grads, X_FAR, Y_FAR)
-    sums, gpre = tied(sums, gpre)
+    *sums, gpre = four_sum(*sums, Z_ONE, Z_TWO, gpre)
     cot, columns, rows = call(
         fine_back_kernel,
         [cot.shape, (2, fx + 2, fk, nz), (2, fy, fk, nz)],
@@ -715,8 +713,6 @@
         f_conv,
     )
     low, high = halos("gy", columns[0], columns[1])
-    sums = four_sum(*sums, Z_ONE, Z_TWO)
-    sums, low, high = tied(sums, low, high)
     (rows,) = call(corners_kernel, [rows.shape], [], 6_000_000_000, rows, low, high)
     below, above = halos("gx", rows[0], rows[1])
     sums = pair_sum(*sums, Z_FAR)

time: 97.6 us -> 92 us (0.943)
  the two profiles are of different devices: /device:TPU:33 before, /device:TPU:235 now
where the time goes in v4:
time: 92 us; the launch traced here: 91.8 us
  starting transfers between devices  61.2 us (67%)
  Pallas kernels  21.2 us (23%)
  waiting for transfers between devices  5.81 us (6%)
  local copies, waits for them, and re-layouts  2.05 us (2%)
  between operations  1.21 us (1%)
    ppermute x16, starting transfers between devices, partner(): return lax.ppermute(x, ('gx', 'gy'), pairs)  33.1 us
    ppermute x6, starting transfers between devices, swapped(): two = lax.ppermute(two, axis, outer)  21.5 us
    pallas_call x13, Pallas kernels, call(): pl.pallas_call(kernel, in_specs=specs, out_shape=[jax.ShapeDtypeStruct(s,...  21.2 us
    ppermute x6, starting transfers between devices, swapped(): one = lax.ppermute(one, axis, inner)  6.5 us
    ppermute x16, waiting for transfers between devices, partner(): return lax.ppermute(x, ('gx', 'gy'), pairs)  5.55 us
    unnamed x21, local copies, waits for them, and re-layouts  2.04 us
  transfers between devices with their start and end apart: 28, of which 7 were waited for; matrix products, arithmetic and copies ran while one was open for 1% of the time, Pallas kernels for 16%

profile of v4, /device:TPU:235, one launch (start us, length us, event | category | flops | bytes accessed | tf_op | source)
XLA Modules:
  0.0 91.8 jit_solution(12115758225942306914)
XLA Ops:
  0.6 0.1 pad_add_fusion.at_ref.refs_0_
  0.7 1.0 %copy-done = f32[64,4,4,128]{3,2,1,0:T(4,128)S(1)} copy-done((f32[64,4,4,128]{3,2,1,0:T(4,128)S(1)}, f32[64,4,4,128]{3,2,1,0:T(4,128)}, u32[]{:S(2)}) %copy-start) | copy-done | bytes 524312
  1.8 0.6 shard_map.177
  2.4 0.8 collective-permute-start
  3.1 3.0 %collective-permute-start.1 = (f32[4,2,32,128]{3,2,1,0:T(8,128)S(1)}, f32[4,2,32,128]{3,2,1,0:T(8,128)S(1)}, u32[]{:S(2)}, u32[]{:S(2)}) collective-permute-start(f32[4,2,32,128]{3,2,1,0:T(8,128)S(1)} %get-tuple-element.55), channel_id=1, source_target_pairs={{1,2},{2,1},{3,4},{4,3},{5,6},{6,5},{7,8},{8,7},{9,10},{10,9},{11,... | collective-permute-start | bytes 393224 | tf_op jit(solution)/shard_map/ppermute | solution.py:501
  6.2 0.7 shard_map.181
  6.9 0.1 collective-permute-start.4
  7.0 3.2 %collective-permute-start.5 = (f32[4,1,64,128]{3,2,1,0:T(8,128)S(1)}, f32[4,1,64,128]{3,2,1,0:T(8,128)S(1)}, u32[]{:S(2)}, u32[]{:S(2)}) collective-permute-start(f32[4,1,64,128]{3,2,1,0:T(8,128)S(1)} %get-tuple-element.66), channel_id=1, source_target_pairs={{1,2},{2,1},{3,4},{4,3},{5,6},{6,5},{7,8},{8,7},{9,10},{10,9},{11,... | collective-permute-start | bytes 393224 | tf_op jit(solution)/shard_map/ppermute | solution.py:501
  10.3 0.6 shard_map.179
  10.9 0.3 collective-permute-start.2
  11.2 4.0 %collective-permute-start.3 = (f32[2,8,32,128]{3,2,1,0:T(8,128)S(1)}, f32[2,8,32,128]{3,2,1,0:T(8,128)S(1)}, u32[]{:S(2)}, u32[]{:S(2)}) collective-permute-start(f32[2,8,32,128]{3,2,1,0:T(8,128)S(1)} %get-tuple-element.58), channel_id=1, source_target_pairs={{16,32},{32,16},{48,64},{64,48},{80,96},{96,80},{112,128},{128,112... | collective-permute-start | bytes 786440 | tf_op jit(solution)/shard_map/ppermute | solution.py:501
  15.2 0.6 shard_map.182
  15.8 1.6 %collective-permute-start.6 = (f32[1,6,64,128]{3,2,1,0:T(8,128)S(1)}, f32[1,6,64,128]{3,2,1,0:T(8,128)S(1)}, u32[]{:S(2)}, u32[]{:S(2)}) collective-permute-start(f32[1,6,64,128]{3,2,1,0:T(8,128)S(1)} %get-tuple-element.67), channel_id=1, source_target_pairs={{0,16},{16,0},{32,48},{48,32},{64,80},{80,64},{96,112},{112,96},{1... | collective-permute-start | bytes 589832 | tf_op jit(solution)/shard_map/ppermute | solution.py:502
  17.4 1.9 %collective-permute-start.7 = (f32[1,6,64,128]{3,2,1,0:T(8,128)S(1)}, f32[1,6,64,128]{3,2,1,0:T(8,128)S(1)}, u32[]{:S(2)}, u32[]{:S(2)}) collective-permute-start(f32[1,6,64,128]{3,2,1,0:T(8,128)S(1)} %get-tuple-element.68), channel_id=1, source_target_pairs={{16,32},{32,16},{48,64},{64,48},{80,96},{96,80},{112,128},{128,112... | collective-permute-start | bytes 589832 | tf_op jit(solution)/shard_map/ppermute | solution.py:501
  19.4 1.9 %shard_map.178 = (f32[4,96,1024]{2,1,0:T(8,128)S(1)}, f32[2,64,768]{2,1,0:T(8,128)S(1)}, f32[192,864]{1,0:T(8,128)S(1)}, f32[64,1]{1,0:T(8,128)S(1)}) custom-call(s32[2]{0:T(128)S(1)} %pad_add_fusion.at_ref.refs_0_, f32[4,4,32,128]{3,2,1,0:T(8,128)S(1)} %get-tuple-element.53.u_ref.f_ref, f32[4,2,32,128]{3,2,1,0:T(8,128)S(1)} %collective-permute-done.ya_ref, ...), custom_call_target="tpu_custom_call" | custom-call | flops 2500000000 | bytes 1000000 | tf_op jit(solution)/shard_map/pallas_call | solution.py:485
  21.3 2.5 %shard_map.180 = (f32[4,96,1024]{2,1,0:T(8,128)S(1)}, f32[4,64,768]{2,1,0:T(8,128)S(1)}) custom-call(s32[2]{0:T(128)S(1)} %pad_add_fusion.at_ref.refs_0_, f32[4,96,1024]{2,1,0:T(8,128)S(1)} %get-tuple-element.56.inner_ref.refs_1_, f32[2,8,32,128]{3,2,1,0:T(8,128)S(1)} %collective-permute-done.2.xa_ref, f32[2,8,32,128]{3,2,1,0:T(8,128)S(1)} %collective-permute-done.3.xb_ref, ...), custom_call_target="tpu_custom_call" | custom-call | flops 4000000000 | bytes 1000000 | tf_op jit(solution)/shard_map/pallas_call | solution.py:485
  23.9 0.2 collective-permute-done.7.refs_9_
  24.1 4.2 %shard_map.183 = (f32[6,6,64,128]{3,2,1,0:T(8,128)S(1)}, f32[6,64,768]{2,1,0:T(8,128)S(1)}, f32[4,32,512]{2,1,0:T(8,128)S(1)}, f32[512,128]{1,0:T(8,128)S(1)}) custom-call(s32[2]{0:T(128)S(1)} %pad_add_fusion.at_ref.refs_0_, f32[4,96,1024]{2,1,0:T(8,128)S(1)} %get-tuple-element.56.inner_ref.refs_1_, f32[4,96,1024]{2,1,0:T(8,128)S(1)} %get-tuple-element.61.refs_2_, ...), custom_call_target="tpu_custom_call" | custom-call | flops 6000000000 | bytes 1000000 | tf_op jit(solution)/shard_map/pallas_call | solution.py:485
  28.3 2.9 %collective-permute-start.8 = (f32[256,128]{1,0:T(8,128)S(1)}, f32[256,128]{1,0:T(8,128)S(1)}, u32[]{:S(2)}, u32[]{:S(2)}) collective-permute-start(f32[256,128]{1,0:T(8,128)S(1)} %slice_select_fusion), channel_id=1, source_target_pairs={{0,1},{1,0},{2,3},{3,2},{4,5},{5,4},{6,7},{7,6},{8,9},{9,8},{10,11... | collective-permute-start | bytes 393224 | tf_op jit(solution)/shard_map/ppermute | solution.py:520
  31.2 1.9 %shard_map.184.refs_1_ = f32[4,4,64,128]{3,2,1,0:T(8,128)S(1)} custom-call(f32[6,64,768]{2,1,0:T(8,128)S(1)} %get-tuple-element.71.gpre_ref, f32[4,32,512]{2,1,0:T(8,128)S(1)} %get-tuple-element.72.low_ref, f32[4,4,32,128]{3,2,1,0:T(8,128)S(1)} %get-tuple-element.73.cot_ref, f32[27,32,64]{2,1,0:T(8,128)S(1)} %bitcast.25), custom_call_target="tpu_custom_call" | custom-call | flops 2500000000 | bytes 1000000 | tf_op jit(solution)/shard_map/pallas_call | solution.py:485
  33.2 5.8 %collective-permute-start.9 = (f32[64,128]{1,0:T(8,128)S(1)}, f32[64,128]{1,0:T(8,128)S(1)}, u32[]{:S(2)}, u32[]{:S(2)}) collective-permute-start(f32[64,128]{1,0:T(8,128)S(1)} %slice_select_fusion.9), channel_id=1, source_target_pairs={{0,2},{1,3},{2,0},{3,1},{4,6},{5,7},{6,4},{7,5},{8,10},{9,11},{10,... | collective-permute-start | bytes 98312 | tf_op jit(solution)/shard_map/ppermute | solution.py:520
  39.1 2.1 %collective-permute-start.10 = (f32[64,128]{1,0:T(8,128)S(1)}, f32[64,128]{1,0:T(8,128)S(1)}, u32[]{:S(2)}, u32[]{:S(2)}) collective-permute-start(f32[64,128]{1,0:T(8,128)S(1)} %get-tuple-element.123), channel_id=1, source_target_pairs={{0,16},{1,17},{2,18},{3,19},{4,20},{5,21},{6,22},{7,23},{8,24},{9,... | collective-permute-start | bytes 98312 | tf_op jit(solution)/shard_map/ppermute | solution.py:520
  41.2 4.3 %shard_map.185 = (f32[8,8,16,128]{3,2,1,0:T(8,128)S(1)}, f32[8,8,16,128]{3,2,1,0:T(8,128)S(1)}, f32[8,8,32,128]{3,2,1,0:T(8,128)S(1)}, f32[80,128]{1,0:T(8,128)S(1)}) custom-call(f32[6,6,64,128]{3,2,1,0:T(8,128)S(1)} %get-tuple-element.74.refs_0_, f32[4,4,64,128]{3,2,1,0:T(8,128)S(1)} %shard_map.184.refs_1_, f32[27,8,32]{2,1,0:T(8,128)S(1)} %bitcast.26, ...), custom_call_target="tpu_custom_call" | custom-call | flops 8999999488 | bytes 1000000 | tf_op jit(solution)/shard_map/pallas_call | solution.py:485
  45.6 1.1 %collective-permute-start.12 = (f32[40,128]{1,0:T(8,128)S(1)}, f32[40,128]{1,0:T(8,128)S(1)}, u32[]{:S(2)}, u32[]{:S(2)}) collective-permute-start(f32[40,128]{1,0:T(8,128)S(1)} %slice_select_fusion.10), channel_id=1, source_target_pairs={{0,1},{1,0},{2,3},{3,2},{4,5},{5,4},{6,7},{7,6},{8,9},{9,8},{10,11... | collective-permute-start | bytes 61448 | tf_op jit(solution)/shard_map/ppermute | solution.py:520
  46.7 0.8 collective-permute-done.12
  47.6 0.1 collective-permute-start.13
  47.7 0.1 collective-permute-start.14
  47.8 2.5 %collective-permute-start.15 = (f32[104,128]{1,0:T(8,128)S(1)}, f32[104,128]{1,0:T(8,128)S(1)}, u32[]{:S(2)}, u32[]{:S(2)}) collective-permute-start(f32[104,128]{1,0:T(8,128)S(1)} %pad_maximum_fusion.4), channel_id=1, source_target_pairs={{0,54},{1,55},{2,52},{3,53},{4,50},{5,51},{6,48},{7,49},{8,62},{9,... | collective-permute-start | bytes 159752 | tf_op jit(solution)/shard_map/ppermute | solution.py:520
  50.3 0.3 collective-permute-done.13
  50.6 0.1 collective-permute-done.14
  50.7 1.2 %collective-permute-done.15 = f32[104,128]{1,0:T(8,128)S(1)} collective-permute-done((f32[104,128]{1,0:T(8,128)S(1)}, f32[104,128]{1,0:T(8,128)S(1)}, u32[]{:S(2)}, u32[]{:S(2)}) %collective-permute-start.15) | collective-permute-done | bytes 53280 | tf_op jit(solution)/shard_map/ppermute | solution.py:520
  51.9 1.8 %collective-permute-start.16 = (f32[104,128]{1,0:T(8,128)S(1)}, f32[104,128]{1,0:T(8,128)S(1)}, u32[]{:S(2)}, u32[]{:S(2)}) collective-permute-start(f32[104,128]{1,0:T(8,128)S(1)} %add_add_fusion.1), channel_id=1, source_target_pairs={{0,64},{1,65},{2,66},{3,67},{4,68},{5,69},{6,70},{7,71},{8,72},{9,... | collective-permute-start | bytes 159752 | tf_op jit(solution)/shard_map/ppermute | solution.py:520
  53.8 0.1 collective-permute-start.21
  53.9 2.1 %collective-permute-start.22 = (f32[104,128]{1,0:T(8,128)S(1)}, f32[104,128]{1,0:T(8,128)S(1)}, u32[]{:S(2)}, u32[]{:S(2)}) collective-permute-start(f32[104,128]{1,0:T(8,128)S(1)} %add_add_fusion.1), channel_id=1, source_target_pairs={{0,192},{1,193},{2,194},{3,195},{4,196},{5,197},{6,198},{7,199},{8... | collective-permute-start | bytes 159752 | tf_op jit(solution)/shard_map/ppermute | solution.py:520
  56.0 1.4 %shard_map.186 = (f32[8,8,16,128]{3,2,1,0:T(8,128)S(1)}, f32[2,10,8,128]{3,2,1,0:T(8,128)S(1)}, f32[2,8,8,128]{3,2,1,0:T(8,128)S(1)}) custom-call(f32[8,8,32,128]{3,2,1,0:T(8,128)S(1)} %get-tuple-element.82.gpre_ref, f32[8,8,16,128]{3,2,1,0:T(8,128)S(1)} %get-tuple-element.83.cot_ref, f32[27,8,32]{2,1,0:T(8,128)S(1)} %bitcast.27), custom_call_target="tpu_custom_call" | custom-call | flops 4000000000 | bytes 1000000 | tf_op jit(solution)/shard_map/pallas_call | solution.py:485
  57.4 5.7 %collective-permute-start.17 = (f32[10,8,128]{2,1,0:T(8,128)S(1)}, f32[10,8,128]{2,1,0:T(8,128)S(1)}, u32[]{:S(2)}, u32[]{:S(2)}) collective-permute-start(f32[10,8,128]{2,1,0:T(8,128)S(1)} %get-tuple-element.117), channel_id=1, source_target_pairs={{1,2},{2,1},{3,4},{4,3},{5,6},{6,5},{7,8},{8,7},{9,10},{10,9},{11,... | collective-permute-start | bytes 122888 | tf_op jit(solution)/shard_map/ppermute | solution.py:501
  63.1 0.1 collective-permute-start.18
  63.3 1.6 %collective-permute-start.23 = (f32[104,128]{1,0:T(8,128)S(1)}, f32[104,128]{1,0:T(8,128)S(1)}, u32[]{:S(2)}, u32[]{:S(2)}) collective-permute-start(f32[104,128]{1,0:T(8,128)S(1)} %add_add_fusion), channel_id=1, source_target_pairs={{0,200},{1,201},{2,202},{3,203},{4,204},{5,205},{6,206},{7,207},{8... | collective-permute-start | bytes 159752 | tf_op jit(solution)/shard_map/ppermute | solution.py:520
  64.9 3.7 %collective-permute-start.19 = (f32[8,8,128]{2,1,0:T(8,128)S(1)}, f32[8,8,128]{2,1,0:T(8,128)S(1)}, u32[]{:S(2)}, u32[]{:S(2)}) collective-permute-start(f32[8,8,128]{2,1,0:T(8,128)S(1)} %get-tuple-element.121), channel_id=1, source_target_pairs={{16,32},{32,16},{48,64},{64,48},{80,96},{96,80},{112,128},{128,112... | collective-permute-start | bytes 98312 | tf_op jit(solution)/shard_map/ppermute | solution.py:501
  68.7 3.7 %collective-permute-start.20 = (f32[8,8,128]{2,1,0:T(8,128)S(1)}, f32[8,8,128]{2,1,0:T(8,128)S(1)}, u32[]{:S(2)}, u32[]{:S(2)}) collective-permute-start(f32[8,8,128]{2,1,0:T(8,128)S(1)} %get-tuple-element.120), channel_id=1, source_target_pairs={{0,16},{16,0},{32,48},{48,32},{64,80},{80,64},{96,112},{112,96},{1... | collective-permute-start | bytes 98312 | tf_op jit(solution)/shard_map/ppermute | solution.py:502
  72.4 1.0 %copy.20 = f32[16,8,8,128]{3,2,1,0:T(8,128)} copy(f32[16,8,8,128]{3,0,2,1:T(8,128)S(1)} %bitcast.23) | data formatting | bytes 1048576
  73.3 1.9 %collective-permute-start.24 = (f32[104,128]{1,0:T(8,128)S(1)}, f32[104,128]{1,0:T(8,128)S(1)}, u32[]{:S(2)}, u32[]{:S(2)}) collective-permute-start(f32[104,128]{1,0:T(8,128)S(1)} %add.92), channel_id=1, source_target_pairs={{0,18},{1,19},{2,16},{3,17},{4,22},{5,23},{6,20},{7,21},{8,26},{9,... | collective-permute-start | bytes 159752 | tf_op jit(solution)/shard_map/ppermute | solution.py:520
  75.3 1.5 %collective-permute-start.25 = (f32[104,128]{1,0:T(8,128)S(1)}, f32[104,128]{1,0:T(8,128)S(1)}, u32[]{:S(2)}, u32[]{:S(2)}) collective-permute-start(f32[104,128]{1,0:T(8,128)S(1)} %add.92), channel_id=1, source_target_pairs={{0,16},{1,17},{2,18},{3,19},{4,20},{5,21},{6,22},{7,23},{8,24},{9,... | collective-permute-start | bytes 159752 | tf_op jit(solution)/shard_map/ppermute | solution.py:520
  76.8 3.0 %collective-permute-done.26 = f32[104,128]{1,0:T(8,128)S(1)} collective-permute-done((f32[104,128]{1,0:T(8,128)S(1)}, f32[104,128]{1,0:T(8,128)S(1)}, u32[]{:S(2)}, u32[]{:S(2)}) %collective-permute-start.26) | collective-permute-done | bytes 53280 | tf_op jit(solution)/shard_map/ppermute | solution.py:520
  79.8 9.4 %collective-permute-start.27 = (f32[296,128]{1,0:T(8,128)S(1)}, f32[296,128]{1,0:T(8,128)S(1)}, u32[]{:S(2)}, u32[]{:S(2)}) collective-permute-start(f32[296,128]{1,0:T(8,128)S(1)} %pad_maximum_fusion), channel_id=1, source_target_pairs={{0,1},{1,0},{2,3},{3,2},{4,5},{5,4},{6,7},{7,6},{8,9},{9,8},{10,11... | collective-permute-start | bytes 454664 | tf_op jit(solution)/shard_map/ppermute | solution.py:520
  89.2 0.9 shard_map.188
  90.1 0.1 collective-permute-done.27
  90.3 1.5 %shard_map.189 = (f32[27,8,32]{2,1,0:T(8,128)}, f32[1,32]{1,0:T(1,128)}, f32[16,32]{1,0:T(8,128)}, f32[1,16]{1,0:T(1,128)}, f32[27,32,64]{2,1,0:T(8,128)}, /*ind...) custom-call(s32[2]{0:T(128)S(1)} %pad_add_fusion.at_ref.refs_0_, f32[256,128]{1,0:T(8,128)S(1)} %pad_maximum_fusion.1.coarse_ref, ...), custom_call_target="tpu_custom_call" | custom-call | flops 1000000 | bytes 1000000 | tf_op jit(solution)/shard_map/pallas_call | solution.py:485
  (67 shorter events, 0.4 us)
Async XLA Ops:
  0.7 1.0 %copy-start = (f32[64,4,4,128]{3,2,1,0:T(4,128)S(1)}, f32[64,4,4,128]{3,2,1,0:T(4,128)}, u32[]{:S(2)}) copy-start(f32[64,4,4,128]{3,2,1,0:T(4,128)} %w_ref.3) | copy-start | bytes 1572868
  1.8 4.4 %copy-start.1 = (f32[64,4,4,128]{3,2,1,0:T(4,128)S(1)}, f32[64,4,4,128]{3,2,1,0:T(4,128)}, u32[]{:S(2)}) copy-start(f32[64,4,4,128]{3,2,1,0:T(4,128)} %dw_ref.1) | copy-start | bytes 1572868
  2.4 7.9 %collective-permute-start = (f32[4,2,32,128]{3,2,1,0:T(8,128)S(1)}, f32[4,2,32,128]{3,2,1,0:T(8,128)S(1)}, u32[]{:S(2)}, u32[]{:S(2)}) collective-permute-start(f32[4,2,32,128]{3,2,1,0:T(8,128)S(1)} %get-tuple-element.54), channel_id=1, source_target_pairs={{0,1},{1,0},{2,3},{3,2},{4,5},{5,4},{6,7},{7,6},{8,9},{9,8},{10,11... | collective-permute-start | bytes 393224 | tf_op jit(solution)/shard_map/ppermute | solution.py:502
  3.1 7.1 %collective-permute-start.1 = (f32[4,2,32,128]{3,2,1,0:T(8,128)S(1)}, f32[4,2,32,128]{3,2,1,0:T(8,128)S(1)}, u32[]{:S(2)}, u32[]{:S(2)}) collective-permute-start(f32[4,2,32,128]{3,2,1,0:T(8,128)S(1)} %get-tuple-element.55), channel_id=1, source_target_pairs={{1,2},{2,1},{3,4},{4,3},{5,6},{6,5},{7,8},{8,7},{9,10},{10,9},{11,... | collective-permute-start | bytes 393224 | tf_op jit(solution)/shard_map/ppermute | solution.py:501
  6.9 8.3 %collective-permute-start.4 = (f32[4,1,64,128]{3,2,1,0:T(8,128)S(1)}, f32[4,1,64,128]{3,2,1,0:T(8,128)S(1)}, u32[]{:S(2)}, u32[]{:S(2)}) collective-permute-start(f32[4,1,64,128]{3,2,1,0:T(8,128)S(1)} %get-tuple-element.65), channel_id=1, source_target_pairs={{0,1},{1,0},{2,3},{3,2},{4,5},{5,4},{6,7},{7,6},{8,9},{9,8},{10,11... | collective-permute-start | bytes 393224 | tf_op jit(solution)/shard_map/ppermute | solution.py:502
  7.0 8.2 %collective-permute-start.5 = (f32[4,1,64,128]{3,2,1,0:T(8,128)S(1)}, f32[4,1,64,128]{3,2,1,0:T(8,128)S(1)}, u32[]{:S(2)}, u32[]{:S(2)}) collective-permute-start(f32[4,1,64,128]{3,2,1,0:T(8,128)S(1)} %get-tuple-element.66), channel_id=1, source_target_pairs={{1,2},{2,1},{3,4},{4,3},{5,6},{6,5},{7,8},{8,7},{9,10},{10,9},{11,... | collective-permute-start | bytes 393224 | tf_op jit(solution)/shard_map/ppermute | solution.py:501
  10.3 9.1 %copy-start.2 = (f32[27,64,32]{1,2,0:T(8,128)S(1)}, f32[27,64,32]{1,2,0:T(8,128)}, u32[]{:S(2)}) copy-start(f32[27,64,32]{1,2,0:T(8,128)} %param.16) | copy-start | bytes 663556
  10.3 9.1 %copy-start.6 = (f32[64]{0:T(128)S(1)}, f32[64]{0:T(128)}, u32[]{:S(2)}) copy-start(f32[64]{0:T(128)} %param.17) | copy-start | bytes 772
  10.9 10.4 %collective-permute-start.2 = (f32[2,8,32,128]{3,2,1,0:T(8,128)S(1)}, f32[2,8,32,128]{3,2,1,0:T(8,128)S(1)}, u32[]{:S(2)}, u32[]{:S(2)}) collective-permute-start(f32[2,8,32,128]{3,2,1,0:T(8,128)S(1)} %get-tuple-element.57), channel_id=1, source_target_pairs={{0,16},{16,0},{32,48},{48,32},{64,80},{80,64},{96,112},{112,96},{1... | collective-permute-start | bytes 786440 | tf_op jit(solution)/shard_map/ppermute | solution.py:502
  11.2 10.1 %collective-permute-start.3 = (f32[2,8,32,128]{3,2,1,0:T(8,128)S(1)}, f32[2,8,32,128]{3,2,1,0:T(8,128)S(1)}, u32[]{:S(2)}, u32[]{:S(2)}) collective-permute-start(f32[2,8,32,128]{3,2,1,0:T(8,128)S(1)} %get-tuple-element.58), channel_id=1, source_target_pairs={{16,32},{32,16},{48,64},{64,48},{80,96},{96,80},{112,128},{128,112... | collective-permute-start | bytes 786440 | tf_op jit(solution)/shard_map/ppermute | solution.py:501
  15.8 8.0 %collective-permute-start.6 = (f32[1,6,64,128]{3,2,1,0:T(8,128)S(1)}, f32[1,6,64,128]{3,2,1,0:T(8,128)S(1)}, u32[]{:S(2)}, u32[]{:S(2)}) collective-permute-start(f32[1,6,64,128]{3,2,1,0:T(8,128)S(1)} %get-tuple-element.67), channel_id=1, source_target_pairs={{0,16},{16,0},{32,48},{48,32},{64,80},{80,64},{96,112},{112,96},{1... | collective-permute-start | bytes 589832 | tf_op jit(solution)/shard_map/ppermute | solution.py:502
  17.4 6.7 %collective-permute-start.7 = (f32[1,6,64,128]{3,2,1,0:T(8,128)S(1)}, f32[1,6,64,128]{3,2,1,0:T(8,128)S(1)}, u32[]{:S(2)}, u32[]{:S(2)}) collective-permute-start(f32[1,6,64,128]{3,2,1,0:T(8,128)S(1)} %get-tuple-element.68), channel_id=1, source_target_pairs={{16,32},{32,16},{48,64},{64,48},{80,96},{96,80},{112,128},{128,112... | collective-permute-start | bytes 589832 | tf_op jit(solution)/shard_map/ppermute | solution.py:501
  21.3 2.8 %copy-start.4 = (f32[64,64]{1,0:T(8,128)S(1)}, f32[64,64]{1,0:T(8,128)}, u32[]{:S(2)}) copy-start(f32[64,64]{1,0:T(8,128)} %refs_10_.1) | copy-start | bytes 49156
  21.3 2.8 %copy-start.7 = (f32[64]{0:T(128)S(1)}, f32[64]{0:T(128)}, u32[]{:S(2)}) copy-start(f32[64]{0:T(128)} %param.19) | copy-start | bytes 772
  28.3 4.8 %collective-permute-start.8 = (f32[256,128]{1,0:T(8,128)S(1)}, f32[256,128]{1,0:T(8,128)S(1)}, u32[]{:S(2)}, u32[]{:S(2)}) collective-permute-start(f32[256,128]{1,0:T(8,128)S(1)} %slice_select_fusion), channel_id=1, source_target_pairs={{0,1},{1,0},{2,3},{3,2},{4,5},{5,4},{6,7},{7,6},{8,9},{9,8},{10,11... | collective-permute-start | bytes 393224 | tf_op jit(solution)/shard_map/ppermute | solution.py:520
  31.2 10.0 %copy-start.3 = (f32[27,32,8]{1,2,0:T(8,128)S(1)}, f32[27,32,8]{1,2,0:T(8,128)}, u32[]{:S(2)}) copy-start(f32[27,32,8]{1,2,0:T(8,128)} %param.12) | copy-start | bytes 82948
  31.2 10.0 %copy-start.5 = (f32[16,32]{1,0:T(8,128)S(1)}, f32[16,32]{1,0:T(8,128)}, u32[]{:S(2)}) copy-start(f32[16,32]{1,0:T(8,128)} %refs_4_.1) | copy-start | bytes 6148
  31.2 10.0 %copy-start.8 = (f32[32]{0:T(128)S(1)}, f32[32]{0:T(128)}, u32[]{:S(2)}) copy-start(f32[32]{0:T(128)} %param.13) | copy-start | bytes 388
  31.2 10.0 %copy-start.9 = (f32[16]{0:T(128)S(1)}, f32[16]{0:T(128)}, u32[]{:S(2)}) copy-start(f32[16]{0:T(128)} %param.15) | copy-start | bytes 196
  33.2 12.3 %collective-permute-start.9 = (f32[64,128]{1,0:T(8,128)S(1)}, f32[64,128]{1,0:T(8,128)S(1)}, u32[]{:S(2)}, u32[]{:S(2)}) collective-permute-start(f32[64,128]{1,0:T(8,128)S(1)} %slice_select_fusion.9), channel_id=1, source_target_pairs={{0,2},{1,3},{2,0},{3,1},{4,6},{5,7},{6,4},{7,5},{8,10},{9,11},{10,... | collective-permute-start | bytes 98312 | tf_op jit(solution)/shard_map/ppermute | solution.py:520
  39.1 6.5 %collective-permute-start.10 = (f32[64,128]{1,0:T(8,128)S(1)}, f32[64,128]{1,0:T(8,128)S(1)}, u32[]{:S(2)}, u32[]{:S(2)}) collective-permute-start(f32[64,128]{1,0:T(8,128)S(1)} %get-tuple-element.123), channel_id=1, source_target_pairs={{0,16},{1,17},{2,18},{3,19},{4,20},{5,21},{6,22},{7,23},{8,24},{9,... | collective-permute-start | bytes 98312 | tf_op jit(solution)/shard_map/ppermute | solution.py:520
  41.2 4.4 %collective-permute-start.11 = (f32[64,128]{1,0:T(8,128)S(1)}, f32[64,128]{1,0:T(8,128)S(1)}, u32[]{:S(2)}, u32[]{:S(2)}) collective-permute-start(f32[64,128]{1,0:T(8,128)S(1)} %get-tuple-element.122), channel_id=1, source_target_pairs={{0,18},{1,19},{2,16},{3,17},{4,22},{5,23},{6,20},{7,21},{8,26},{9,... | collective-permute-start | bytes 98312 | tf_op jit(solution)/shard_map/ppermute | solution.py:520
  45.6 2.0 %collective-permute-start.12 = (f32[40,128]{1,0:T(8,128)S(1)}, f32[40,128]{1,0:T(8,128)S(1)}, u32[]{:S(2)}, u32[]{:S(2)}) collective-permute-start(f32[40,128]{1,0:T(8,128)S(1)} %slice_select_fusion.10), channel_id=1, source_target_pairs={{0,1},{1,0},{2,3},{3,2},{4,5},{5,4},{6,7},{7,6},{8,9},{9,8},{10,11... | collective-permute-start | bytes 61448 | tf_op jit(solution)/shard_map/ppermute | solution.py:520
  47.6 3.1 %collective-permute-start.13 = (f32[104,128]{1,0:T(8,128)S(1)}, f32[104,128]{1,0:T(8,128)S(1)}, u32[]{:S(2)}, u32[]{:S(2)}) collective-permute-start(f32[104,128]{1,0:T(8,128)S(1)} %pad_maximum_fusion.4), channel_id=1, source_target_pairs={{0,6},{1,7},{2,4},{3,5},{4,2},{5,3},{6,0},{7,1},{8,14},{9,15},{10,... | collective-permute-start | bytes 159752 | tf_op jit(solution)/shard_map/ppermute | solution.py:520
  47.7 3.1 %collective-permute-start.14 = (f32[104,128]{1,0:T(8,128)S(1)}, f32[104,128]{1,0:T(8,128)S(1)}, u32[]{:S(2)}, u32[]{:S(2)}) collective-permute-start(f32[104,128]{1,0:T(8,128)S(1)} %pad_maximum_fusion.4), channel_id=1, source_target_pairs={{0,48},{1,49},{2,50},{3,51},{4,52},{5,53},{6,54},{7,55},{8,56},{9,... | collective-permute-start | bytes 159752 | tf_op jit(solution)/shard_map/ppermute | solution.py:520
  47.8 4.2 %collective-permute-start.15 = (f32[104,128]{1,0:T(8,128)S(1)}, f32[104,128]{1,0:T(8,128)S(1)}, u32[]{:S(2)}, u32[]{:S(2)}) collective-permute-start(f32[104,128]{1,0:T(8,128)S(1)} %pad_maximum_fusion.4), channel_id=1, source_target_pairs={{0,54},{1,55},{2,52},{3,53},{4,50},{5,51},{6,48},{7,49},{8,62},{9,... | collective-permute-start | bytes 159752 | tf_op jit(solution)/shard_map/ppermute | solution.py:520
  51.9 4.0 %collective-permute-start.16 = (f32[104,128]{1,0:T(8,128)S(1)}, f32[104,128]{1,0:T(8,128)S(1)}, u32[]{:S(2)}, u32[]{:S(2)}) collective-permute-start(f32[104,128]{1,0:T(8,128)S(1)} %add_add_fusion.1), channel_id=1, source_target_pairs={{0,64},{1,65},{2,66},{3,67},{4,68},{5,69},{6,70},{7,71},{8,72},{9,... | collective-permute-start | bytes 159752 | tf_op jit(solution)/shard_map/ppermute | solution.py:520
  53.8 9.4 %collective-permute-start.21 = (f32[104,128]{1,0:T(8,128)S(1)}, f32[104,128]{1,0:T(8,128)S(1)}, u32[]{:S(2)}, u32[]{:S(2)}) collective-permute-start(f32[104,128]{1,0:T(8,128)S(1)} %add_add_fusion.1), channel_id=1, source_target_pairs={{0,128},{1,129},{2,130},{3,131},{4,132},{5,133},{6,134},{7,135},{8... | collective-permute-start | bytes 159752 | tf_op jit(solution)/shard_map/ppermute | solution.py:520
  53.9 9.3 %collective-permute-start.22 = (f32[104,128]{1,0:T(8,128)S(1)}, f32[104,128]{1,0:T(8,128)S(1)}, u32[]{:S(2)}, u32[]{:S(2)}) collective-permute-start(f32[104,128]{1,0:T(8,128)S(1)} %add_add_fusion.1), channel_id=1, source_target_pairs={{0,192},{1,193},{2,194},{3,195},{4,196},{5,197},{6,198},{7,199},{8... | collective-permute-start | bytes 159752 | tf_op jit(solution)/shard_map/ppermute | solution.py:520
  57.4 7.5 %collective-permute-start.17 = (f32[10,8,128]{2,1,0:T(8,128)S(1)}, f32[10,8,128]{2,1,0:T(8,128)S(1)}, u32[]{:S(2)}, u32[]{:S(2)}) collective-permute-start(f32[10,8,128]{2,1,0:T(8,128)S(1)} %get-tuple-element.117), channel_id=1, source_target_pairs={{1,2},{2,1},{3,4},{4,3},{5,6},{6,5},{7,8},{8,7},{9,10},{10,9},{11,... | collective-permute-start | bytes 122888 | tf_op jit(solution)/shard_map/ppermute | solution.py:501
  63.1 1.8 %collective-permute-start.18 = (f32[10,8,128]{2,1,0:T(8,128)S(1)}, f32[10,8,128]{2,1,0:T(8,128)S(1)}, u32[]{:S(2)}, u32[]{:S(2)}) collective-permute-start(f32[10,8,128]{2,1,0:T(8,128)S(1)} %get-tuple-element.116), channel_id=1, source_target_pairs={{0,1},{1,0},{2,3},{3,2},{4,5},{5,4},{6,7},{7,6},{8,9},{9,8},{10,11... | collective-permute-start | bytes 122888 | tf_op jit(solution)/shard_map/ppermute | solution.py:502
  63.3 10.0 %collective-permute-start.23 = (f32[104,128]{1,0:T(8,128)S(1)}, f32[104,128]{1,0:T(8,128)S(1)}, u32[]{:S(2)}, u32[]{:S(2)}) collective-permute-start(f32[104,128]{1,0:T(8,128)S(1)} %add_add_fusion), channel_id=1, source_target_pairs={{0,200},{1,201},{2,202},{3,203},{4,204},{5,205},{6,206},{7,207},{8... | collective-permute-start | bytes 159752 | tf_op jit(solution)/shard_map/ppermute | solution.py:520
  64.9 11.8 %collective-permute-start.19 = (f32[8,8,128]{2,1,0:T(8,128)S(1)}, f32[8,8,128]{2,1,0:T(8,128)S(1)}, u32[]{:S(2)}, u32[]{:S(2)}) collective-permute-start(f32[8,8,128]{2,1,0:T(8,128)S(1)} %get-tuple-element.121), channel_id=1, source_target_pairs={{16,32},{32,16},{48,64},{64,48},{80,96},{96,80},{112,128},{128,112... | collective-permute-start | bytes 98312 | tf_op jit(solution)/shard_map/ppermute | solution.py:501
  68.7 8.1 %collective-permute-start.20 = (f32[8,8,128]{2,1,0:T(8,128)S(1)}, f32[8,8,128]{2,1,0:T(8,128)S(1)}, u32[]{:S(2)}, u32[]{:S(2)}) collective-permute-start(f32[8,8,128]{2,1,0:T(8,128)S(1)} %get-tuple-element.120), channel_id=1, source_target_pairs={{0,16},{16,0},{32,48},{48,32},{64,80},{80,64},{96,112},{112,96},{1... | collective-permute-start | bytes 98312 | tf_op jit(solution)/shard_map/ppermute | solution.py:502
  73.3 6.4 %collective-permute-start.24 = (f32[104,128]{1,0:T(8,128)S(1)}, f32[104,128]{1,0:T(8,128)S(1)}, u32[]{:S(2)}, u32[]{:S(2)}) collective-permute-start(f32[104,128]{1,0:T(8,128)S(1)} %add.92), channel_id=1, source_target_pairs={{0,18},{1,19},{2,16},{3,17},{4,22},{5,23},{6,20},{7,21},{8,26},{9,... | collective-permute-start | bytes 159752 | tf_op jit(solution)/shard_map/ppermute | solution.py:520
  75.3 4.5 %collective-permute-start.25 = (f32[104,128]{1,0:T(8,128)S(1)}, f32[104,128]{1,0:T(8,128)S(1)}, u32[]{:S(2)}, u32[]{:S(2)}) collective-permute-start(f32[104,128]{1,0:T(8,128)S(1)} %add.92), channel_id=1, source_target_pairs={{0,16},{1,17},{2,18},{3,19},{4,20},{5,21},{6,22},{7,23},{8,24},{9,... | collective-permute-start | bytes 159752 | tf_op jit(solution)/shard_map/ppermute | solution.py:520
  76.7 3.0 %collective-permute-start.26 = (f32[104,128]{1,0:T(8,128)S(1)}, f32[104,128]{1,0:T(8,128)S(1)}, u32[]{:S(2)}, u32[]{:S(2)}) collective-permute-start(f32[104,128]{1,0:T(8,128)S(1)} %add.92), channel_id=1, source_target_pairs={{0,2},{1,3},{2,0},{3,1},{4,6},{5,7},{6,4},{7,5},{8,10},{9,11},{10,... | collective-permute-start | bytes 159752 | tf_op jit(solution)/shard_map/ppermute | solution.py:520
  79.8 10.4 %collective-permute-start.27 = (f32[296,128]{1,0:T(8,128)S(1)}, f32[296,128]{1,0:T(8,128)S(1)}, u32[]{:S(2)}, u32[]{:S(2)}) collective-permute-start(f32[296,128]{1,0:T(8,128)S(1)} %pad_maximum_fusion), channel_id=1, source_target_pairs={{0,1},{1,0},{2,3},{3,2},{4,5},{5,4},{6,7},{7,6},{8,9},{9,8},{10,11... | collective-permute-start | bytes 454664 | tf_op jit(solution)/shard_map/ppermute | solution.py:520

commit v5 on v4

--- a/solution.py
+++ b/solution.py
@@ -424,6 +424,11 @@
         for y in range(count):
             more = [ref[x] for ref, at in ((low_ref, 0), (high_ref, count - 1)) if at == y]
             out_ref[i, y] = sum(more, rows_ref[i, y])
+
+
+def channels_first_kernel(field_ref, out_ref):
+    for x in range(field_ref.shape[0]):
+        out_ref[:, x] = jnp.swapaxes(field_ref[x], 0, 1)
 
 
 def rims_kernel(cot_ref, low_ref, high_ref, below_ref, above_ref, out_ref):
@@ -713,6 +718,8 @@
         f_conv,
     )
     low, high = halos("gy", columns[0], columns[1])
+    (field,) = call(channels_first_kernel, [(2 * fk, fx, fy, nz)], [], 1_000_000_000, field)
+    rows, field = tied(rows, field)
     (rows,) = call(corners_kernel, [rows.shape], [], 6_000_000_000, rows, low, high)
     below, above = halos("gx", rows[0], rows[1])
     sums = pair_sum(*sums, Z_FAR)
@@ -733,7 +740,7 @@
     )
     f_conv, f_in, f_proj, f_out, c_conv, c_in, c_proj, c_out = grads
     return (
-        jnp.transpose(field, (2, 0, 1, 3)),
+        field,
         cot,
         jnp.transpose(f_conv, (0, 2, 1)),
         f_in[0],

time: 92 us -> 90.9 us (0.988)
  the two profiles are of different devices: /device:TPU:235 before, /device:TPU:7 now
where the time goes in v5:
time: 90.9 us; the launch traced here: 89.4 us
  starting transfers between devices  47.9 us (53%)
  Pallas kernels  22.1 us (24%)
  waiting for transfers between devices  16.8 us (18%)
  between operations  1.26 us (1%)
  local copies, waits for them, and re-layouts  1.11 us (1%)
    ppermute x16, starting transfers between devices, partner(): return lax.ppermute(x, ('gx', 'gy'), pairs)  22.2 us
    pallas_call x14, Pallas kernels, call(): pl.pallas_call(kernel, in_specs=specs, out_shape=[jax.ShapeDtypeStruct(s,...  22.1 us
    ppermute x6, starting transfers between devices, swapped(): two = lax.ppermute(two, axis, outer)  21.4 us
    ppermute x6, waiting for transfers between devices, swapped(): two = lax.ppermute(two, axis, outer)  10.1 us
    ppermute x16, waiting for transfers between devices, partner(): return lax.ppermute(x, ('gx', 'gy'), pairs)  6.66 us
    ppermute x6, starting transfers between devices, swapped(): one = lax.ppermute(one, axis, inner)  4.18 us
  transfers between devices with their start and end apart: 28, of which 6 were waited for; matrix products, arithmetic and copies ran while one was open for 0% of the time, Pallas kernels for 18%

profile of v5, /device:TPU:7, one launch (start us, length us, event | category | flops | bytes accessed | tf_op | source)
XLA Modules:
  0.0 89.4 jit_solution(4355768575628105235)
XLA Ops:
  0.7 1.0 %copy-done = f32[64,4,4,128]{3,2,1,0:T(4,128)S(1)} copy-done((f32[64,4,4,128]{3,2,1,0:T(4,128)S(1)}, f32[64,4,4,128]{3,2,1,0:T(4,128)}, u32[]{:S(2)}) %copy-start) | copy-done | bytes 524312
  1.8 0.6 shard_map.177
  2.4 0.8 collective-permute-start
  3.1 8.6 %collective-permute-start.1 = (f32[4,2,32,128]{3,2,1,0:T(8,128)S(1)}, f32[4,2,32,128]{3,2,1,0:T(8,128)S(1)}, u32[]{:S(2)}, u32[]{:S(2)}) collective-permute-start(f32[4,2,32,128]{3,2,1,0:T(8,128)S(1)} %get-tuple-element.57), channel_id=1, source_target_pairs={{1,2},{2,1},{3,4},{4,3},{5,6},{6,5},{7,8},{8,7},{9,10},{10,9},{11,... | collective-permute-start | bytes 393224 | tf_op jit(solution)/shard_map/ppermute | solution.py:506
  11.8 0.7 shard_map.181
  12.5 0.1 collective-permute-start.4
  12.6 3.5 %collective-permute-start.5 = (f32[4,1,64,128]{3,2,1,0:T(8,128)S(1)}, f32[4,1,64,128]{3,2,1,0:T(8,128)S(1)}, u32[]{:S(2)}, u32[]{:S(2)}) collective-permute-start(f32[4,1,64,128]{3,2,1,0:T(8,128)S(1)} %get-tuple-element.68), channel_id=1, source_target_pairs={{1,2},{2,1},{3,4},{4,3},{5,6},{6,5},{7,8},{8,7},{9,10},{10,9},{11,... | collective-permute-start | bytes 393224 | tf_op jit(solution)/shard_map/ppermute | solution.py:506
  16.2 0.6 shard_map.179
  16.8 1.4 %collective-permute-start.2 = (f32[2,8,32,128]{3,2,1,0:T(8,128)S(1)}, f32[2,8,32,128]{3,2,1,0:T(8,128)S(1)}, u32[]{:S(2)}, u32[]{:S(2)}) collective-permute-start(f32[2,8,32,128]{3,2,1,0:T(8,128)S(1)} %get-tuple-element.59), channel_id=1, source_target_pairs={{0,16},{16,0},{32,48},{48,32},{64,80},{80,64},{96,112},{112,96},{1... | collective-permute-start | bytes 786440 | tf_op jit(solution)/shard_map/ppermute | solution.py:507
  18.2 0.7 collective-permute-start.3
  18.9 6.1 %collective-permute-done.5.yb_ref.refs_7_ = f32[4,1,64,128]{3,2,1,0:T(8,128)S(1)} collective-permute-done((f32[4,1,64,128]{3,2,1,0:T(8,128)S(1)}, f32[4,1,64,128]{3,2,1,0:T(8,128)S(1)}, u32[]{:S(2)}, u32[]{:S(2)}) %collective-permute-start.5) | collective-permute-done | bytes 131104 | tf_op jit(solution)/shard_map/ppermute | solution.py:506
  25.0 0.6 shard_map.182
  25.6 1.4 %collective-permute-start.6 = (f32[1,6,64,128]{3,2,1,0:T(8,128)S(1)}, f32[1,6,64,128]{3,2,1,0:T(8,128)S(1)}, u32[]{:S(2)}, u32[]{:S(2)}) collective-permute-start(f32[1,6,64,128]{3,2,1,0:T(8,128)S(1)} %get-tuple-element.69), channel_id=1, source_target_pairs={{0,16},{16,0},{32,48},{48,32},{64,80},{80,64},{96,112},{112,96},{1... | collective-permute-start | bytes 589832 | tf_op jit(solution)/shard_map/ppermute | solution.py:507
  27.0 0.7 collective-permute-start.7
  27.7 1.9 %shard_map.178 = (f32[4,96,1024]{2,1,0:T(8,128)S(1)}, f32[2,64,768]{2,1,0:T(8,128)S(1)}, f32[192,864]{1,0:T(8,128)S(1)}, f32[64,1]{1,0:T(8,128)S(1)}) custom-call(s32[2]{0:T(128)S(1)} %pad_add_fusion.at_ref.refs_0_, f32[4,4,32,128]{3,2,1,0:T(8,128)S(1)} %get-tuple-element.55.u_ref.f_ref, f32[4,2,32,128]{3,2,1,0:T(8,128)S(1)} %collective-permute-done.ya_ref, ...), custom_call_target="tpu_custom_call" | custom-call | flops 2500000000 | bytes 1000000 | tf_op jit(solution)/shard_map/pallas_call | solution.py:490
  29.6 2.5 %shard_map.180 = (f32[4,96,1024]{2,1,0:T(8,128)S(1)}, f32[4,64,768]{2,1,0:T(8,128)S(1)}) custom-call(s32[2]{0:T(128)S(1)} %pad_add_fusion.at_ref.refs_0_, f32[4,96,1024]{2,1,0:T(8,128)S(1)} %get-tuple-element.58.inner_ref.refs_1_, f32[2,8,32,128]{3,2,1,0:T(8,128)S(1)} %collective-permute-done.2.xa_ref, f32[2,8,32,128]{3,2,1,0:T(8,128)S(1)} %collective-permute-done.3.xb_ref, ...), custom_call_target="tpu_custom_call" | custom-call | flops 4000000000 | bytes 1000000 | tf_op jit(solution)/shard_map/pallas_call | solution.py:490
  32.2 4.2 %shard_map.183 = (f32[6,6,64,128]{3,2,1,0:T(8,128)S(1)}, f32[6,64,768]{2,1,0:T(8,128)S(1)}, f32[4,32,512]{2,1,0:T(8,128)S(1)}, f32[512,128]{1,0:T(8,128)S(1)}) custom-call(s32[2]{0:T(128)S(1)} %pad_add_fusion.at_ref.refs_0_, f32[4,96,1024]{2,1,0:T(8,128)S(1)} %get-tuple-element.58.inner_ref.refs_1_, f32[4,96,1024]{2,1,0:T(8,128)S(1)} %get-tuple-element.63.refs_2_, ...), custom_call_target="tpu_custom_call" | custom-call | flops 6000000000 | bytes 1000000 | tf_op jit(solution)/shard_map/pallas_call | solution.py:490
  36.4 0.1 collective-permute-start.8
  36.6 1.9 %shard_map.184.refs_1_ = f32[4,4,64,128]{3,2,1,0:T(8,128)S(1)} custom-call(f32[6,64,768]{2,1,0:T(8,128)S(1)} %get-tuple-element.73.gpre_ref, f32[4,32,512]{2,1,0:T(8,128)S(1)} %get-tuple-element.74.low_ref, f32[4,4,32,128]{3,2,1,0:T(8,128)S(1)} %get-tuple-element.75.cot_ref, f32[27,32,64]{2,1,0:T(8,128)S(1)} %bitcast.23), custom_call_target="tpu_custom_call" | custom-call | flops 2500000000 | bytes 1000000 | tf_op jit(solution)/shard_map/pallas_call | solution.py:490
  38.6 0.1 collective-permute-start.9
  38.7 5.1 %collective-permute-start.10 = (f32[64,128]{1,0:T(8,128)S(1)}, f32[64,128]{1,0:T(8,128)S(1)}, u32[]{:S(2)}, u32[]{:S(2)}) collective-permute-start(f32[64,128]{1,0:T(8,128)S(1)} %get-tuple-element.117), channel_id=1, source_target_pairs={{0,16},{1,17},{2,18},{3,19},{4,20},{5,21},{6,22},{7,23},{8,24},{9,... | collective-permute-start | bytes 98312 | tf_op jit(solution)/shard_map/ppermute | solution.py:525
  43.8 1.3 %collective-permute-start.11 = (f32[64,128]{1,0:T(8,128)S(1)}, f32[64,128]{1,0:T(8,128)S(1)}, u32[]{:S(2)}, u32[]{:S(2)}) collective-permute-start(f32[64,128]{1,0:T(8,128)S(1)} %get-tuple-element.116), channel_id=1, source_target_pairs={{0,18},{1,19},{2,16},{3,17},{4,22},{5,23},{6,20},{7,21},{8,26},{9,... | collective-permute-start | bytes 98312 | tf_op jit(solution)/shard_map/ppermute | solution.py:525
  45.1 4.3 %shard_map.185 = (f32[8,8,16,128]{3,2,1,0:T(8,128)S(1)}, f32[8,8,16,128]{3,2,1,0:T(8,128)S(1)}, f32[8,8,32,128]{3,2,1,0:T(8,128)S(1)}, f32[80,128]{1,0:T(8,128)S(1)}) custom-call(f32[6,6,64,128]{3,2,1,0:T(8,128)S(1)} %get-tuple-element.77.refs_0_, f32[4,4,64,128]{3,2,1,0:T(8,128)S(1)} %shard_map.184.refs_1_, f32[27,8,32]{2,1,0:T(8,128)S(1)} %bitcast.24, ...), custom_call_target="tpu_custom_call" | custom-call | flops 8999999488 | bytes 1000000 | tf_op jit(solution)/shard_map/pallas_call | solution.py:490
  49.4 1.1 %collective-permute-start.12 = (f32[40,128]{1,0:T(8,128)S(1)}, f32[40,128]{1,0:T(8,128)S(1)}, u32[]{:S(2)}, u32[]{:S(2)}) collective-permute-start(f32[40,128]{1,0:T(8,128)S(1)} %slice_select_fusion.10), channel_id=1, source_target_pairs={{0,1},{1,0},{2,3},{3,2},{4,5},{5,4},{6,7},{7,6},{8,9},{9,8},{10,11... | collective-permute-start | bytes 61448 | tf_op jit(solution)/shard_map/ppermute | solution.py:525
  50.5 0.8 collective-permute-done.12
  51.4 0.1 collective-permute-start.13
  51.5 3.0 %collective-permute-start.14 = (f32[104,128]{1,0:T(8,128)S(1)}, f32[104,128]{1,0:T(8,128)S(1)}, u32[]{:S(2)}, u32[]{:S(2)}) collective-permute-start(f32[104,128]{1,0:T(8,128)S(1)} %pad_maximum_fusion.4), channel_id=1, source_target_pairs={{0,48},{1,49},{2,50},{3,51},{4,52},{5,53},{6,54},{7,55},{8,56},{9,... | collective-permute-start | bytes 159752 | tf_op jit(solution)/shard_map/ppermute | solution.py:525
  54.5 2.3 %collective-permute-start.15 = (f32[104,128]{1,0:T(8,128)S(1)}, f32[104,128]{1,0:T(8,128)S(1)}, u32[]{:S(2)}, u32[]{:S(2)}) collective-permute-start(f32[104,128]{1,0:T(8,128)S(1)} %pad_maximum_fusion.4), channel_id=1, source_target_pairs={{0,54},{1,55},{2,52},{3,53},{4,50},{5,51},{6,48},{7,49},{8,62},{9,... | collective-permute-start | bytes 159752 | tf_op jit(solution)/shard_map/ppermute | solution.py:525
  56.8 4.0 %collective-permute-done.15 = f32[104,128]{1,0:T(8,128)S(1)} collective-permute-done((f32[104,128]{1,0:T(8,128)S(1)}, f32[104,128]{1,0:T(8,128)S(1)}, u32[]{:S(2)}, u32[]{:S(2)}) %collective-permute-start.15) | collective-permute-done | bytes 53280 | tf_op jit(solution)/shard_map/ppermute | solution.py:525
  60.8 1.3 %collective-permute-start.16 = (f32[104,128]{1,0:T(8,128)S(1)}, f32[104,128]{1,0:T(8,128)S(1)}, u32[]{:S(2)}, u32[]{:S(2)}) collective-permute-start(f32[104,128]{1,0:T(8,128)S(1)} %add_add_fusion.1), channel_id=1, source_target_pairs={{0,64},{1,65},{2,66},{3,67},{4,68},{5,69},{6,70},{7,71},{8,72},{9,... | collective-permute-start | bytes 159752 | tf_op jit(solution)/shard_map/ppermute | solution.py:525
  62.1 0.9 %shard_map.187 = f32[16,8,8,128]{3,2,1,0:T(8,128)} custom-call(f32[8,8,16,128]{3,2,1,0:T(8,128)S(1)} %get-tuple-element.86.field_ref), custom_call_target="tpu_custom_call" | custom-call | flops 1000000000 | bytes 1000000 | tf_op jit(solution)/shard_map/pallas_call | solution.py:490
  63.0 1.2 %collective-permute-start.21 = (f32[104,128]{1,0:T(8,128)S(1)}, f32[104,128]{1,0:T(8,128)S(1)}, u32[]{:S(2)}, u32[]{:S(2)}) collective-permute-start(f32[104,128]{1,0:T(8,128)S(1)} %add_add_fusion.1), channel_id=1, source_target_pairs={{0,128},{1,129},{2,130},{3,131},{4,132},{5,133},{6,134},{7,135},{8... | collective-permute-start | bytes 159752 | tf_op jit(solution)/shard_map/ppermute | solution.py:525
  64.2 1.2 %collective-permute-start.22 = (f32[104,128]{1,0:T(8,128)S(1)}, f32[104,128]{1,0:T(8,128)S(1)}, u32[]{:S(2)}, u32[]{:S(2)}) collective-permute-start(f32[104,128]{1,0:T(8,128)S(1)} %add_add_fusion.1), channel_id=1, source_target_pairs={{0,192},{1,193},{2,194},{3,195},{4,196},{5,197},{6,198},{7,199},{8... | collective-permute-start | bytes 159752 | tf_op jit(solution)/shard_map/ppermute | solution.py:525
  65.4 1.4 %shard_map.186 = (f32[8,8,16,128]{3,2,1,0:T(8,128)S(1)}, f32[2,10,8,128]{3,2,1,0:T(8,128)S(1)}, f32[2,8,8,128]{3,2,1,0:T(8,128)S(1)}) custom-call(f32[8,8,32,128]{3,2,1,0:T(8,128)S(1)} %get-tuple-element.83.gpre_ref, f32[8,8,16,128]{3,2,1,0:T(8,128)S(1)} %get-tuple-element.84.cot_ref, f32[27,8,32]{2,1,0:T(8,128)S(1)} %bitcast.25), custom_call_target="tpu_custom_call" | custom-call | flops 4000000000 | bytes 1000000 | tf_op jit(solution)/shard_map/pallas_call | solution.py:490
  66.8 7.3 %collective-permute-start.17 = (f32[10,8,128]{2,1,0:T(8,128)S(1)}, f32[10,8,128]{2,1,0:T(8,128)S(1)}, u32[]{:S(2)}, u32[]{:S(2)}) collective-permute-start(f32[10,8,128]{2,1,0:T(8,128)S(1)} %get-tuple-element.111), channel_id=1, source_target_pairs={{1,2},{2,1},{3,4},{4,3},{5,6},{6,5},{7,8},{8,7},{9,10},{10,9},{11,... | collective-permute-start | bytes 122888 | tf_op jit(solution)/shard_map/ppermute | solution.py:506
  74.2 0.1 collective-permute-start.18
  74.3 0.1 collective-permute-start.23
  74.4 4.0 %collective-permute-done.17 = f32[10,8,128]{2,1,0:T(8,128)S(1)} collective-permute-done((f32[10,8,128]{2,1,0:T(8,128)S(1)}, f32[10,8,128]{2,1,0:T(8,128)S(1)}, u32[]{:S(2)}, u32[]{:S(2)}) %collective-permute-start.17) | collective-permute-done | bytes 40992 | tf_op jit(solution)/shard_map/ppermute | solution.py:506
  78.4 0.7 collective-permute-start.19
  79.1 0.5 collective-permute-start.20
  79.6 0.1 collective-permute-start.24
  79.7 1.2 %collective-permute-start.25 = (f32[104,128]{1,0:T(8,128)S(1)}, f32[104,128]{1,0:T(8,128)S(1)}, u32[]{:S(2)}, u32[]{:S(2)}) collective-permute-start(f32[104,128]{1,0:T(8,128)S(1)} %add.92), channel_id=1, source_target_pairs={{0,16},{1,17},{2,18},{3,19},{4,20},{5,21},{6,22},{7,23},{8,24},{9,... | collective-permute-start | bytes 159752 | tf_op jit(solution)/shard_map/ppermute | solution.py:525
  80.9 1.5 %collective-permute-start.26 = (f32[104,128]{1,0:T(8,128)S(1)}, f32[104,128]{1,0:T(8,128)S(1)}, u32[]{:S(2)}, u32[]{:S(2)}) collective-permute-start(f32[104,128]{1,0:T(8,128)S(1)} %add.92), channel_id=1, source_target_pairs={{0,2},{1,3},{2,0},{3,1},{4,6},{5,7},{6,4},{7,5},{8,10},{9,11},{10,... | collective-permute-start | bytes 159752 | tf_op jit(solution)/shard_map/ppermute | solution.py:525
  82.3 1.7 %collective-permute-done.26 = f32[104,128]{1,0:T(8,128)S(1)} collective-permute-done((f32[104,128]{1,0:T(8,128)S(1)}, f32[104,128]{1,0:T(8,128)S(1)}, u32[]{:S(2)}, u32[]{:S(2)}) %collective-permute-start.26) | collective-permute-done | bytes 53280 | tf_op jit(solution)/shard_map/ppermute | solution.py:525
  84.1 2.8 %collective-permute-start.27 = (f32[296,128]{1,0:T(8,128)S(1)}, f32[296,128]{1,0:T(8,128)S(1)}, u32[]{:S(2)}, u32[]{:S(2)}) collective-permute-start(f32[296,128]{1,0:T(8,128)S(1)} %pad_maximum_fusion), channel_id=1, source_target_pairs={{0,1},{1,0},{2,3},{3,2},{4,5},{5,4},{6,7},{7,6},{8,9},{9,8},{10,11... | collective-permute-start | bytes 454664 | tf_op jit(solution)/shard_map/ppermute | solution.py:525
  86.9 0.9 %shard_map.189 = f32[16,8,8,128]{3,2,1,0:T(8,128)} custom-call(f32[8,8,16,128]{3,2,1,0:T(8,128)S(1)} %get-tuple-element.88.cot_ref, f32[10,8,128]{2,1,0:T(8,128)S(1)} %get-tuple-element.109.low_ref, f32[10,8,128]{2,1,0:T(8,128)S(1)} %get-tuple-element.108.high_ref, f32[8,8,128]{2,1,0:T(8,128)S(1)} %get-tuple-element.113.below_ref, ...), custom_call_target="tpu_custom_call" | custom-call | flops 2000000000 | bytes 1000000 | tf_op jit(solution)/shard_map/pallas_call | solution.py:490
  87.8 0.1 collective-permute-done.27
  87.9 1.5 %shard_map.190 = (f32[27,8,32]{2,1,0:T(8,128)}, f32[1,32]{1,0:T(1,128)}, f32[16,32]{1,0:T(8,128)}, f32[1,16]{1,0:T(1,128)}, f32[27,32,64]{2,1,0:T(8,128)}, /*ind...) custom-call(s32[2]{0:T(128)S(1)} %pad_add_fusion.at_ref.refs_0_, f32[256,128]{1,0:T(8,128)S(1)} %pad_maximum_fusion.1.coarse_ref, ...), custom_call_target="tpu_custom_call" | custom-call | flops 1000000 | bytes 1000000 | tf_op jit(solution)/shard_map/pallas_call | solution.py:490
  (67 shorter events, 0.5 us)
Async XLA Ops:
  0.7 1.0 %copy-start = (f32[64,4,4,128]{3,2,1,0:T(4,128)S(1)}, f32[64,4,4,128]{3,2,1,0:T(4,128)}, u32[]{:S(2)}) copy-start(f32[64,4,4,128]{3,2,1,0:T(4,128)} %w_ref.3) | copy-start | bytes 1572868
  1.8 10.0 %copy-start.1 = (f32[64,4,4,128]{3,2,1,0:T(4,128)S(1)}, f32[64,4,4,128]{3,2,1,0:T(4,128)}, u32[]{:S(2)}) copy-start(f32[64,4,4,128]{3,2,1,0:T(4,128)} %dw_ref.1) | copy-start | bytes 1572868
  2.4 13.8 %collective-permute-start = (f32[4,2,32,128]{3,2,1,0:T(8,128)S(1)}, f32[4,2,32,128]{3,2,1,0:T(8,128)S(1)}, u32[]{:S(2)}, u32[]{:S(2)}) collective-permute-start(f32[4,2,32,128]{3,2,1,0:T(8,128)S(1)} %get-tuple-element.56), channel_id=1, source_target_pairs={{0,1},{1,0},{2,3},{3,2},{4,5},{5,4},{6,7},{7,6},{8,9},{9,8},{10,11... | collective-permute-start | bytes 393224 | tf_op jit(solution)/shard_map/ppermute | solution.py:507
  3.1 13.0 %collective-permute-start.1 = (f32[4,2,32,128]{3,2,1,0:T(8,128)S(1)}, f32[4,2,32,128]{3,2,1,0:T(8,128)S(1)}, u32[]{:S(2)}, u32[]{:S(2)}) collective-permute-start(f32[4,2,32,128]{3,2,1,0:T(8,128)S(1)} %get-tuple-element.57), channel_id=1, source_target_pairs={{1,2},{2,1},{3,4},{4,3},{5,6},{6,5},{7,8},{8,7},{9,10},{10,9},{11,... | collective-permute-start | bytes 393224 | tf_op jit(solution)/shard_map/ppermute | solution.py:506
  12.5 6.4 %collective-permute-start.4 = (f32[4,1,64,128]{3,2,1,0:T(8,128)S(1)}, f32[4,1,64,128]{3,2,1,0:T(8,128)S(1)}, u32[]{:S(2)}, u32[]{:S(2)}) collective-permute-start(f32[4,1,64,128]{3,2,1,0:T(8,128)S(1)} %get-tuple-element.67), channel_id=1, source_target_pairs={{0,1},{1,0},{2,3},{3,2},{4,5},{5,4},{6,7},{7,6},{8,9},{9,8},{10,11... | collective-permute-start | bytes 393224 | tf_op jit(solution)/shard_map/ppermute | solution.py:507
  12.6 12.4 %collective-permute-start.5 = (f32[4,1,64,128]{3,2,1,0:T(8,128)S(1)}, f32[4,1,64,128]{3,2,1,0:T(8,128)S(1)}, u32[]{:S(2)}, u32[]{:S(2)}) collective-permute-start(f32[4,1,64,128]{3,2,1,0:T(8,128)S(1)} %get-tuple-element.68), channel_id=1, source_target_pairs={{1,2},{2,1},{3,4},{4,3},{5,6},{6,5},{7,8},{8,7},{9,10},{10,9},{11,... | collective-permute-start | bytes 393224 | tf_op jit(solution)/shard_map/ppermute | solution.py:506
  16.2 11.5 %copy-start.2 = (f32[27,64,32]{1,2,0:T(8,128)S(1)}, f32[27,64,32]{1,2,0:T(8,128)}, u32[]{:S(2)}) copy-start(f32[27,64,32]{1,2,0:T(8,128)} %param.16) | copy-start | bytes 663556
  16.2 11.5 %copy-start.6 = (f32[64]{0:T(128)S(1)}, f32[64]{0:T(128)}, u32[]{:S(2)}) copy-start(f32[64]{0:T(128)} %param.17) | copy-start | bytes 772
  16.8 12.8 %collective-permute-start.2 = (f32[2,8,32,128]{3,2,1,0:T(8,128)S(1)}, f32[2,8,32,128]{3,2,1,0:T(8,128)S(1)}, u32[]{:S(2)}, u32[]{:S(2)}) collective-permute-start(f32[2,8,32,128]{3,2,1,0:T(8,128)S(1)} %get-tuple-element.59), channel_id=1, source_target_pairs={{0,16},{16,0},{32,48},{48,32},{64,80},{80,64},{96,112},{112,96},{1... | collective-permute-start | bytes 786440 | tf_op jit(solution)/shard_map/ppermute | solution.py:507
  18.2 11.4 %collective-permute-start.3 = (f32[2,8,32,128]{3,2,1,0:T(8,128)S(1)}, f32[2,8,32,128]{3,2,1,0:T(8,128)S(1)}, u32[]{:S(2)}, u32[]{:S(2)}) collective-permute-start(f32[2,8,32,128]{3,2,1,0:T(8,128)S(1)} %get-tuple-element.60), channel_id=1, source_target_pairs={{16,32},{32,16},{48,64},{64,48},{80,96},{96,80},{112,128},{128,112... | collective-permute-start | bytes 786440 | tf_op jit(solution)/shard_map/ppermute | solution.py:506
  25.6 6.6 %collective-permute-start.6 = (f32[1,6,64,128]{3,2,1,0:T(8,128)S(1)}, f32[1,6,64,128]{3,2,1,0:T(8,128)S(1)}, u32[]{:S(2)}, u32[]{:S(2)}) collective-permute-start(f32[1,6,64,128]{3,2,1,0:T(8,128)S(1)} %get-tuple-element.69), channel_id=1, source_target_pairs={{0,16},{16,0},{32,48},{48,32},{64,80},{80,64},{96,112},{112,96},{1... | collective-permute-start | bytes 589832 | tf_op jit(solution)/shard_map/ppermute | solution.py:507
  27.0 5.2 %collective-permute-start.7 = (f32[1,6,64,128]{3,2,1,0:T(8,128)S(1)}, f32[1,6,64,128]{3,2,1,0:T(8,128)S(1)}, u32[]{:S(2)}, u32[]{:S(2)}) collective-permute-start(f32[1,6,64,128]{3,2,1,0:T(8,128)S(1)} %get-tuple-element.70), channel_id=1, source_target_pairs={{16,32},{32,16},{48,64},{64,48},{80,96},{96,80},{112,128},{128,112... | collective-permute-start | bytes 589832 | tf_op jit(solution)/shard_map/ppermute | solution.py:506
  29.6 2.6 %copy-start.4 = (f32[64,64]{1,0:T(8,128)S(1)}, f32[64,64]{1,0:T(8,128)}, u32[]{:S(2)}) copy-start(f32[64,64]{1,0:T(8,128)} %refs_10_.1) | copy-start | bytes 49156
  29.6 2.6 %copy-start.7 = (f32[64]{0:T(128)S(1)}, f32[64]{0:T(128)}, u32[]{:S(2)}) copy-start(f32[64]{0:T(128)} %param.19) | copy-start | bytes 772
  36.4 2.1 %collective-permute-start.8 = (f32[256,128]{1,0:T(8,128)S(1)}, f32[256,128]{1,0:T(8,128)S(1)}, u32[]{:S(2)}, u32[]{:S(2)}) collective-permute-start(f32[256,128]{1,0:T(8,128)S(1)} %slice_select_fusion), channel_id=1, source_target_pairs={{0,1},{1,0},{2,3},{3,2},{4,5},{5,4},{6,7},{7,6},{8,9},{9,8},{10,11... | collective-permute-start | bytes 393224 | tf_op jit(solution)/shard_map/ppermute | solution.py:525
  36.5 8.5 %copy-start.3 = (f32[27,32,8]{1,2,0:T(8,128)S(1)}, f32[27,32,8]{1,2,0:T(8,128)}, u32[]{:S(2)}) copy-start(f32[27,32,8]{1,2,0:T(8,128)} %param.12) | copy-start | bytes 82948
  36.6 8.5 %copy-start.5 = (f32[16,32]{1,0:T(8,128)S(1)}, f32[16,32]{1,0:T(8,128)}, u32[]{:S(2)}) copy-start(f32[16,32]{1,0:T(8,128)} %refs_4_.1) | copy-start | bytes 6148
  36.6 8.5 %copy-start.8 = (f32[32]{0:T(128)S(1)}, f32[32]{0:T(128)}, u32[]{:S(2)}) copy-start(f32[32]{0:T(128)} %param.13) | copy-start | bytes 388
  36.6 8.5 %copy-start.9 = (f32[16]{0:T(128)S(1)}, f32[16]{0:T(128)}, u32[]{:S(2)}) copy-start(f32[16]{0:T(128)} %param.15) | copy-start | bytes 196
  38.6 10.8 %collective-permute-start.9 = (f32[64,128]{1,0:T(8,128)S(1)}, f32[64,128]{1,0:T(8,128)S(1)}, u32[]{:S(2)}, u32[]{:S(2)}) collective-permute-start(f32[64,128]{1,0:T(8,128)S(1)} %slice_select_fusion.9), channel_id=1, source_target_pairs={{0,2},{1,3},{2,0},{3,1},{4,6},{5,7},{6,4},{7,5},{8,10},{9,11},{10,... | collective-permute-start | bytes 98312 | tf_op jit(solution)/shard_map/ppermute | solution.py:525
  38.7 10.7 %collective-permute-start.10 = (f32[64,128]{1,0:T(8,128)S(1)}, f32[64,128]{1,0:T(8,128)S(1)}, u32[]{:S(2)}, u32[]{:S(2)}) collective-permute-start(f32[64,128]{1,0:T(8,128)S(1)} %get-tuple-element.117), channel_id=1, source_target_pairs={{0,16},{1,17},{2,18},{3,19},{4,20},{5,21},{6,22},{7,23},{8,24},{9,... | collective-permute-start | bytes 98312 | tf_op jit(solution)/shard_map/ppermute | solution.py:525
  43.8 5.6 %collective-permute-start.11 = (f32[64,128]{1,0:T(8,128)S(1)}, f32[64,128]{1,0:T(8,128)S(1)}, u32[]{:S(2)}, u32[]{:S(2)}) collective-permute-start(f32[64,128]{1,0:T(8,128)S(1)} %get-tuple-element.116), channel_id=1, source_target_pairs={{0,18},{1,19},{2,16},{3,17},{4,22},{5,23},{6,20},{7,21},{8,26},{9,... | collective-permute-start | bytes 98312 | tf_op jit(solution)/shard_map/ppermute | solution.py:525
  49.4 2.0 %collective-permute-start.12 = (f32[40,128]{1,0:T(8,128)S(1)}, f32[40,128]{1,0:T(8,128)S(1)}, u32[]{:S(2)}, u32[]{:S(2)}) collective-permute-start(f32[40,128]{1,0:T(8,128)S(1)} %slice_select_fusion.10), channel_id=1, source_target_pairs={{0,1},{1,0},{2,3},{3,2},{4,5},{5,4},{6,7},{7,6},{8,9},{9,8},{10,11... | collective-permute-start | bytes 61448 | tf_op jit(solution)/shard_map/ppermute | solution.py:525
  51.4 5.4 %collective-permute-start.13 = (f32[104,128]{1,0:T(8,128)S(1)}, f32[104,128]{1,0:T(8,128)S(1)}, u32[]{:S(2)}, u32[]{:S(2)}) collective-permute-start(f32[104,128]{1,0:T(8,128)S(1)} %pad_maximum_fusion.4), channel_id=1, source_target_pairs={{0,6},{1,7},{2,4},{3,5},{4,2},{5,3},{6,0},{7,1},{8,14},{9,15},{10,... | collective-permute-start | bytes 159752 | tf_op jit(solution)/shard_map/ppermute | solution.py:525
  51.5 5.3 %collective-permute-start.14 = (f32[104,128]{1,0:T(8,128)S(1)}, f32[104,128]{1,0:T(8,128)S(1)}, u32[]{:S(2)}, u32[]{:S(2)}) collective-permute-start(f32[104,128]{1,0:T(8,128)S(1)} %pad_maximum_fusion.4), channel_id=1, source_target_pairs={{0,48},{1,49},{2,50},{3,51},{4,52},{5,53},{6,54},{7,55},{8,56},{9,... | collective-permute-start | bytes 159752 | tf_op jit(solution)/shard_map/ppermute | solution.py:525
  54.5 6.3 %collective-permute-start.15 = (f32[104,128]{1,0:T(8,128)S(1)}, f32[104,128]{1,0:T(8,128)S(1)}, u32[]{:S(2)}, u32[]{:S(2)}) collective-permute-start(f32[104,128]{1,0:T(8,128)S(1)} %pad_maximum_fusion.4), channel_id=1, source_target_pairs={{0,54},{1,55},{2,52},{3,53},{4,50},{5,51},{6,48},{7,49},{8,62},{9,... | collective-permute-start | bytes 159752 | tf_op jit(solution)/shard_map/ppermute | solution.py:525
  60.8 4.6 %collective-permute-start.16 = (f32[104,128]{1,0:T(8,128)S(1)}, f32[104,128]{1,0:T(8,128)S(1)}, u32[]{:S(2)}, u32[]{:S(2)}) collective-permute-start(f32[104,128]{1,0:T(8,128)S(1)} %add_add_fusion.1), channel_id=1, source_target_pairs={{0,64},{1,65},{2,66},{3,67},{4,68},{5,69},{6,70},{7,71},{8,72},{9,... | collective-permute-start | bytes 159752 | tf_op jit(solution)/shard_map/ppermute | solution.py:525
  63.0 11.3 %collective-permute-start.21 = (f32[104,128]{1,0:T(8,128)S(1)}, f32[104,128]{1,0:T(8,128)S(1)}, u32[]{:S(2)}, u32[]{:S(2)}) collective-permute-start(f32[104,128]{1,0:T(8,128)S(1)} %add_add_fusion.1), channel_id=1, source_target_pairs={{0,128},{1,129},{2,130},{3,131},{4,132},{5,133},{6,134},{7,135},{8... | collective-permute-start | bytes 159752 | tf_op jit(solution)/shard_map/ppermute | solution.py:525
  64.2 10.1 %collective-permute-start.22 = (f32[104,128]{1,0:T(8,128)S(1)}, f32[104,128]{1,0:T(8,128)S(1)}, u32[]{:S(2)}, u32[]{:S(2)}) collective-permute-start(f32[104,128]{1,0:T(8,128)S(1)} %add_add_fusion.1), channel_id=1, source_target_pairs={{0,192},{1,193},{2,194},{3,195},{4,196},{5,197},{6,198},{7,199},{8... | collective-permute-start | bytes 159752 | tf_op jit(solution)/shard_map/ppermute | solution.py:525
  66.8 11.5 %collective-permute-start.17 = (f32[10,8,128]{2,1,0:T(8,128)S(1)}, f32[10,8,128]{2,1,0:T(8,128)S(1)}, u32[]{:S(2)}, u32[]{:S(2)}) collective-permute-start(f32[10,8,128]{2,1,0:T(8,128)S(1)} %get-tuple-element.111), channel_id=1, source_target_pairs={{1,2},{2,1},{3,4},{4,3},{5,6},{6,5},{7,8},{8,7},{9,10},{10,9},{11,... | collective-permute-start | bytes 122888 | tf_op jit(solution)/shard_map/ppermute | solution.py:506
  74.2 4.2 %collective-permute-start.18 = (f32[10,8,128]{2,1,0:T(8,128)S(1)}, f32[10,8,128]{2,1,0:T(8,128)S(1)}, u32[]{:S(2)}, u32[]{:S(2)}) collective-permute-start(f32[10,8,128]{2,1,0:T(8,128)S(1)} %get-tuple-element.110), channel_id=1, source_target_pairs={{0,1},{1,0},{2,3},{3,2},{4,5},{5,4},{6,7},{7,6},{8,9},{9,8},{10,11... | collective-permute-start | bytes 122888 | tf_op jit(solution)/shard_map/ppermute | solution.py:507
  74.3 5.3 %collective-permute-start.23 = (f32[104,128]{1,0:T(8,128)S(1)}, f32[104,128]{1,0:T(8,128)S(1)}, u32[]{:S(2)}, u32[]{:S(2)}) collective-permute-start(f32[104,128]{1,0:T(8,128)S(1)} %add_add_fusion), channel_id=1, source_target_pairs={{0,200},{1,201},{2,202},{3,203},{4,204},{5,205},{6,206},{7,207},{8... | collective-permute-start | bytes 159752 | tf_op jit(solution)/shard_map/ppermute | solution.py:525
  78.4 3.9 %collective-permute-start.19 = (f32[8,8,128]{2,1,0:T(8,128)S(1)}, f32[8,8,128]{2,1,0:T(8,128)S(1)}, u32[]{:S(2)}, u32[]{:S(2)}) collective-permute-start(f32[8,8,128]{2,1,0:T(8,128)S(1)} %get-tuple-element.115), channel_id=1, source_target_pairs={{16,32},{32,16},{48,64},{64,48},{80,96},{96,80},{112,128},{128,112... | collective-permute-start | bytes 98312 | tf_op jit(solution)/shard_map/ppermute | solution.py:506
  79.1 3.2 %collective-permute-start.20 = (f32[8,8,128]{2,1,0:T(8,128)S(1)}, f32[8,8,128]{2,1,0:T(8,128)S(1)}, u32[]{:S(2)}, u32[]{:S(2)}) collective-permute-start(f32[8,8,128]{2,1,0:T(8,128)S(1)} %get-tuple-element.114), channel_id=1, source_target_pairs={{0,16},{16,0},{32,48},{48,32},{64,80},{80,64},{96,112},{112,96},{1... | collective-permute-start | bytes 98312 | tf_op jit(solution)/shard_map/ppermute | solution.py:507
  79.6 4.5 %collective-permute-start.24 = (f32[104,128]{1,0:T(8,128)S(1)}, f32[104,128]{1,0:T(8,128)S(1)}, u32[]{:S(2)}, u32[]{:S(2)}) collective-permute-start(f32[104,128]{1,0:T(8,128)S(1)} %add.92), channel_id=1, source_target_pairs={{0,18},{1,19},{2,16},{3,17},{4,22},{5,23},{6,20},{7,21},{8,26},{9,... | collective-permute-start | bytes 159752 | tf_op jit(solution)/shard_map/ppermute | solution.py:525
  79.7 4.4 %collective-permute-start.25 = (f32[104,128]{1,0:T(8,128)S(1)}, f32[104,128]{1,0:T(8,128)S(1)}, u32[]{:S(2)}, u32[]{:S(2)}) collective-permute-start(f32[104,128]{1,0:T(8,128)S(1)} %add.92), channel_id=1, source_target_pairs={{0,16},{1,17},{2,18},{3,19},{4,20},{5,21},{6,22},{7,23},{8,24},{9,... | collective-permute-start | bytes 159752 | tf_op jit(solution)/shard_map/ppermute | solution.py:525
  80.9 3.2 %collective-permute-start.26 = (f32[104,128]{1,0:T(8,128)S(1)}, f32[104,128]{1,0:T(8,128)S(1)}, u32[]{:S(2)}, u32[]{:S(2)}) collective-permute-start(f32[104,128]{1,0:T(8,128)S(1)} %add.92), channel_id=1, source_target_pairs={{0,2},{1,3},{2,0},{3,1},{4,6},{5,7},{6,4},{7,5},{8,10},{9,11},{10,... | collective-permute-start | bytes 159752 | tf_op jit(solution)/shard_map/ppermute | solution.py:525
  84.1 3.8 %collective-permute-start.27 = (f32[296,128]{1,0:T(8,128)S(1)}, f32[296,128]{1,0:T(8,128)S(1)}, u32[]{:S(2)}, u32[]{:S(2)}) collective-permute-start(f32[296,128]{1,0:T(8,128)S(1)} %pad_maximum_fusion), channel_id=1, source_target_pairs={{0,1},{1,0},{2,3},{3,2},{4,5},{5,4},{6,7},{7,6},{8,9},{9,8},{10,11... | collective-permute-start | bytes 454664 | tf_op jit(solution)/shard_map/ppermute | solution.py:525
